TPU v7x, 256 devices: a whole 4x4x8 slice. The times are simulated.
256 devices in a mesh: tm: 16 (over z, core), gx: 4 (over y), gy: 4 (over x).
Axes of the slice: x: 4, y: 4, z: 8, core: 2. Of those that a mesh axis runs over, the one named last changes fastest.
Arguments:
- field: float32 [16, 32, 32, 256], P('tm', 'gx', 'gy'), may hold values from -6 to 6
- modes: float32 [16, 16, 32, 32, 256], P('tm', None, 'gx', 'gy'), may hold values from -2 to 2
- source: float32 [32, 32, 256], P('gx', 'gy'), may hold values from -6 to 6
- regions: int32 [32, 32, 256], P('gx', 'gy'), may hold values from 0 to 7
- region_kappa: float32 [8], replicated, may hold values from 0.6 to 1
- mode_rate: float32 [16], replicated, may hold values from 0.02 to 4
- mode_weight: float32 [16], replicated, may hold values from 0.02 to 0.3
Outputs:
- new_field: float32 [16, 32, 32, 256], P('tm', 'gx', 'gy')
- new_modes: float32 [16, 16, 32, 32, 256], P('tm', None, 'gx', 'gy')
- correction_size: float32 [16], P('tm')
All inputs are finite; a program needn't handle non-finite values.
Results may differ from a plain program's by a relative error of at most 0.00021.
Values sent between devices are 32-bit elements; how exact they have to be, the bound alone decides.
No kernel may reach another device: no remote copies, remote signals or barrier semaphores. Data moves between devices by JAX's collectives and lax.ppermute only.
A program may use at most 64 MiB of HBM per device.

v0:
```python
import jax
import jax.numpy as jnp
from jax import lax
from jax.sharding import PartitionSpec as P

SUBSTEPS = 2


coarse_size = 0.12


def padded_2(array, sides, width):
    for axis, dim in sides:
        size, length = (lax.axis_size(axis), array.shape[dim])
        up = [(i, (i + 1) % size) for i in range(size - 1)]
        down = [(j, i) for i, j in up]
        last = lax.slice_in_dim(array, length - width, length, axis=dim)
        first = lax.slice_in_dim(array, 0, width, axis=dim)
        before = lax.ppermute(last, axis, up)
        after = lax.ppermute(first, axis, down)
        array = jnp.concatenate([before, array, after], axis=dim)
    return array


def shifted(value, axis, steps):
    count = lax.axis_size(axis)
    first, last = (max(0, -steps), min(count, count - steps))
    return lax.ppermute(value, axis, [(source, source + steps) for source in range(first, last)])


def laplace(padded_field, padded_kappa):
    centre_field = padded_field[1:-1, 1:-1, 1:-1]
    centre_kappa = padded_kappa[1:-1, 1:-1, 1:-1]
    total = jnp.zeros_like(centre_field)
    offsets = [(2, 1, 1), (0, 1, 1), (1, 2, 1), (1, 0, 1), (1, 1, 2), (1, 1, 0)]
    sx, sy, sz = centre_field.shape
    for ox, oy, oz in offsets:
        near_field = padded_field[ox : ox + sx, oy : oy + sy, oz : oz + sz]
        near_kappa = padded_kappa[ox : ox + sx, oy : oy + sy, oz : oz + sz]
        total = total + 0.5 * (centre_kappa + near_kappa) * (near_field - centre_field)
    return total


def advance(field, modes, padded_field, padded_kappa, source, step_size, decay, mode_weight):
    memory = jnp.einsum("m,mxyz->xyz", mode_weight, modes, precision=lax.Precision.HIGHEST)
    change = step_size * (laplace(padded_field, padded_kappa) - memory + source)
    new_modes = (
        decay[:, None, None, None] * modes + (1.0 - decay)[:, None, None, None] * change[None]
    )
    return (field + change, new_modes)


def depth_pad(block):
    return jnp.pad(block, ((0, 0), (0, 0), (1, 1)))


def per_device(field, modes, source, regions, region_kappa, mode_rate, mode_weight):
    start_u = field[0]
    start_h = modes[0]
    table = jnp.arange(region_kappa.shape[0], dtype=jnp.int32)
    kappa = jnp.sum(jnp.where(regions[..., None] == table, region_kappa, jnp.float32(0.0)), axis=-1)
    padded_kappa = depth_pad(padded_2(kappa, (("gx", 0), ("gy", 1)), 1))
    coarse_decay = jnp.exp(-mode_rate)
    fine_decay = jnp.exp(-mode_rate / SUBSTEPS)

    def fine_turn(turn, carry):
        now_u, now_h = carry
        padded = depth_pad(padded_2(now_u, (("gx", 0), ("gy", 1)), 1))
        return advance(
            now_u,
            now_h,
            padded,
            padded_kappa,
            source,
            coarse_size / SUBSTEPS,
            fine_decay,
            mode_weight,
        )

    fine_u, fine_h = lax.fori_loop(0, SUBSTEPS, fine_turn, (start_u, start_h))
    padded_start = depth_pad(padded_2(start_u, (("gx", 0), ("gy", 1)), 1))
    old_u, old_h = advance(
        start_u, start_h, padded_start, padded_kappa, source, coarse_size, coarse_decay, mode_weight
    )
    lift_u = coarse_size * source
    lift_h = (1.0 - coarse_decay)[:, None, None, None] * lift_u[None]
    first = lax.axis_index("tm") == 0
    base_u = jnp.where(first, fine_u, fine_u - old_u + lift_u)
    base_h = jnp.where(first, fine_h, fine_h - old_h + lift_h)

    def link_turn(turn, carry):
        now_u, now_h = carry
        came_u, came_h = shifted((now_u, now_h), "tm", 1)
        padded = depth_pad(padded_2(came_u, (("gx", 0), ("gy", 1)), 1))
        next_u, next_h = advance(
            came_u, came_h, padded, padded_kappa, 0.0, coarse_size, coarse_decay, mode_weight
        )
        return (base_u + next_u, base_h + next_h)

    end_u, end_h = lax.fori_loop(0, lax.axis_size("tm") - 1, link_turn, (base_u, base_h))
    diff = end_u - fine_u
    total = lax.psum(jnp.sum(diff * diff), ("gx", "gy"))
    cells = (
        end_u.shape[0] * lax.axis_size("gx") * end_u.shape[1] * lax.axis_size("gy") * end_u.shape[2]
    )
    size_now = jnp.sqrt(total / cells)
    return (end_u[None], end_h[None], size_now.reshape(1))


def solution(mesh):
    return jax.shard_map(
        per_device,
        mesh=mesh,
        in_specs=(
            P("tm", "gx", "gy", None),
            P("tm", None, "gx", "gy", None),
            P("gx", "gy", None),
            P("gx", "gy", None),
            P(),
            P(),
            P(),
        ),
        out_specs=(P("tm", "gx", "gy", None), P("tm", None, "gx", "gy", None), P("tm")),
        check_vma=False,
    )
```

profile of v0, /device:TPU:96, one launch (start us, length us, event | category | flops | bytes accessed | tf_op | source)
XLA Modules:
  0.0 476.8 jit_solution(12930270152823592963)
XLA Ops:
  30.8 34.2 %while.28 = (s32[]{:T(128)}, f32[8,8,256]{2,1,0:T(8,128)S(1)}, f32[16,8,8,256]{3,2,1,0:T(8,128)S(1)}, f32[8,8,256]{2,1,0:T(8,128)S(1)}, f32[8,8,256]{2,1,0:T(8,1...) while((s32[]{:T(128)}, f32[8,8,256]{2,1,0:T(8,128)S(1)}, ...), condition=%wide.region_2.3_spmd, body=%wide.region_1.2_spmd.sunk | while | flops 4646482 | bytes 4969853 | solution.py:80
  68.0 367.7 %while.29 = (s32[]{:T(128)}, f32[8,8,256]{2,1,0:T(8,128)S(1)}, f32[16,8,8,256]{3,2,1,0:T(8,128)}, f32[8,8,256]{2,1,0:T(8,128)S(1)}, f32[8,8,256]{2,1,0:T(8,128)S...) while((s32[]{:T(128)}, f32[8,8,256]{2,1,0:T(8,128)S(1)}, ...), condition=%wide.region_4.5_spmd, body=%wide.region_3.4_spmd.sunk | while | flops 4908626 | bytes 10343893 | solution.py:100
  70.0 5.1 %collective-permute-start.5 = (f32[16,8,8,256]{3,2,1,0:T(8,128)}, f32[16,8,8,256]{3,2,1,0:T(8,128)S(1)}, u32[]{:S(2)}, u32[]{:S(2)}) collective-permute-start(f32[16,8,8,256]{3,2,1,0:T(8,128)} %get-tuple-element.569), channel_id=1, source_target_pairs={{0,16},{16,32},{32,48},{48,64},{64,80},{80,96},{96,112},{112,128},... | collective-permute-start | bytes 3145736 | tf_op jit(solution)/shard_map/while/body/eval_jaxpr/ppermute | solution.py:28
  84.0 4.8 %collective-permute-start.9 = (f32[10,1,256]{2,1,0:T(1,128)S(1)}, f32[10,1,256]{2,1,0:T(1,128)S(1)}, u32[]{:S(2)}, u32[]{:S(2)}) collective-permute-start(f32[10,1,256]{2,1,0:T(1,128)S(1)} %get-tuple-element.511), channel_id=1, source_target_pairs={{0,1},{1,2},{2,3},{4,5},{5,6},{6,7},{8,9},{9,10},{10,11},{12,13},{... | collective-permute-start | bytes 30728 | tf_op jit(solution)/shard_map/while/body/eval_jaxpr/ppermute | solution.py:19
  94.8 4.8 %collective-permute-start.5 = (f32[16,8,8,256]{3,2,1,0:T(8,128)}, f32[16,8,8,256]{3,2,1,0:T(8,128)S(1)}, u32[]{:S(2)}, u32[]{:S(2)}) collective-permute-start(f32[16,8,8,256]{3,2,1,0:T(8,128)} %get-tuple-element.569), channel_id=1, source_target_pairs={{0,16},{16,32},{32,48},{48,64},{64,80},{80,96},{96,112},{112,128},... | collective-permute-start | bytes 3145736 | tf_op jit(solution)/shard_map/while/body/eval_jaxpr/ppermute | solution.py:28
  108.5 4.8 %collective-permute-start.9 = (f32[10,1,256]{2,1,0:T(1,128)S(1)}, f32[10,1,256]{2,1,0:T(1,128)S(1)}, u32[]{:S(2)}, u32[]{:S(2)}) collective-permute-start(f32[10,1,256]{2,1,0:T(1,128)S(1)} %get-tuple-element.511), channel_id=1, source_target_pairs={{0,1},{1,2},{2,3},{4,5},{5,6},{6,7},{8,9},{9,10},{10,11},{12,13},{... | collective-permute-start | bytes 30728 | tf_op jit(solution)/shard_map/while/body/eval_jaxpr/ppermute | solution.py:19
  119.3 4.8 %collective-permute-start.5 = (f32[16,8,8,256]{3,2,1,0:T(8,128)}, f32[16,8,8,256]{3,2,1,0:T(8,128)S(1)}, u32[]{:S(2)}, u32[]{:S(2)}) collective-permute-start(f32[16,8,8,256]{3,2,1,0:T(8,128)} %get-tuple-element.569), channel_id=1, source_target_pairs={{0,16},{16,32},{32,48},{48,64},{64,80},{80,96},{96,112},{112,128},... | collective-permute-start | bytes 3145736 | tf_op jit(solution)/shard_map/while/body/eval_jaxpr/ppermute | solution.py:28
  143.8 4.8 %collective-permute-start.5 = (f32[16,8,8,256]{3,2,1,0:T(8,128)}, f32[16,8,8,256]{3,2,1,0:T(8,128)S(1)}, u32[]{:S(2)}, u32[]{:S(2)}) collective-permute-start(f32[16,8,8,256]{3,2,1,0:T(8,128)} %get-tuple-element.569), channel_id=1, source_target_pairs={{0,16},{16,32},{32,48},{48,64},{64,80},{80,96},{96,112},{112,128},... | collective-permute-start | bytes 3145736 | tf_op jit(solution)/shard_map/while/body/eval_jaxpr/ppermute | solution.py:28
  168.2 4.8 %collective-permute-start.5 = (f32[16,8,8,256]{3,2,1,0:T(8,128)}, f32[16,8,8,256]{3,2,1,0:T(8,128)S(1)}, u32[]{:S(2)}, u32[]{:S(2)}) collective-permute-start(f32[16,8,8,256]{3,2,1,0:T(8,128)} %get-tuple-element.569), channel_id=1, source_target_pairs={{0,16},{16,32},{32,48},{48,64},{64,80},{80,96},{96,112},{112,128},... | collective-permute-start | bytes 3145736 | tf_op jit(solution)/shard_map/while/body/eval_jaxpr/ppermute | solution.py:28
  192.7 4.8 %collective-permute-start.5 = (f32[16,8,8,256]{3,2,1,0:T(8,128)}, f32[16,8,8,256]{3,2,1,0:T(8,128)S(1)}, u32[]{:S(2)}, u32[]{:S(2)}) collective-permute-start(f32[16,8,8,256]{3,2,1,0:T(8,128)} %get-tuple-element.569), channel_id=1, source_target_pairs={{0,16},{16,32},{32,48},{48,64},{64,80},{80,96},{96,112},{112,128},... | collective-permute-start | bytes 3145736 | tf_op jit(solution)/shard_map/while/body/eval_jaxpr/ppermute | solution.py:28
  206.4 4.8 %collective-permute-start.9 = (f32[10,1,256]{2,1,0:T(1,128)S(1)}, f32[10,1,256]{2,1,0:T(1,128)S(1)}, u32[]{:S(2)}, u32[]{:S(2)}) collective-permute-start(f32[10,1,256]{2,1,0:T(1,128)S(1)} %get-tuple-element.511), channel_id=1, source_target_pairs={{0,1},{1,2},{2,3},{4,5},{5,6},{6,7},{8,9},{9,10},{10,11},{12,13},{... | collective-permute-start | bytes 30728 | tf_op jit(solution)/shard_map/while/body/eval_jaxpr/ppermute | solution.py:19
  217.2 4.8 %collective-permute-start.5 = (f32[16,8,8,256]{3,2,1,0:T(8,128)}, f32[16,8,8,256]{3,2,1,0:T(8,128)S(1)}, u32[]{:S(2)}, u32[]{:S(2)}) collective-permute-start(f32[16,8,8,256]{3,2,1,0:T(8,128)} %get-tuple-element.569), channel_id=1, source_target_pairs={{0,16},{16,32},{32,48},{48,64},{64,80},{80,96},{96,112},{112,128},... | collective-permute-start | bytes 3145736 | tf_op jit(solution)/shard_map/while/body/eval_jaxpr/ppermute | solution.py:28
  241.7 4.8 %collective-permute-start.5 = (f32[16,8,8,256]{3,2,1,0:T(8,128)}, f32[16,8,8,256]{3,2,1,0:T(8,128)S(1)}, u32[]{:S(2)}, u32[]{:S(2)}) collective-permute-start(f32[16,8,8,256]{3,2,1,0:T(8,128)} %get-tuple-element.569), channel_id=1, source_target_pairs={{0,16},{16,32},{32,48},{48,64},{64,80},{80,96},{96,112},{112,128},... | collective-permute-start | bytes 3145736 | tf_op jit(solution)/shard_map/while/body/eval_jaxpr/ppermute | solution.py:28
  266.2 4.8 %collective-permute-start.5 = (f32[16,8,8,256]{3,2,1,0:T(8,128)}, f32[16,8,8,256]{3,2,1,0:T(8,128)S(1)}, u32[]{:S(2)}, u32[]{:S(2)}) collective-permute-start(f32[16,8,8,256]{3,2,1,0:T(8,128)} %get-tuple-element.569), channel_id=1, source_target_pairs={{0,16},{16,32},{32,48},{48,64},{64,80},{80,96},{96,112},{112,128},... | collective-permute-start | bytes 3145736 | tf_op jit(solution)/shard_map/while/body/eval_jaxpr/ppermute | solution.py:28
  279.8 4.8 %collective-permute-start.9 = (f32[10,1,256]{2,1,0:T(1,128)S(1)}, f32[10,1,256]{2,1,0:T(1,128)S(1)}, u32[]{:S(2)}, u32[]{:S(2)}) collective-permute-start(f32[10,1,256]{2,1,0:T(1,128)S(1)} %get-tuple-element.511), channel_id=1, source_target_pairs={{0,1},{1,2},{2,3},{4,5},{5,6},{6,7},{8,9},{9,10},{10,11},{12,13},{... | collective-permute-start | bytes 30728 | tf_op jit(solution)/shard_map/while/body/eval_jaxpr/ppermute | solution.py:19
  290.7 4.8 %collective-permute-start.5 = (f32[16,8,8,256]{3,2,1,0:T(8,128)}, f32[16,8,8,256]{3,2,1,0:T(8,128)S(1)}, u32[]{:S(2)}, u32[]{:S(2)}) collective-permute-start(f32[16,8,8,256]{3,2,1,0:T(8,128)} %get-tuple-element.569), channel_id=1, source_target_pairs={{0,16},{16,32},{32,48},{48,64},{64,80},{80,96},{96,112},{112,128},... | collective-permute-start | bytes 3145736 | tf_op jit(solution)/shard_map/while/body/eval_jaxpr/ppermute | solution.py:28
  315.1 4.8 %collective-permute-start.5 = (f32[16,8,8,256]{3,2,1,0:T(8,128)}, f32[16,8,8,256]{3,2,1,0:T(8,128)S(1)}, u32[]{:S(2)}, u32[]{:S(2)}) collective-permute-start(f32[16,8,8,256]{3,2,1,0:T(8,128)} %get-tuple-element.569), channel_id=1, source_target_pairs={{0,16},{16,32},{32,48},{48,64},{64,80},{80,96},{96,112},{112,128},... | collective-permute-start | bytes 3145736 | tf_op jit(solution)/shard_map/while/body/eval_jaxpr/ppermute | solution.py:28
  339.6 4.8 %collective-permute-start.5 = (f32[16,8,8,256]{3,2,1,0:T(8,128)}, f32[16,8,8,256]{3,2,1,0:T(8,128)S(1)}, u32[]{:S(2)}, u32[]{:S(2)}) collective-permute-start(f32[16,8,8,256]{3,2,1,0:T(8,128)} %get-tuple-element.569), channel_id=1, source_target_pairs={{0,16},{16,32},{32,48},{48,64},{64,80},{80,96},{96,112},{112,128},... | collective-permute-start | bytes 3145736 | tf_op jit(solution)/shard_map/while/body/eval_jaxpr/ppermute | solution.py:28
  353.3 4.8 %collective-permute-start.9 = (f32[10,1,256]{2,1,0:T(1,128)S(1)}, f32[10,1,256]{2,1,0:T(1,128)S(1)}, u32[]{:S(2)}, u32[]{:S(2)}) collective-permute-start(f32[10,1,256]{2,1,0:T(1,128)S(1)} %get-tuple-element.511), channel_id=1, source_target_pairs={{0,1},{1,2},{2,3},{4,5},{5,6},{6,7},{8,9},{9,10},{10,11},{12,13},{... | collective-permute-start | bytes 30728 | tf_op jit(solution)/shard_map/while/body/eval_jaxpr/ppermute | solution.py:19
  364.1 4.8 %collective-permute-start.5 = (f32[16,8,8,256]{3,2,1,0:T(8,128)}, f32[16,8,8,256]{3,2,1,0:T(8,128)S(1)}, u32[]{:S(2)}, u32[]{:S(2)}) collective-permute-start(f32[16,8,8,256]{3,2,1,0:T(8,128)} %get-tuple-element.569), channel_id=1, source_target_pairs={{0,16},{16,32},{32,48},{48,64},{64,80},{80,96},{96,112},{112,128},... | collective-permute-start | bytes 3145736 | tf_op jit(solution)/shard_map/while/body/eval_jaxpr/ppermute | solution.py:28
  388.6 4.8 %collective-permute-start.5 = (f32[16,8,8,256]{3,2,1,0:T(8,128)}, f32[16,8,8,256]{3,2,1,0:T(8,128)S(1)}, u32[]{:S(2)}, u32[]{:S(2)}) collective-permute-start(f32[16,8,8,256]{3,2,1,0:T(8,128)} %get-tuple-element.569), channel_id=1, source_target_pairs={{0,16},{16,32},{32,48},{48,64},{64,80},{80,96},{96,112},{112,128},... | collective-permute-start | bytes 3145736 | tf_op jit(solution)/shard_map/while/body/eval_jaxpr/ppermute | solution.py:28
  413.1 4.8 %collective-permute-start.5 = (f32[16,8,8,256]{3,2,1,0:T(8,128)}, f32[16,8,8,256]{3,2,1,0:T(8,128)S(1)}, u32[]{:S(2)}, u32[]{:S(2)}) collective-permute-start(f32[16,8,8,256]{3,2,1,0:T(8,128)} %get-tuple-element.569), channel_id=1, source_target_pairs={{0,16},{16,32},{32,48},{48,64},{64,80},{80,96},{96,112},{112,128},... | collective-permute-start | bytes 3145736 | tf_op jit(solution)/shard_map/while/body/eval_jaxpr/ppermute | solution.py:28
  426.7 4.8 %collective-permute-start.9 = (f32[10,1,256]{2,1,0:T(1,128)S(1)}, f32[10,1,256]{2,1,0:T(1,128)S(1)}, u32[]{:S(2)}, u32[]{:S(2)}) collective-permute-start(f32[10,1,256]{2,1,0:T(1,128)S(1)} %get-tuple-element.511), channel_id=1, source_target_pairs={{0,1},{1,2},{2,3},{4,5},{5,6},{6,7},{8,9},{9,10},{10,11},{12,13},{... | collective-permute-start | bytes 30728 | tf_op jit(solution)/shard_map/while/body/eval_jaxpr/ppermute | solution.py:19
  436.3 38.7 %psum.7 = f32[]{:T(128)} all-reduce(f32[]{:T(128)} %multiply_reduce_fusion), channel_id=1, replica_groups=mesh['tm'=16,'gx'=4,'gy'=4] {'gx','gy'}, use_global_device_ids=true, to_apply=%region_6.7 | all-reduce | flops 1 | bytes 8 | tf_op jit(solution)/shard_map/psum | solution.py:102
  (405 shorter events, 331.7 us)
Async XLA Ops:
  1.9 14.9 %collective-permute-start.10 = (f32[1,8,256]{2,1,0:T(8,128)S(1)}, f32[1,8,256]{2,1,0:T(8,128)S(1)}, u32[]{:S(2)}, u32[]{:S(2)}) collective-permute-start(f32[1,8,256]{2,1,0:T(8,128)S(1)} %get-tuple-element.334), channel_id=1, source_target_pairs={{4,0},{8,4},{12,8},{5,1},{9,5},{13,9},{6,2},{10,6},{14,10},{7,3},{... | collective-permute-start | bytes 24584 | tf_op jit(solution)/shard_map/ppermute | solution.py:20
  3.2 13.7 %collective-permute-start.11 = (f32[1,8,256]{2,1,0:T(8,128)S(1)}, f32[1,8,256]{2,1,0:T(8,128)S(1)}, u32[]{:S(2)}, u32[]{:S(2)}) collective-permute-start(f32[1,8,256]{2,1,0:T(8,128)S(1)} %get-tuple-element.333), channel_id=1, source_target_pairs={{0,4},{4,8},{8,12},{1,5},{5,9},{9,13},{2,6},{6,10},{10,14},{3,7},{... | collective-permute-start | bytes 24584 | tf_op jit(solution)/shard_map/ppermute | solution.py:19
  7.7 15.0 %collective-permute-start.14 = (f32[1,8,256]{2,1,0:T(8,128)S(1)}, f32[1,8,256]{2,1,0:T(8,128)S(1)}, u32[]{:S(2)}, u32[]{:S(2)}) collective-permute-start(f32[1,8,256]{2,1,0:T(8,128)S(1)} %get-tuple-element.328), channel_id=1, source_target_pairs={{4,0},{8,4},{12,8},{5,1},{9,5},{13,9},{6,2},{10,6},{14,10},{7,3},{... | collective-permute-start | bytes 24584 | tf_op jit(solution)/shard_map/ppermute | solution.py:20
  9.0 13.7 %collective-permute-start.15 = (f32[1,8,256]{2,1,0:T(8,128)S(1)}, f32[1,8,256]{2,1,0:T(8,128)S(1)}, u32[]{:S(2)}, u32[]{:S(2)}) collective-permute-start(f32[1,8,256]{2,1,0:T(8,128)S(1)} %get-tuple-element.327), channel_id=1, source_target_pairs={{0,4},{4,8},{8,12},{1,5},{5,9},{9,13},{2,6},{6,10},{10,14},{3,7},{... | collective-permute-start | bytes 24584 | tf_op jit(solution)/shard_map/ppermute | solution.py:19
  16.8 11.8 %collective-permute-start.12 = (f32[10,1,256]{2,1,0:T(1,128)S(1)}, f32[10,1,256]{2,1,0:T(1,128)S(1)}, u32[]{:S(2)}, u32[]{:S(2)}) collective-permute-start(f32[10,1,256]{2,1,0:T(1,128)S(1)} %get-tuple-element.324), channel_id=1, source_target_pairs={{1,0},{2,1},{3,2},{5,4},{6,5},{7,6},{9,8},{10,9},{11,10},{13,12},{... | collective-permute-start | bytes 30728 | tf_op jit(solution)/shard_map/ppermute | solution.py:20
  18.1 10.5 %collective-permute-start.13 = (f32[10,1,256]{2,1,0:T(1,128)S(1)}, f32[10,1,256]{2,1,0:T(1,128)S(1)}, u32[]{:S(2)}, u32[]{:S(2)}) collective-permute-start(f32[10,1,256]{2,1,0:T(1,128)S(1)} %get-tuple-element.323), channel_id=1, source_target_pairs={{0,1},{1,2},{2,3},{4,5},{5,6},{6,7},{8,9},{9,10},{10,11},{12,13},{... | collective-permute-start | bytes 30728 | tf_op jit(solution)/shard_map/ppermute | solution.py:19
  68.0 7.2 %collective-permute-start.4 = (f32[8,8,256]{2,1,0:T(8,128)S(1)}, f32[8,8,256]{2,1,0:T(8,128)S(1)}, u32[]{:S(2)}, u32[]{:S(2)}) collective-permute-start(f32[8,8,256]{2,1,0:T(8,128)S(1)} %get-tuple-element.568), channel_id=1, source_target_pairs={{0,16},{16,32},{32,48},{48,64},{64,80},{80,96},{96,112},{112,128},... | collective-permute-start | bytes 196616 | tf_op jit(solution)/shard_map/while/body/eval_jaxpr/ppermute | solution.py:28
  70.0 20.4 %collective-permute-start.5 = (f32[16,8,8,256]{3,2,1,0:T(8,128)}, f32[16,8,8,256]{3,2,1,0:T(8,128)S(1)}, u32[]{:S(2)}, u32[]{:S(2)}) collective-permute-start(f32[16,8,8,256]{3,2,1,0:T(8,128)} %get-tuple-element.569), channel_id=1, source_target_pairs={{0,16},{16,32},{32,48},{48,64},{64,80},{80,96},{96,112},{112,128},... | collective-permute-start | bytes 3145736 | tf_op jit(solution)/shard_map/while/body/eval_jaxpr/ppermute | solution.py:28
  94.8 20.1 %collective-permute-start.5 = (f32[16,8,8,256]{3,2,1,0:T(8,128)}, f32[16,8,8,256]{3,2,1,0:T(8,128)S(1)}, u32[]{:S(2)}, u32[]{:S(2)}) collective-permute-start(f32[16,8,8,256]{3,2,1,0:T(8,128)} %get-tuple-element.569), channel_id=1, source_target_pairs={{0,16},{16,32},{32,48},{48,64},{64,80},{80,96},{96,112},{112,128},... | collective-permute-start | bytes 3145736 | tf_op jit(solution)/shard_map/while/body/eval_jaxpr/ppermute | solution.py:28
  119.3 20.1 %collective-permute-start.5 = (f32[16,8,8,256]{3,2,1,0:T(8,128)}, f32[16,8,8,256]{3,2,1,0:T(8,128)S(1)}, u32[]{:S(2)}, u32[]{:S(2)}) collective-permute-start(f32[16,8,8,256]{3,2,1,0:T(8,128)} %get-tuple-element.569), channel_id=1, source_target_pairs={{0,16},{16,32},{32,48},{48,64},{64,80},{80,96},{96,112},{112,128},... | collective-permute-start | bytes 3145736 | tf_op jit(solution)/shard_map/while/body/eval_jaxpr/ppermute | solution.py:28
  143.8 20.1 %collective-permute-start.5 = (f32[16,8,8,256]{3,2,1,0:T(8,128)}, f32[16,8,8,256]{3,2,1,0:T(8,128)S(1)}, u32[]{:S(2)}, u32[]{:S(2)}) collective-permute-start(f32[16,8,8,256]{3,2,1,0:T(8,128)} %get-tuple-element.569), channel_id=1, source_target_pairs={{0,16},{16,32},{32,48},{48,64},{64,80},{80,96},{96,112},{112,128},... | collective-permute-start | bytes 3145736 | tf_op jit(solution)/shard_map/while/body/eval_jaxpr/ppermute | solution.py:28
  168.2 20.1 %collective-permute-start.5 = (f32[16,8,8,256]{3,2,1,0:T(8,128)}, f32[16,8,8,256]{3,2,1,0:T(8,128)S(1)}, u32[]{:S(2)}, u32[]{:S(2)}) collective-permute-start(f32[16,8,8,256]{3,2,1,0:T(8,128)} %get-tuple-element.569), channel_id=1, source_target_pairs={{0,16},{16,32},{32,48},{48,64},{64,80},{80,96},{96,112},{112,128},... | collective-permute-start | bytes 3145736 | tf_op jit(solution)/shard_map/while/body/eval_jaxpr/ppermute | solution.py:28
  190.8 6.8 %collective-permute-start.4 = (f32[8,8,256]{2,1,0:T(8,128)S(1)}, f32[8,8,256]{2,1,0:T(8,128)S(1)}, u32[]{:S(2)}, u32[]{:S(2)}) collective-permute-start(f32[8,8,256]{2,1,0:T(8,128)S(1)} %get-tuple-element.568), channel_id=1, source_target_pairs={{0,16},{16,32},{32,48},{48,64},{64,80},{80,96},{96,112},{112,128},... | collective-permute-start | bytes 196616 | tf_op jit(solution)/shard_map/while/body/eval_jaxpr/ppermute | solution.py:28
  192.7 20.1 %collective-permute-start.5 = (f32[16,8,8,256]{3,2,1,0:T(8,128)}, f32[16,8,8,256]{3,2,1,0:T(8,128)S(1)}, u32[]{:S(2)}, u32[]{:S(2)}) collective-permute-start(f32[16,8,8,256]{3,2,1,0:T(8,128)} %get-tuple-element.569), channel_id=1, source_target_pairs={{0,16},{16,32},{32,48},{48,64},{64,80},{80,96},{96,112},{112,128},... | collective-permute-start | bytes 3145736 | tf_op jit(solution)/shard_map/while/body/eval_jaxpr/ppermute | solution.py:28
  217.2 20.1 %collective-permute-start.5 = (f32[16,8,8,256]{3,2,1,0:T(8,128)}, f32[16,8,8,256]{3,2,1,0:T(8,128)S(1)}, u32[]{:S(2)}, u32[]{:S(2)}) collective-permute-start(f32[16,8,8,256]{3,2,1,0:T(8,128)} %get-tuple-element.569), channel_id=1, source_target_pairs={{0,16},{16,32},{32,48},{48,64},{64,80},{80,96},{96,112},{112,128},... | collective-permute-start | bytes 3145736 | tf_op jit(solution)/shard_map/while/body/eval_jaxpr/ppermute | solution.py:28
  241.7 20.1 %collective-permute-start.5 = (f32[16,8,8,256]{3,2,1,0:T(8,128)}, f32[16,8,8,256]{3,2,1,0:T(8,128)S(1)}, u32[]{:S(2)}, u32[]{:S(2)}) collective-permute-start(f32[16,8,8,256]{3,2,1,0:T(8,128)} %get-tuple-element.569), channel_id=1, source_target_pairs={{0,16},{16,32},{32,48},{48,64},{64,80},{80,96},{96,112},{112,128},... | collective-permute-start | bytes 3145736 | tf_op jit(solution)/shard_map/while/body/eval_jaxpr/ppermute | solution.py:28
  264.3 6.8 %collective-permute-start.4 = (f32[8,8,256]{2,1,0:T(8,128)S(1)}, f32[8,8,256]{2,1,0:T(8,128)S(1)}, u32[]{:S(2)}, u32[]{:S(2)}) collective-permute-start(f32[8,8,256]{2,1,0:T(8,128)S(1)} %get-tuple-element.568), channel_id=1, source_target_pairs={{0,16},{16,32},{32,48},{48,64},{64,80},{80,96},{96,112},{112,128},... | collective-permute-start | bytes 196616 | tf_op jit(solution)/shard_map/while/body/eval_jaxpr/ppermute | solution.py:28
  266.2 20.1 %collective-permute-start.5 = (f32[16,8,8,256]{3,2,1,0:T(8,128)}, f32[16,8,8,256]{3,2,1,0:T(8,128)S(1)}, u32[]{:S(2)}, u32[]{:S(2)}) collective-permute-start(f32[16,8,8,256]{3,2,1,0:T(8,128)} %get-tuple-element.569), channel_id=1, source_target_pairs={{0,16},{16,32},{32,48},{48,64},{64,80},{80,96},{96,112},{112,128},... | collective-permute-start | bytes 3145736 | tf_op jit(solution)/shard_map/while/body/eval_jaxpr/ppermute | solution.py:28
  290.7 20.1 %collective-permute-start.5 = (f32[16,8,8,256]{3,2,1,0:T(8,128)}, f32[16,8,8,256]{3,2,1,0:T(8,128)S(1)}, u32[]{:S(2)}, u32[]{:S(2)}) collective-permute-start(f32[16,8,8,256]{3,2,1,0:T(8,128)} %get-tuple-element.569), channel_id=1, source_target_pairs={{0,16},{16,32},{32,48},{48,64},{64,80},{80,96},{96,112},{112,128},... | collective-permute-start | bytes 3145736 | tf_op jit(solution)/shard_map/while/body/eval_jaxpr/ppermute | solution.py:28
  315.1 20.1 %collective-permute-start.5 = (f32[16,8,8,256]{3,2,1,0:T(8,128)}, f32[16,8,8,256]{3,2,1,0:T(8,128)S(1)}, u32[]{:S(2)}, u32[]{:S(2)}) collective-permute-start(f32[16,8,8,256]{3,2,1,0:T(8,128)} %get-tuple-element.569), channel_id=1, source_target_pairs={{0,16},{16,32},{32,48},{48,64},{64,80},{80,96},{96,112},{112,128},... | collective-permute-start | bytes 3145736 | tf_op jit(solution)/shard_map/while/body/eval_jaxpr/ppermute | solution.py:28
  339.6 20.1 %collective-permute-start.5 = (f32[16,8,8,256]{3,2,1,0:T(8,128)}, f32[16,8,8,256]{3,2,1,0:T(8,128)S(1)}, u32[]{:S(2)}, u32[]{:S(2)}) collective-permute-start(f32[16,8,8,256]{3,2,1,0:T(8,128)} %get-tuple-element.569), channel_id=1, source_target_pairs={{0,16},{16,32},{32,48},{48,64},{64,80},{80,96},{96,112},{112,128},... | collective-permute-start | bytes 3145736 | tf_op jit(solution)/shard_map/while/body/eval_jaxpr/ppermute | solution.py:28
  364.1 20.1 %collective-permute-start.5 = (f32[16,8,8,256]{3,2,1,0:T(8,128)}, f32[16,8,8,256]{3,2,1,0:T(8,128)S(1)}, u32[]{:S(2)}, u32[]{:S(2)}) collective-permute-start(f32[16,8,8,256]{3,2,1,0:T(8,128)} %get-tuple-element.569), channel_id=1, source_target_pairs={{0,16},{16,32},{32,48},{48,64},{64,80},{80,96},{96,112},{112,128},... | collective-permute-start | bytes 3145736 | tf_op jit(solution)/shard_map/while/body/eval_jaxpr/ppermute | solution.py:28
  388.6 20.1 %collective-permute-start.5 = (f32[16,8,8,256]{3,2,1,0:T(8,128)}, f32[16,8,8,256]{3,2,1,0:T(8,128)S(1)}, u32[]{:S(2)}, u32[]{:S(2)}) collective-permute-start(f32[16,8,8,256]{3,2,1,0:T(8,128)} %get-tuple-element.569), channel_id=1, source_target_pairs={{0,16},{16,32},{32,48},{48,64},{64,80},{80,96},{96,112},{112,128},... | collective-permute-start | bytes 3145736 | tf_op jit(solution)/shard_map/while/body/eval_jaxpr/ppermute | solution.py:28
  413.1 20.1 %collective-permute-start.5 = (f32[16,8,8,256]{3,2,1,0:T(8,128)}, f32[16,8,8,256]{3,2,1,0:T(8,128)S(1)}, u32[]{:S(2)}, u32[]{:S(2)}) collective-permute-start(f32[16,8,8,256]{3,2,1,0:T(8,128)} %get-tuple-element.569), channel_id=1, source_target_pairs={{0,16},{16,32},{32,48},{48,64},{64,80},{80,96},{96,112},{112,128},... | collective-permute-start | bytes 3145736 | tf_op jit(solution)/shard_map/while/body/eval_jaxpr/ppermute | solution.py:28
  (94 other events, 869.9 us)
where the time goes:
time: 480 us; the launch traced here: 477 us
  starting transfers between devices  287 us (60%)
  waiting for transfers between devices  93.7 us (20%)
  blocking collectives  38.7 us (8%)
  other arithmetic  27.2 us (6%)
  matrix products  22.4 us (5%)
    ppermute x38, starting transfers between devices, padded_2(): before = lax.ppermute(last, axis, up)  136 us
    ppermute x30, starting transfers between devices, shifted(): lax.ppermute(value, axis, [(source, source + steps) for source in range(f...  102 us
    ppermute x38, waiting for transfers between devices, padded_2(): after = lax.ppermute(first, axis, down)  68.9 us
    ppermute x38, starting transfers between devices, padded_2(): after = lax.ppermute(first, axis, down)  49.1 us
    psum x1, blocking collectives, per_device(): total = lax.psum(jnp.sum(diff * diff), ('gx', 'gy'))  38.7 us
    ppermute x38, waiting for transfers between devices, padded_2(): before = lax.ppermute(last, axis, up)  24.7 us
    dot_general x18, matrix products, advance(): jnp.einsum('m,mxyz->xyz', mode_weight, modes, precision=lax.Precision.HIG...  22.4 us
    add x30, other arithmetic, link_turn(): return (base_u + next_u, base_h + next_h)  19.6 us
  transfers between devices with their start and end apart: 106, of which 35 were waited for; matrix products, arithmetic and copies ran while one was open for 2% of the time, Pallas kernels for 0%

commit v1 on v0

v1 whole, which is shorter than its diff:
```python
import functools
import jax
import jax.numpy as jnp
from jax import lax
from jax.experimental import pallas as pl
from jax.experimental.pallas import tpu as pltpu
from jax.sharding import PartitionSpec as P

STEP = 0.12
F32 = jnp.float32
VM = pl.BlockSpec(memory_space=pltpu.VMEM)
SM = pl.BlockSpec(memory_space=pltpu.SMEM)
PARAMS = pltpu.CompilerParams(vmem_limit_bytes=40 * 1024 * 1024)
HALO = 15
TRI = [HALO] + [HALO - j for j in range(1, HALO)]
OFF = [sum(TRI[:j]) for j in range(HALO)]
KOFF = sum(TRI)
MSG = KOFF + HALO
LAY = 48
NEW = 46


def call(kernel, outs, ins, smem, scratch=()):
    return pl.pallas_call(
        kernel,
        out_shape=[jax.ShapeDtypeStruct(shape, F32) for shape in outs],
        in_specs=[SM] * smem + [VM] * (ins - smem),
        out_specs=[VM] * len(outs),
        scratch_shapes=[pltpu.VMEM(shape, F32) for shape in scratch],
        compiler_params=PARAMS,
    )


def lane_low(shape):
    return lax.broadcasted_iota(jnp.int32, shape, len(shape) - 1) < 64


def local_kernel(rk, w, wf, u, reg, s, modes, kap, g0, q1s, up, dn):
    for x in range(8):
        rows = slice(8 * x, 8 * x + 8)
        region = reg[rows]
        k = jnp.zeros((8, 256), F32)
        for r in range(8):
            k = jnp.where(region == r, rk[r], k)
        kap[rows] = k
        a = jnp.zeros((8, 256), F32)
        b = jnp.zeros((8, 256), F32)
        for m in range(16):
            h = modes[m, rows]
            a += w[m] * h
            b += wf[m] * h
        g0[rows] = s[rows] - a
        q1s[rows] = s[rows] - b
    up[0:16] = u[48:64]
    up[16:32] = kap[48:64]
    up[32:40] = g0[56:64]
    dn[0:16] = u[0:16]
    dn[16:32] = kap[0:16]
    dn[32:40] = g0[0:8]


def scatter_pack_kernel(at, u, s, kap, modes, sk, packed):
    sk[...] = jnp.concatenate([s[...], kap[...]], axis=0).T

    @pl.when(at[0] == 0)
    def _():
        for m in range(8):
            both = jnp.concatenate([modes[m], modes[m + 8]], axis=0).T
            packed[:, 16 * m : 16 * m + 16] = both.reshape(16, 16, 128)
        both = jnp.concatenate([u[...], u[...]], axis=0).T
        packed[:, 128:144] = both.reshape(16, 16, 128)


def side_kernel(at, u, kap, g0, xlo, xhi, yup, ydn):
    has_lo = jnp.where(at[1] > 0, 1.0, 0.0).astype(F32)
    has_hi = jnp.where(at[1] < 3, 1.0, 0.0).astype(F32)
    for out, first in ((yup, 6), (ydn, 0)):
        for piece in range(5):
            if piece < 4:
                src, base = (u, 0) if piece < 2 else (kap, 16)
                y = first + piece % 2
                out[16 * piece : 16 * piece + 1] = has_lo * xlo[base + 8 + y : base + 9 + y]
                out[16 * piece + 9 : 16 * piece + 10] = has_hi * xhi[base + y : base + y + 1]
            else:
                src = g0
                y = 7 if first else 0
            for x in range(8):
                at_row = 16 * piece + 1 + x
                out[at_row : at_row + 1] = src[8 * x + y : 8 * x + y + 1]


def fine_kernel(at, omega, u, kap, g0, q1s, xlo, xhi, ylo, yhi, fine, both, up, kp, gp, u1):
    gx, gy = at[1], at[2]
    zero = jnp.zeros((24, 256), F32)
    for ref in (up, kp, gp):
        for x in range(12):
            ref[x] = zero
    for x in range(8):
        rows = slice(8 * x, 8 * x + 8)
        up[2 + x, 8:16] = u[rows]
        kp[2 + x, 8:16] = kap[rows]
        gp[2 + x, 8:16] = g0[rows]

    @pl.when(gx > 0)
    def _():
        for i in range(2):
            up[i, 8:16] = xlo[8 * i : 8 * i + 8]
            kp[i, 8:16] = xlo[16 + 8 * i : 24 + 8 * i]
        gp[1, 8:16] = xlo[32:40]

    @pl.when(gx < 3)
    def _():
        for i in range(2):
            up[10 + i, 8:16] = xhi[8 * i : 8 * i + 8]
            kp[10 + i, 8:16] = xhi[16 + 8 * i : 24 + 8 * i]
        gp[10, 8:16] = xhi[32:40]

    for cond, ref, row in ((gy > 0, ylo, 6), (gy < 3, yhi, 16)):

        @pl.when(cond)
        def _(ref=ref, row=row):
            for x in range(10):
                for i in range(2):
                    up[1 + x, row + i : row + i + 1] = ref[16 * i + x : 16 * i + x + 1]
                    kp[1 + x, row + i : row + i + 1] = ref[32 + 16 * i + x : 33 + 16 * i + x]
                if 1 <= x <= 8:
                    near = 7 if row == 6 else 16
                    gp[1 + x, near : near + 1] = ref[64 + x : 65 + x]

    z = lax.broadcasted_iota(jnp.int32, (24, 256), 1)

    def above(v):
        return jnp.where(z == 255, 0.0, pltpu.roll(v, 255, 1))

    def below(v):
        return jnp.where(z == 0, 0.0, pltpu.roll(v, 1, 1))

    def laplace(ref, x):
        uc, kc = ref[x], kp[x]
        total = jnp.zeros((24, 256), F32)
        for near_u, near_k in (
            (ref[x + 1], kp[x + 1]),
            (ref[x - 1], kp[x - 1]),
            (pltpu.roll(uc, 23, 0), pltpu.roll(kc, 23, 0)),
            (pltpu.roll(uc, 1, 0), pltpu.roll(kc, 1, 0)),
            (above(uc), above(kc)),
            (below(uc), below(kc)),
        ):
            total += (kc + near_k) * (near_u - uc)
        return 0.5 * total

    for x in range(1, 11):
        change = (0.5 * STEP) * (laplace(up, x) + gp[x])
        u1[x] = up[x] + change
        gp[x] = change

    @pl.when(gx == 0)
    def _():
        u1[1] = zero

    @pl.when(gx == 3)
    def _():
        u1[10] = zero

    @pl.when(gy == 0)
    def _():
        for x in range(1, 11):
            u1[x, 0:8] = zero[0:8]

    @pl.when(gy == 3)
    def _():
        for x in range(1, 11):
            u1[x, 16:24] = zero[0:8]

    first, second = [], []
    for x in range(8):
        rows = slice(8 * x, 8 * x + 8)
        c1 = gp[2 + x, 8:16]
        lap = laplace(u1, 2 + x)[8:16]
        c2 = (0.5 * STEP) * (lap + q1s[rows] - omega[0] * c1)
        fine[rows] = u1[2 + x, 8:16] + c2
        first.append(c1)
        second.append(c2)
    both[...] = jnp.concatenate(first + second, axis=0).T


def doubled(v, low):
    turned = pltpu.roll(v, 64, 1)
    return jnp.where(low, v, turned), jnp.where(low, turned, v)


def known_kernel(at, parts, sk, start, coef, msg, known):
    low = lane_low((16, 128))
    slab = sk[pl.ds(pl.multiple_of(at[0] * 16, 16), 16), :]
    source, kap = doubled(slab, low)
    h = [start[16 * m : 16 * m + 16] for m in range(8)]
    field = start[128:144]
    seen = []
    for j in range(16):
        c1, c2 = doubled(parts[j], low)
        if j == 0:
            n = 2.0 * c1
            seen.append(field + c1 + c2)
        else:
            q = coef[24:25] * h[0]
            for m in range(1, 8):
                q += coef[24 + m : 25 + m] * h[m]
            n = STEP * (source - (q + pltpu.roll(q, 64, 1)))
            seen.append(n + c2 - c1)
        known[j] = n
        xn = c2 - 2.0 * c1 + n
        yn = n - c1
        for m in range(8):
            h[m] = coef[m : m + 1] * h[m] + coef[16 + m : 17 + m] * (xn + coef[8 + m : 9 + m] * yn)
    rows = [jnp.where(low, seen[j], seen[j + 8]) for j in range(8)]
    last = jnp.where(low[0:8], kap[0:8], kap[8:16])
    for p in range(16):
        for j in range(8):
            msg[p, 16 * j : 16 * j + 16] = rows[j]
        msg[p, 128:136] = last


def gather_kernel(got, own, kap, up, dn):
    low = lane_low((8, 128))

    def pair(row):
        even = got[pl.ds(row, 8, stride=272), :]
        odd = got[pl.ds(row + 136, 8, stride=272), :]
        left = jnp.where(low, even, pltpu.roll(odd, 64, 1))
        right = jnp.where(low, pltpu.roll(even, 64, 1), odd)
        return left, right

    def place(j, z, v):
        own[j, z] = v
        if j < HALO:
            if z < TRI[j]:
                dn[OFF[j] + z] = v
            if z >= 16 - TRI[j]:
                up[OFF[j] + z - (16 - TRI[j])] = v

    for j in range(8):
        for z in range(16):
            left, right = pair(16 * j + z)
            place(j, z, left)
            place(j + 8, z, right)
    for z in range(8):
        left, right = pair(128 + z)
        for at, v in ((z, left), (z + 8, right)):
            kap[at] = v
            if at < HALO:
                dn[KOFF + at] = v
            if at >= 1:
                up[KOFF + at - 1] = v


def sweep_kernel(at, beta, own, kown, lo, hi, parts, known, start, coef, out, v, e, g, c, kw):
    t = at[0]
    p = at[1] * 4 + at[2]
    has_lo = jnp.where(t > 0, 1.0, 0.0).astype(F32)
    has_hi = jnp.where(t < 15, 1.0, 0.0).astype(F32)

    def row(j, layer):
        return pl.ds(pl.multiple_of((j * LAY + layer) * 8, 8), 8)

    zero = jnp.zeros((8, 128), F32)
    for j in range(16):
        dst = e if j == 0 else v
        if j < HALO:
            n = TRI[j]
            for i in range(n):
                dst[row(j, HALO - n + i), :] = has_lo * lo[OFF[j] + i]
                dst[row(j, 31 + i), :] = has_hi * hi[OFF[j] + i]
        for i in range(16):
            dst[row(j, 15 + i), :] = own[j, i]
    kw[0] = zero
    kw[47] = zero
    for i in range(HALO):
        kw[1 + i] = has_lo * lo[KOFF + i]
        kw[32 + i] = has_hi * hi[KOFF + i]
    for i in range(16):
        kw[16 + i] = kown[i]

    lane = lax.broadcasted_iota(jnp.int32, (8, 128), 1)
    sub = lax.broadcasted_iota(jnp.int32, (8, 128), 0)
    y, x, half = lane % 8, (lane // 8) % 8, lane // 64
    half_y, gx = sub % 2, sub // 2
    y_end, y_start = y == 7, y == 0
    x_end, x_start = x == 7, x == 0
    turn_up, turn_dn = half == 1, half == 0
    inside = (
        jnp.logical_not(x_end & (gx == 3)),
        jnp.logical_not(x_start & (gx == 0)),
        jnp.logical_not(y_end & (half == 1) & (half_y == 1)),
        jnp.logical_not(y_start & (half == 0) & (half_y == 0)),
    )

    def near(a):
        far = pltpu.roll(a, 56, 1)
        xp = jnp.where(x_end, pltpu.roll(far, 6, 0), pltpu.roll(a, 120, 1))
        far = pltpu.roll(a, 72, 1)
        xm = jnp.where(x_start, pltpu.roll(far, 2, 0), pltpu.roll(a, 8, 1))
        far = pltpu.roll(a, 71, 1)
        far = jnp.where(turn_up, pltpu.roll(far, 7, 0), far)
        yp = jnp.where(y_end, far, pltpu.roll(a, 127, 1))
        far = pltpu.roll(a, 57, 1)
        far = jnp.where(turn_dn, pltpu.roll(far, 1, 0), far)
        ym = jnp.where(y_start, far, pltpu.roll(a, 1, 1))
        return xp, xm, yp, ym

    def faces(layer, carry):
        kc = kw[layer + 1]
        place = t * 16 - HALO + layer
        scale = jnp.where((place >= 0) & (place < 256), 0.5 * STEP, 0.0).astype(F32)
        total = zero
        for i, kn in enumerate(near(kc)):
            face = scale * (kc + jnp.where(inside[i], kn, 0.0))
            total += face
            c[i, layer] = jnp.where(inside[i], face, 0.0)
        for i, kn in ((4, kw[layer + 2]), (5, kw[layer])):
            face = scale * (kc + kn)
            total += face
            c[i, layer] = face
        c[6, layer] = -total
        return carry

    lax.fori_loop(0, NEW, faces, 0)

    for j in range(1, 16):
        count = NEW - 2 * j
        block = 4 if count % 4 == 0 else 2

        def layers(i, carry, j=j, block=block):
            for k in range(block):
                layer = j + i * block + k
                mid = e[row(j - 1, layer), :]
                acc = c[6, layer] * mid
                acc += c[4, layer] * e[row(j - 1, layer + 1), :]
                acc += c[5, layer] * e[row(j - 1, layer - 1), :]
                for d, un in enumerate(near(mid)):
                    acc += c[d, layer] * un
                for i2 in range(1, j):
                    acc -= beta[j - 1 - i2] * g[row(i2 - 1, layer), :]
                g[row(j - 1, layer), :] = acc
                e[row(j, layer), :] = mid + acc + v[row(j, layer), :]
            return carry

        lax.fori_loop(0, count // block, layers, 0)

    low = lane_low((16, 128))
    sublane = p // 2
    mine = low == (p % 2 == 0)

    def block_of(ref, j):
        first = (j * LAY + HALO) * 8 + sublane
        a = ref[pl.ds(first, 8, stride=8), :]
        b = ref[pl.ds(first + 64, 8, stride=8), :]
        got = jnp.concatenate([a, b], axis=0)
        return jnp.where(mine, got, pltpu.roll(got, 64, 1))

    h = [start[16 * m : 16 * m + 16] for m in range(8)]
    for j in range(16):
        c1, c2 = doubled(parts[j], low)
        n = known[j]
        if j > 0:
            n = n + block_of(g, j - 1)
        xn = c2 - 2.0 * c1 + n
        yn = n - c1
        for m in range(8):
            h[m] = coef[m : m + 1] * h[m] + coef[16 + m : 17 + m] * (xn + coef[8 + m : 9 + m] * yn)
            out[j, 16 * m : 16 * m + 16] = h[m]
        out[j, 128:144] = block_of(e, j)


def final_kernel(got, fine, field, modes, total):
    for m in range(8):
        both = got[:, 16 * m : 16 * m + 16].reshape(256, 128).T
        modes[m] = both[0:64]
        modes[m + 8] = both[64:128]
    now = got[:, 128:144].reshape(256, 128).T[0:64]
    field[...] = now
    diff = now - fine[...]
    diff = diff * diff
    part = jnp.zeros((8, 128), F32)
    for x in range(8):
        part += diff[8 * x : 8 * x + 8, 0:128] + diff[8 * x : 8 * x + 8, 128:256]
    total[...] = part


def size_kernel(got, out):
    part = got[0]
    for p in range(1, 16):
        part += got[p]
    whole = jnp.sum(jnp.sum(part, axis=1, keepdims=True), axis=0, keepdims=True)
    out[...] = jnp.broadcast_to(jnp.sqrt(whole / 262144.0), (8, 128))


def ring(axis, step):
    n = lax.axis_size(axis)
    return [(i, (i + step) % n) for i in range(n)]


def swap(value, axis):
    return lax.all_to_all(value, axis, 0, 0, tiled=True)


def per_device(field, modes, source, regions, region_kappa, mode_rate, mode_weight):
    u = field.reshape(64, 256)
    h = modes.reshape(16, 64, 256)
    s = source.reshape(64, 256)
    reg = regions.reshape(64, 256)
    t = lax.axis_index("tm")
    at = jnp.stack([t, lax.axis_index("gx"), lax.axis_index("gy")]).astype(jnp.int32)

    f = jnp.exp(-0.5 * mode_rate)
    e = jnp.exp(-mode_rate)
    w = mode_weight
    omega = jnp.sum(w * (1.0 - f)).reshape(1)
    powers = jnp.exp(-mode_rate[None, :] * jnp.arange(16, dtype=F32)[:, None])
    beta = STEP * jnp.sum((w * (1.0 - e))[None, :] * powers, axis=1)
    coef = jnp.concatenate([e, f, 1.0 - f, w]).reshape(4, 2, 8).transpose(0, 2, 1)
    coef = jnp.broadcast_to(coef[..., None], (4, 8, 2, 64)).reshape(32, 128)

    plane = (64, 256)
    kap, g0, q1s, up, dn = call(local_kernel, [plane] * 3 + [(40, 256)] * 2, 7, 3)(
        region_kappa, w, w * f, u, reg, s, h
    )
    xlo = lax.ppermute(up, "gx", ring("gx", 1))
    xhi = lax.ppermute(dn, "gx", ring("gx", -1))

    sk, packed = call(scatter_pack_kernel, [(256, 128), (16, 144, 128)], 5, 1)(at, u, s, kap, h)
    far = [lax.ppermute(packed[4 * k : 4 * k + 4], "tm", [(0, 4 * k)]) for k in (1, 2, 3)]

    yup, ydn = call(side_kernel, [(80, 256)] * 2, 6, 1)(at, u, kap, g0, xlo, xhi)
    ylo = lax.ppermute(yup, "gy", ring("gy", 1))
    yhi = lax.ppermute(ydn, "gy", ring("gy", -1))

    quarter = jnp.where(t == 0, packed[0:4], far[0] + far[1] + far[2])
    close = [
        lax.ppermute(quarter[k], "tm", [(4 * a, 4 * a + k) for a in range(4)]) for k in (1, 2, 3)
    ]
    start = jnp.where(t % 4 == 0, quarter[0], close[0] + close[1] + close[2])

    fine, both = call(
        fine_kernel, [plane, (256, 128)], 10, 2, [(12, 24, 256)] * 4
    )(at, omega, u, kap, g0, q1s, xlo, xhi, ylo, yhi)
    parts = swap(both.reshape(16, 16, 128), "tm")

    msg, known = call(known_kernel, [(16, 136, 128), (16, 16, 128)], 5, 1)(
        at, parts, sk, start, coef
    )
    got = swap(msg, ("gx", "gy"))
    own, kown, up, dn = call(
        gather_kernel, [(16, 16, 8, 128), (16, 8, 128), (MSG, 8, 128), (MSG, 8, 128)], 1, 0
    )(got.reshape(16 * 136, 128))
    lo = lax.ppermute(up, "tm", ring("tm", 1))
    hi = lax.ppermute(dn, "tm", ring("tm", -1))
    out = call(
        sweep_kernel,
        [(16, 144, 128)],
        10,
        2,
        [(16 * LAY * 8, 128)] * 3 + [(7, LAY, 8, 128), (LAY, 8, 128)],
    )(at, beta, own, kown, lo, hi, parts, known, start, coef)[0]
    back = swap(out, "tm")
    new_field, new_modes, total = call(final_kernel, [plane, (16, 64, 256), (8, 128)], 2, 0)(
        back, fine
    )
    sums = swap(jnp.broadcast_to(total, (16, 8, 128)), ("gx", "gy"))
    size = call(size_kernel, [(8, 128)], 1, 0)(sums)[0]
    return (
        new_field.reshape(1, 8, 8, 256),
        new_modes.reshape(1, 16, 8, 8, 256),
        size[0, 0:1],
    )


def solution(mesh):
    return jax.shard_map(
        per_device,
        mesh=mesh,
        in_specs=(
            P("tm", "gx", "gy", None),
            P("tm", None, "gx", "gy", None),
            P("gx", "gy", None),
            P("gx", "gy", None),
            P(),
            P(),
            P(),
        ),
        out_specs=(P("tm", "gx", "gy", None), P("tm", None, "gx", "gy", None), P("tm")),
        check_vma=False,
    )
```

time: 480 us -> 158 us (0.33)
  the two profiles are of different devices: /device:TPU:96 before, /device:TPU:1 now
where the time goes in v1:
time: 158 us; the launch traced here: 157 us
  blocking collectives  71.3 us (45%)
  Pallas kernels  29.6 us (19%)
  starting transfers between devices  29.4 us (19%)
  waiting for transfers between devices  17.1 us (11%)
  local copies, waits for them, and re-layouts  6.74 us (4%)
  other arithmetic  2.54 us (2%)
    all_to_all x3, blocking collectives, swap(): return lax.all_to_all(value, axis, 0, 0, tiled=True)  71.3 us
    pallas_call x1, Pallas kernels, per_device(): call(sweep_kernel, [(16, 144, 128)], 10, 2, [(16 * LAY * 8, 128)] * 3 + [...  21.4 us
    all_to_all x1, starting transfers between devices, swap(): return lax.all_to_all(value, axis, 0, 0, tiled=True)  16.5 us
    ppermute x1, waiting for transfers between devices, per_device(): lo = lax.ppermute(up, 'tm', ring('tm', 1))  6.3 us
    unnamed x18, local copies, waits for them, and re-layouts  5.53 us
    ppermute x3, waiting for transfers between devices, per_device(): lax.ppermute(quarter[k], 'tm', [(4 * a, 4 * a + k) for a in range(4)])  4.32 us
  transfers between devices with their start and end apart: 13, of which 6 were waited for; matrix products, arithmetic and copies ran while one was open for 1% of the time, Pallas kernels for 2%

profile of v1, /device:TPU:1, one launch (start us, length us, event | category | flops | bytes accessed | tf_op | source)
XLA Modules:
  0.0 157.5 jit_solution(8595490151484294447)
XLA Ops:
  0.6 1.3 negate_exponential_fusion
  2.0 1.2 copy-done
  3.2 0.8 copy-done.2
  10.3 1.4 collective-permute-start.4
  11.7 2.1 %collective-permute-start = (f32[40,256]{1,0:T(8,128)S(1)}, f32[40,256]{1,0:T(8,128)S(1)}, u32[]{:S(2)}, u32[]{:S(2)}) collective-permute-start(f32[40,256]{1,0:T(8,128)S(1)} %get-tuple-element.26), channel_id=1, source_target_pairs={{0,4},{4,8},{8,12},{12,0},{1,5},{5,9},{9,13},{13,1},{2,6},{6,10},{... | collective-permute-start | bytes 122888 | tf_op jit(solution)/shard_map/ppermute | solution.py:427
  13.9 1.4 collective-permute-start.1
  15.3 1.4 collective-permute-done.xlo
  17.3 1.3 collective-permute-start.2
  18.6 1.5 collective-permute-start.3
  20.4 1.5 collective-permute-done.2.ylo
  21.9 2.4 %shard_map.96 = (f32[64,256]{1,0:T(8,128)S(1)}, f32[256,128]{1,0:T(8,128)}) custom-call(s32[3]{0:T(128)S(1)} %pad_add_fusion.at, f32[1]{0:T(128)} %bitcast.3.omega, f32[64,256]{1,0:T(8,128)S(1)} %bitcast.31, f32[64,256]{1,0:T(8,128)S(1)} %get-tuple-element.23.kap, f32[64,256]{1,0:T(8,128)S(1)} %get-tuple-element.24.g0, f32[64,256]{1,0:T(8,128)S(1)} %get-tuple-element.25.q1s, ...), custom_call_target="tpu_custom_call" | custom-call | tf_op jit(solution)/shard_map/pallas_call | solution.py:443
  24.3 16.5 %all-to-all-start = ((f32[16,16,128]{2,1,0:T(8,128)}), f32[16,16,128]{2,1,0:T(8,128)S(1)}, u32[]{:S(2)}, u32[]{:S(2)}) async-start(f32[16,16,128]{2,1,0:T(8,128)} %bitcast.8), calls=%async_computation | async-start | bytes 262144 | tf_op jit(solution)/shard_map/all_to_all | solution.py:403
  40.9 1.1 add_select_fusion
  43.3 1.3 collective-permute-start.7
  44.9 4.3 %collective-permute-done.7 = f32[144,128]{1,0:T(8,128)S(1)} collective-permute-done((f32[144,128]{1,0:T(8,128)S(1)}, f32[144,128]{1,0:T(8,128)S(1)}, u32[]{:S(2)}, u32[]{:S(2)}) %collective-permute-start.7) | collective-permute-done | bytes 73760 | tf_op jit(solution)/shard_map/ppermute | solution.py:439
  50.1 1.9 %shard_map.98 = (f32[16,136,128]{2,1,0:T(8,128)S(1)}, f32[16,16,128]{2,1,0:T(8,128)S(1)}) custom-call(s32[3]{0:T(128)S(1)} %pad_add_fusion.at, f32[16,16,128]{2,1,0:T(8,128)S(1)} %all-to-all-done.parts, f32[256,128]{1,0:T(8,128)S(1)} %get-tuple-element.31.sk, f32[144,128]{1,0:T(8,128)S(1)} %fusion.start, f32[32,128]{1,0:T(8,128)S(1)} %reshape.51.coef), custom_call_target="tpu_custom_call" | custom-call | tf_op jit(solution)/shard_map/pallas_call | solution.py:448
  52.0 24.3 %all_to_all.20 = f32[16,136,128]{2,1,0:T(8,128)S(1)} all-to-all(f32[16,136,128]{2,1,0:T(8,128)S(1)} %get-tuple-element.33), channel_id=1, replica_groups=mesh['tm'=16,'gx'=4,'gy'=4] {'gx','gy'}, dimensions={0} | all-to-all | bytes 2228224 | tf_op jit(solution)/shard_map/all_to_all | solution.py:403
  76.7 1.2 collective-permute-start.10
  78.1 6.3 %collective-permute-done.10.lo = f32[135,8,128]{2,1,0:T(8,128)S(1)} collective-permute-done((f32[135,8,128]{2,1,0:T(8,128)S(1)}, f32[135,8,128]{2,1,0:T(8,128)S(1)}, u32[]{:S(2)}, u32[]{:S(2)}) %collective-permute-start.10) | collective-permute-done | bytes 552992 | tf_op jit(solution)/shard_map/ppermute | solution.py:455
  84.4 2.8 %collective-permute-done.11.hi = f32[135,8,128]{2,1,0:T(8,128)S(1)} collective-permute-done((f32[135,8,128]{2,1,0:T(8,128)S(1)}, f32[135,8,128]{2,1,0:T(8,128)S(1)}, u32[]{:S(2)}, u32[]{:S(2)}) %collective-permute-start.11) | collective-permute-done | bytes 552992 | tf_op jit(solution)/shard_map/ppermute | solution.py:456
  87.1 21.4 %shard_map.100 = f32[16,144,128]{2,1,0:T(8,128)S(1)} custom-call(s32[3]{0:T(128)S(1)} %pad_add_fusion.at, f32[16]{0:T(128)S(1)} %broadcast_multiply_fusion.beta, f32[16,16,8,128]{3,2,1,0:T(8,128)S(1)} %get-tuple-element.34.own, f32[16,8,128]{2,1,0:T(8,128)S(1)} %get-tuple-element.35.kown, f32[135,8,128]{2,1,0:T(8,128)S(1)} %collective-permute-done.10.lo, ...), custom_call_target="tpu_custom_call" | custom-call | tf_op jit(solution)/shard_map/pallas_call | solution.py:457
  108.5 37.4 %all_to_all.21.got = f32[16,144,128]{2,1,0:T(8,128)S(1)} all-to-all(f32[16,144,128]{2,1,0:T(8,128)S(1)} %shard_map.100), channel_id=1, replica_groups=mesh['tm'=16,'gx'=4,'gy'=4] {'tm'}, dimensions={0} | all-to-all | bytes 2359296 | tf_op jit(solution)/shard_map/all_to_all | solution.py:403
  145.9 1.3 shard_map.101
  147.3 9.6 %all_to_all.22.got = f32[16,8,128]{2,1,0:T(8,128)S(1)} all-to-all(f32[16,8,128]{2,1,0:T(8,128)S(1)} %broadcast_in_dim.5), channel_id=1, replica_groups=mesh['tm'=16,'gx'=4,'gy'=4] {'gx','gy'}, dimensions={0} | all-to-all | bytes 131072 | tf_op jit(solution)/shard_map/all_to_all | solution.py:403
  (50 shorter events, 11.0 us)
Async XLA Ops:
  2.0 1.2 copy-start
  3.2 0.8 copy-start.2
  4.0 0.8 copy-start.4
  4.9 0.8 copy-start.5
  5.7 0.7 copy-start.6
  6.4 0.7 copy-start.8
  7.0 1.2 copy-start.1
  7.0 1.2 copy-start.3
  8.9 11.2 %copy-start.7 = (f32[16]{0:T(128)S(1)}, f32[16]{0:T(128)}, u32[]{:S(2)}) copy-start(f32[16]{0:T(128)} %w.1) | copy-start | bytes 196
  9.0 31.9 %collective-permute-start.5 = (f32[4,144,128]{2,1,0:T(8,128)S(1)}, f32[4,144,128]{2,1,0:T(8,128)S(1)}, u32[]{:S(2)}, u32[]{:S(2)}) collective-permute-start(f32[4,144,128]{2,1,0:T(8,128)S(1)} %get-tuple-element.43), channel_id=1, source_target_pairs={{0,128},{1,129},{2,130},{3,131},{4,132},{5,133},{6,134},{7,135},{8... | collective-permute-start | bytes 884744 | tf_op jit(solution)/shard_map/ppermute | solution.py:431
  9.7 31.2 %collective-permute-start.6 = (f32[4,144,128]{2,1,0:T(8,128)S(1)}, f32[4,144,128]{2,1,0:T(8,128)S(1)}, u32[]{:S(2)}, u32[]{:S(2)}) collective-permute-start(f32[4,144,128]{2,1,0:T(8,128)S(1)} %get-tuple-element.44), channel_id=1, source_target_pairs={{0,192},{1,193},{2,194},{3,195},{4,196},{5,197},{6,198},{7,199},{8... | collective-permute-start | bytes 884744 | tf_op jit(solution)/shard_map/ppermute | solution.py:431
  10.3 30.5 %collective-permute-start.4 = (f32[4,144,128]{2,1,0:T(8,128)S(1)}, f32[4,144,128]{2,1,0:T(8,128)}, u32[]{:S(2)}, u32[]{:S(2)}) collective-permute-start(f32[4,144,128]{2,1,0:T(8,128)S(1)} %get-tuple-element.45), channel_id=1, source_target_pairs={{0,64},{1,65},{2,66},{3,67},{4,68},{5,69},{6,70},{7,71},{8,72},{9,... | collective-permute-start | bytes 884744 | tf_op jit(solution)/shard_map/ppermute | solution.py:431
  11.7 5.0 %collective-permute-start = (f32[40,256]{1,0:T(8,128)S(1)}, f32[40,256]{1,0:T(8,128)S(1)}, u32[]{:S(2)}, u32[]{:S(2)}) collective-permute-start(f32[40,256]{1,0:T(8,128)S(1)} %get-tuple-element.26), channel_id=1, source_target_pairs={{0,4},{4,8},{8,12},{12,0},{1,5},{5,9},{9,13},{13,1},{2,6},{6,10},{... | collective-permute-start | bytes 122888 | tf_op jit(solution)/shard_map/ppermute | solution.py:427
  13.9 2.9 %collective-permute-start.1 = (f32[40,256]{1,0:T(8,128)S(1)}, f32[40,256]{1,0:T(8,128)S(1)}, u32[]{:S(2)}, u32[]{:S(2)}) collective-permute-start(f32[40,256]{1,0:T(8,128)S(1)} %get-tuple-element.27), channel_id=1, source_target_pairs={{0,12},{4,0},{8,4},{12,8},{1,13},{5,1},{9,5},{13,9},{2,14},{6,2},{... | collective-permute-start | bytes 122888 | tf_op jit(solution)/shard_map/ppermute | solution.py:428
  17.3 4.6 %collective-permute-start.2 = (f32[80,256]{1,0:T(8,128)S(1)}, f32[80,256]{1,0:T(8,128)S(1)}, u32[]{:S(2)}, u32[]{:S(2)}) collective-permute-start(f32[80,256]{1,0:T(8,128)S(1)} %get-tuple-element.28), channel_id=1, source_target_pairs={{0,1},{1,2},{2,3},{3,0},{4,5},{5,6},{6,7},{7,4},{8,9},{9,10},{10,1... | collective-permute-start | bytes 245768 | tf_op jit(solution)/shard_map/ppermute | solution.py:434
  18.6 3.3 %collective-permute-start.3 = (f32[80,256]{1,0:T(8,128)S(1)}, f32[80,256]{1,0:T(8,128)S(1)}, u32[]{:S(2)}, u32[]{:S(2)}) collective-permute-start(f32[80,256]{1,0:T(8,128)S(1)} %get-tuple-element.29), channel_id=1, source_target_pairs={{0,3},{1,0},{2,1},{3,2},{4,7},{5,4},{6,5},{7,6},{8,11},{9,8},{10,9... | collective-permute-start | bytes 245768 | tf_op jit(solution)/shard_map/ppermute | solution.py:435
  24.3 25.7 %all-to-all-start = ((f32[16,16,128]{2,1,0:T(8,128)}), f32[16,16,128]{2,1,0:T(8,128)S(1)}, u32[]{:S(2)}, u32[]{:S(2)}) async-start(f32[16,16,128]{2,1,0:T(8,128)} %bitcast.8), calls=%async_computation | async-start | bytes 262144 | tf_op jit(solution)/shard_map/all_to_all | solution.py:403
  41.9 3.0 %collective-permute-start.8 = (f32[144,128]{1,0:T(8,128)S(1)}, f32[144,128]{1,0:T(8,128)S(1)}, u32[]{:S(2)}, u32[]{:S(2)}) collective-permute-start(f32[144,128]{1,0:T(8,128)S(1)} %get-tuple-element.46), channel_id=1, source_target_pairs={{0,32},{64,96},{128,160},{192,224},{1,33},{65,97},{129,161},{193,2... | collective-permute-start | bytes 221192 | tf_op jit(solution)/shard_map/ppermute | solution.py:439
  42.6 2.3 %collective-permute-start.9 = (f32[144,128]{1,0:T(8,128)S(1)}, f32[144,128]{1,0:T(8,128)S(1)}, u32[]{:S(2)}, u32[]{:S(2)}) collective-permute-start(f32[144,128]{1,0:T(8,128)S(1)} %get-tuple-element.47), channel_id=1, source_target_pairs={{0,48},{64,112},{128,176},{192,240},{1,49},{65,113},{129,177},{193... | collective-permute-start | bytes 221192 | tf_op jit(solution)/shard_map/ppermute | solution.py:439
  43.3 5.9 %collective-permute-start.7 = (f32[144,128]{1,0:T(8,128)S(1)}, f32[144,128]{1,0:T(8,128)S(1)}, u32[]{:S(2)}, u32[]{:S(2)}) collective-permute-start(f32[144,128]{1,0:T(8,128)S(1)} %get-tuple-element.48), channel_id=1, source_target_pairs={{0,16},{64,80},{128,144},{192,208},{1,17},{65,81},{129,145},{193,2... | collective-permute-start | bytes 221192 | tf_op jit(solution)/shard_map/ppermute | solution.py:439
  76.7 7.6 %collective-permute-start.10 = (f32[135,8,128]{2,1,0:T(8,128)S(1)}, f32[135,8,128]{2,1,0:T(8,128)S(1)}, u32[]{:S(2)}, u32[]{:S(2)}) collective-permute-start(f32[135,8,128]{2,1,0:T(8,128)S(1)} %get-tuple-element.36), channel_id=1, source_target_pairs={{0,16},{16,32},{32,48},{48,64},{64,80},{80,96},{96,112},{112,128},... | collective-permute-start | bytes 1658888 | tf_op jit(solution)/shard_map/ppermute | solution.py:455
  77.9 9.2 %collective-permute-start.11 = (f32[135,8,128]{2,1,0:T(8,128)S(1)}, f32[135,8,128]{2,1,0:T(8,128)S(1)}, u32[]{:S(2)}, u32[]{:S(2)}) collective-permute-start(f32[135,8,128]{2,1,0:T(8,128)S(1)} %get-tuple-element.37), channel_id=1, source_target_pairs={{0,240},{16,0},{32,16},{48,32},{64,48},{80,64},{96,80},{112,96},{1... | collective-permute-start | bytes 1658888 | tf_op jit(solution)/shard_map/ppermute | solution.py:456

commit v2 on v1

--- a/solution.py
+++ b/solution.py
@@ -18,6 +18,8 @@
 MSG = KOFF + HALO
 LAY = 48
 NEW = 46
+SIZES = [0, 11, 7, 10, 10, 12, 9, 8, 10, 7, 9, 12, 11, 10, 9, 8]
+BLOCKS = [(size, -(-(NEW - 2 * j) // size) if size else 0) for j, size in enumerate(SIZES)]
 
 
 def call(kernel, outs, ins, smem, scratch=()):
@@ -35,7 +37,18 @@
     return lax.broadcasted_iota(jnp.int32, shape, len(shape) - 1) < 64
 
 
-def local_kernel(rk, w, wf, u, reg, s, modes, kap, g0, q1s, up, dn):
+def local_kernel(at, rk_in, w_in, rate_in, u_in, reg_in, s_in, modes_in, u, kap, g0, q1s, up, dn, sk, packed,
+                 rk, w, rate, reg, s, modes, sems):
+    pairs = (
+        (rk_in, rk), (w_in, w), (rate_in, rate), (modes_in, modes),
+        (s_in, s), (reg_in, reg), (u_in, u),
+    )
+    copies = [pltpu.make_async_copy(a, b, sems.at[i]) for i, (a, b) in enumerate(pairs)]
+    for copy in copies:
+        copy.start()
+    for copy in copies:
+        copy.wait()
+    half = [jnp.exp(jnp.full((8, 256), -0.5 * rate[m], F32)) for m in range(16)]
     for x in range(8):
         rows = slice(8 * x, 8 * x + 8)
         region = reg[rows]
@@ -46,9 +59,9 @@
         a = jnp.zeros((8, 256), F32)
         b = jnp.zeros((8, 256), F32)
         for m in range(16):
-            h = modes[m, rows]
-            a += w[m] * h
-            b += wf[m] * h
+            h = w[m] * modes[m, rows]
+            a += h
+            b += half[m] * h
         g0[rows] = s[rows] - a
         q1s[rows] = s[rows] - b
     up[0:16] = u[48:64]
@@ -57,9 +70,6 @@
     dn[0:16] = u[0:16]
     dn[16:32] = kap[0:16]
     dn[32:40] = g0[0:8]
-
-
-def scatter_pack_kernel(at, u, s, kap, modes, sk, packed):
     sk[...] = jnp.concatenate([s[...], kap[...]], axis=0).T
 
     @pl.when(at[0] == 0)
@@ -67,8 +77,6 @@
         for m in range(8):
             both = jnp.concatenate([modes[m], modes[m + 8]], axis=0).T
             packed[:, 16 * m : 16 * m + 16] = both.reshape(16, 16, 128)
-        both = jnp.concatenate([u[...], u[...]], axis=0).T
-        packed[:, 128:144] = both.reshape(16, 16, 128)
 
 
 def side_kernel(at, u, kap, g0, xlo, xhi, yup, ydn):
@@ -89,7 +97,7 @@
                 out[at_row : at_row + 1] = src[8 * x + y : 8 * x + y + 1]
 
 
-def fine_kernel(at, omega, u, kap, g0, q1s, xlo, xhi, ylo, yhi, fine, both, up, kp, gp, u1):
+def fine_kernel(at, omega, u, kap, g0, q1s, xlo, xhi, ylo, yhi, both, up, kp, gp, u1):
     gx, gy = at[1], at[2]
     zero = jnp.zeros((24, 256), F32)
     for ref in (up, kp, gp):
@@ -178,10 +186,11 @@
         c1 = gp[2 + x, 8:16]
         lap = laplace(u1, 2 + x)[8:16]
         c2 = (0.5 * STEP) * (lap + q1s[rows] - omega[0] * c1)
-        fine[rows] = u1[2 + x, 8:16] + c2
         first.append(c1)
         second.append(c2)
-    both[...] = jnp.concatenate(first + second, axis=0).T
+    both[:, 0:16] = jnp.concatenate(first + second, axis=0).T.reshape(16, 16, 128)
+    now = jnp.concatenate([u[...], u[...]], axis=0).T.reshape(16, 16, 128)
+    both[:, 16:24] = jnp.where(lane_low((16, 8, 128)), now[:, 0:8], now[:, 8:16])
 
 
 def doubled(v, low):
@@ -189,18 +198,28 @@
     return jnp.where(low, v, turned), jnp.where(low, turned, v)
 
 
-def known_kernel(at, parts, sk, start, coef, msg, known):
+def unpacked(v):
+    low = lane_low((8, 128))
+    first, second = doubled(v, low)
+    return jnp.concatenate([first, second], axis=0)
+
+
+def packed_rows(v):
+    return jnp.where(lane_low((8, 128)), v[0:8], v[8:16])
+
+
+def known_kernel(at, parts, sk, start, coef, msg, fmsg, known):
     low = lane_low((16, 128))
     slab = sk[pl.ds(pl.multiple_of(at[0] * 16, 16), 16), :]
     source, kap = doubled(slab, low)
     h = [start[16 * m : 16 * m + 16] for m in range(8)]
-    field = start[128:144]
-    seen = []
+    seen, fine = [], []
     for j in range(16):
-        c1, c2 = doubled(parts[j], low)
+        c1, c2 = doubled(parts[j, 0:16], low)
+        fine.append(unpacked(parts[j, 16:24]) + c1 + c2)
         if j == 0:
             n = 2.0 * c1
-            seen.append(field + c1 + c2)
+            seen.append(fine[0])
         else:
             q = coef[24:25] * h[0]
             for m in range(1, 8):
@@ -212,11 +231,15 @@
         yn = n - c1
         for m in range(8):
             h[m] = coef[m : m + 1] * h[m] + coef[16 + m : 17 + m] * (xn + coef[8 + m : 9 + m] * yn)
-    rows = [jnp.where(low, seen[j], seen[j + 8]) for j in range(8)]
-    last = jnp.where(low[0:8], kap[0:8], kap[8:16])
+    last = packed_rows(kap)
+    for j in range(8):
+        rows = slice(16 * j, 16 * j + 16)
+        v = jnp.where(low, seen[j], seen[j + 8])
+        w = jnp.where(low, fine[j], fine[j + 8])
+        for p in range(16):
+            msg[p, rows] = v
+            fmsg[p, rows] = w
     for p in range(16):
-        for j in range(8):
-            msg[p, 16 * j : 16 * j + 16] = rows[j]
         msg[p, 128:136] = last
 
 
@@ -253,9 +276,8 @@
                 up[KOFF + at - 1] = v
 
 
-def sweep_kernel(at, beta, own, kown, lo, hi, parts, known, start, coef, out, v, e, g, c, kw):
+def sweep_kernel(at, beta, own, kown, lo, hi, e_out, g_out, v, e, g, c, kw):
     t = at[0]
-    p = at[1] * 4 + at[2]
     has_lo = jnp.where(t > 0, 1.0, 0.0).astype(F32)
     has_hi = jnp.where(t < 15, 1.0, 0.0).astype(F32)
 
@@ -307,7 +329,7 @@
         ym = jnp.where(y_start, far, pltpu.roll(a, 1, 1))
         return xp, xm, yp, ym
 
-    def faces(layer, carry):
+    def faces(layer):
         kc = kw[layer + 1]
         place = t * 16 - HALO + layer
         scale = jnp.where((place >= 0) & (place < 256), 0.5 * STEP, 0.0).astype(F32)
@@ -321,13 +343,12 @@
             total += face
             c[i, layer] = face
         c[6, layer] = -total
-        return carry
-
-    lax.fori_loop(0, NEW, faces, 0)
+
+    for layer in range(NEW):
+        faces(layer)
 
     for j in range(1, 16):
-        count = NEW - 2 * j
-        block = 4 if count % 4 == 0 else 2
+        block, blocks = BLOCKS[j]
 
         def layers(i, carry, j=j, block=block):
             for k in range(block):
@@ -344,54 +365,97 @@
                 e[row(j, layer), :] = mid + acc + v[row(j, layer), :]
             return carry
 
-        lax.fori_loop(0, count // block, layers, 0)
-
+        lax.fori_loop(0, blocks, layers, 0)
+
+    for j in range(16):
+        for i in range(16):
+            e_out[j, i] = e[row(j, HALO + i), :]
+            if j > 0:
+                g_out[j, i] = g[row(j - 1, HALO + i), :]
+            else:
+                g_out[j, i] = zero
+
+
+def pack_kernel(at, got, e, g, parts, known, start, coef, out):
+    p = at[1] * 4 + at[2]
     low = lane_low((16, 128))
     sublane = p // 2
     mine = low == (p % 2 == 0)
 
     def block_of(ref, j):
-        first = (j * LAY + HALO) * 8 + sublane
+        first = j * 128 + sublane
         a = ref[pl.ds(first, 8, stride=8), :]
         b = ref[pl.ds(first + 64, 8, stride=8), :]
-        got = jnp.concatenate([a, b], axis=0)
-        return jnp.where(mine, got, pltpu.roll(got, 64, 1))
+        both = jnp.concatenate([a, b], axis=0)
+        return jnp.where(mine, both, pltpu.roll(both, 64, 1))
 
     h = [start[16 * m : 16 * m + 16] for m in range(8)]
     for j in range(16):
-        c1, c2 = doubled(parts[j], low)
-        n = known[j]
-        if j > 0:
-            n = n + block_of(g, j - 1)
+        c1, c2 = doubled(parts[j, 0:16], low)
+        n = known[j] + block_of(g, j)
         xn = c2 - 2.0 * c1 + n
         yn = n - c1
         for m in range(8):
             h[m] = coef[m : m + 1] * h[m] + coef[16 + m : 17 + m] * (xn + coef[8 + m : 9 + m] * yn)
-            out[j, 16 * m : 16 * m + 16] = h[m]
-        out[j, 128:144] = block_of(e, j)
-
-
-def final_kernel(got, fine, field, modes, total):
-    for m in range(8):
-        both = got[:, 16 * m : 16 * m + 16].reshape(256, 128).T
-        modes[m] = both[0:64]
-        modes[m + 8] = both[64:128]
-    now = got[:, 128:144].reshape(256, 128).T[0:64]
-    field[...] = now
-    diff = now - fine[...]
-    diff = diff * diff
-    part = jnp.zeros((8, 128), F32)
-    for x in range(8):
-        part += diff[8 * x : 8 * x + 8, 0:128] + diff[8 * x : 8 * x + 8, 128:256]
-    total[...] = part
-
-
-def size_kernel(got, out):
-    part = got[0]
-    for p in range(1, 16):
-        part += got[p]
+            if j % 2 == 0:
+                at_row = 16 * (m % 4)
+                out[j + m // 4, at_row : at_row + 16] = h[m]
+        if j % 2 == 1:
+            out[j - 1, 64:72] = packed_rows(xn)
+            out[j, 64:72] = packed_rows(yn)
+        out[j, 72:80] = packed_rows(block_of(e, j))
+
+    half = lane_low((8, 128))
+    for j in range(8):
+        one = jnp.zeros((8, 128), F32)
+        two = jnp.zeros((8, 128), F32)
+        for z in range(16):
+            even = got[pl.ds(16 * j + z, 8, stride=256), :]
+            odd = got[pl.ds(16 * j + z + 128, 8, stride=256), :]
+            left = jnp.where(half, even, pltpu.roll(odd, 64, 1))
+            right = jnp.where(half, pltpu.roll(even, 64, 1), odd)
+            at_row = (j * 16 + z) * 8
+            diff = e[at_row : at_row + 8] - left
+            one += diff * diff
+            at_row = ((j + 8) * 16 + z) * 8
+            diff = e[at_row : at_row + 8] - right
+            two += diff * diff
+        out[j, 80:88] = one
+        out[j + 8, 80:88] = two
+
+
+def final_kernel(at, got, other, coef, modes, field, size):
+    def finish(low, high, odd):
+        x = y = None
+        if odd:
+            x = jnp.concatenate([unpacked(low[t, 64:72]) for t in range(16)], axis=0)
+            y = jnp.concatenate([unpacked(high[t, 64:72]) for t in range(16)], axis=0)
+        for m in range(8):
+            src = low if m < 4 else high
+            first = 16 * (m % 4)
+            both = src[:, first : first + 16].reshape(256, 128)
+            if odd:
+                both = coef[m : m + 1] * both
+                both += coef[16 + m : 17 + m] * (x + coef[8 + m : 9 + m] * y)
+            both = both.T
+            modes[m] = both[0:64]
+            modes[m + 8] = both[64:128]
+
+    @pl.when(at[0] % 2 == 0)
+    def _():
+        finish(got, other, False)
+
+    @pl.when(at[0] % 2 == 1)
+    def _():
+        finish(other, got, True)
+
+    now = jnp.concatenate([unpacked(got[t, 72:80]) for t in range(16)], axis=0)
+    field[...] = now.T[0:64]
+    part = got[0, 80:88]
+    for t in range(1, 16):
+        part += got[t, 80:88]
     whole = jnp.sum(jnp.sum(part, axis=1, keepdims=True), axis=0, keepdims=True)
-    out[...] = jnp.broadcast_to(jnp.sqrt(whole / 262144.0), (8, 128))
+    size[...] = jnp.broadcast_to(jnp.sqrt(whole / 262144.0), (8, 128))
 
 
 def ring(axis, step):
@@ -421,13 +485,19 @@
     coef = jnp.broadcast_to(coef[..., None], (4, 8, 2, 64)).reshape(32, 128)
 
     plane = (64, 256)
-    kap, g0, q1s, up, dn = call(local_kernel, [plane] * 3 + [(40, 256)] * 2, 7, 3)(
-        region_kappa, w, w * f, u, reg, s, h
-    )
+    outs = [plane] * 4 + [(40, 256)] * 2 + [(256, 128), (16, 128, 128)]
+    u, kap, g0, q1s, up, dn, sk, packed = pl.pallas_call(
+        local_kernel,
+        out_shape=[jax.ShapeDtypeStruct(shape, F32) for shape in outs],
+        in_specs=[SM] + [pl.BlockSpec(memory_space=pl.ANY)] * 7,
+        out_specs=[VM] * 8,
+        scratch_shapes=[pltpu.SMEM((8,), F32), pltpu.SMEM((16,), F32), pltpu.SMEM((16,), F32)]
+        + [pltpu.VMEM(plane, jnp.int32), pltpu.VMEM(plane, F32), pltpu.VMEM((16, 64, 256), F32)]
+        + [pltpu.SemaphoreType.DMA((7,))],
+        compiler_params=pltpu.CompilerParams(vmem_limit_bytes=60 * 1024 * 1024),
+    )(at, region_kappa, w, mode_rate, u, reg, s, h)
     xlo = lax.ppermute(up, "gx", ring("gx", 1))
     xhi = lax.ppermute(dn, "gx", ring("gx", -1))
-
-    sk, packed = call(scatter_pack_kernel, [(256, 128), (16, 144, 128)], 5, 1)(at, u, s, kap, h)
     far = [lax.ppermute(packed[4 * k : 4 * k + 4], "tm", [(0, 4 * k)]) for k in (1, 2, 3)]
 
     yup, ydn = call(side_kernel, [(80, 256)] * 2, 6, 1)(at, u, kap, g0, xlo, xhi)
@@ -440,33 +510,38 @@
     ]
     start = jnp.where(t % 4 == 0, quarter[0], close[0] + close[1] + close[2])
 
-    fine, both = call(
-        fine_kernel, [plane, (256, 128)], 10, 2, [(12, 24, 256)] * 4
-    )(at, omega, u, kap, g0, q1s, xlo, xhi, ylo, yhi)
-    parts = swap(both.reshape(16, 16, 128), "tm")
-
-    msg, known = call(known_kernel, [(16, 136, 128), (16, 16, 128)], 5, 1)(
-        at, parts, sk, start, coef
-    )
+    both = call(
+        fine_kernel, [(16, 24, 128)], 10, 2, [(12, 24, 256)] * 4
+    )(at, omega, u, kap, g0, q1s, xlo, xhi, ylo, yhi)[0]
+    parts = swap(both, "tm")
+
+    msg, fmsg, known = call(
+        known_kernel, [(16, 136, 128), (16, 128, 128), (16, 16, 128)], 5, 1
+    )(at, parts, sk, start, coef)
     got = swap(msg, ("gx", "gy"))
+    got, fmsg = lax.optimization_barrier((got, fmsg))
     own, kown, up, dn = call(
         gather_kernel, [(16, 16, 8, 128), (16, 8, 128), (MSG, 8, 128), (MSG, 8, 128)], 1, 0
     )(got.reshape(16 * 136, 128))
     lo = lax.ppermute(up, "tm", ring("tm", 1))
     hi = lax.ppermute(dn, "tm", ring("tm", -1))
-    out = call(
+    fine = swap(fmsg, ("gx", "gy"))
+    now, grown = call(
         sweep_kernel,
-        [(16, 144, 128)],
-        10,
+        [(16, 16, 8, 128)] * 2,
+        6,
         2,
         [(16 * LAY * 8, 128)] * 3 + [(7, LAY, 8, 128), (LAY, 8, 128)],
-    )(at, beta, own, kown, lo, hi, parts, known, start, coef)[0]
+    )(at, beta, own, kown, lo, hi)
+    flat = (2048, 128)
+    out = call(pack_kernel, [(16, 88, 128)], 8, 1)(
+        at, fine.reshape(flat), now.reshape(flat), grown.reshape(flat), parts, known, start, coef
+    )[0]
     back = swap(out, "tm")
-    new_field, new_modes, total = call(final_kernel, [plane, (16, 64, 256), (8, 128)], 2, 0)(
-        back, fine
-    )
-    sums = swap(jnp.broadcast_to(total, (16, 8, 128)), ("gx", "gy"))
-    size = call(size_kernel, [(8, 128)], 1, 0)(sums)[0]
+    other = lax.ppermute(back, "tm", [(i, i ^ 1) for i in range(16)])
+    new_modes, new_field, size = call(
+        final_kernel, [(16, 64, 256), plane, (8, 128)], 4, 1
+    )(at, back, other, coef)
     return (
         new_field.reshape(1, 8, 8, 256),
         new_modes.reshape(1, 16, 8, 8, 256),

time: 158 us -> 129 us (0.82)
  blocking collectives: 71.3 us -> 50.4 us
  Pallas kernels: 29.6 us -> 22.4 us
  local copies, waits for them, and re-layouts: 6.74 us -> 3.23 us
  starting transfers between devices: 29.4 us -> 31.1 us
    all_to_all x3 -> x2, blocking collectives: 71.3 us -> 50.4 us  [swap(): return lax.all_to_all(value, axis, 0, 0, tiled=True)]
    pallas_call x7 -> x6, Pallas kernels: 28.5 us -> 21.4 us  [the longest x1 8.92 us: per_device(): call(sweep_kernel, [(16, 16, 8, 128)] * 2, 6, 2, [(16 * LAY * 8, 128)] *...]
    unnamed x18 -> x20, local copies, waits for them, and re-layouts: 5.53 us -> 0.94 us
    all_to_all x1 -> x2, starting transfers between devices: 16.5 us -> 19.2 us  [swap(): return lax.all_to_all(value, axis, 0, 0, tiled=True)]
    ppermute x0 -> x1, waiting for transfers between devices: none -> 2.19 us  [per_device(): other = lax.ppermute(back, 'tm', [(i, i ^ 1) for i in range(16)])]
  transfers between devices with their start and end apart: 13 -> 15, of which waited for: 6 -> 6; matrix products, arithmetic and copies ran while one was open for 1% -> 3% of each run, Pallas kernels for 2% -> 10%
where the time goes in v2:
time: 129 us
  blocking collectives  50.4 us (39%)
  starting transfers between devices  31.1 us (24%)
  Pallas kernels  22.4 us (17%)
  waiting for transfers between devices  18.3 us (14%)
  local copies, waits for them, and re-layouts  3.23 us (3%)
  other arithmetic  2.45 us (2%)
    all_to_all x2, blocking collectives, swap(): return lax.all_to_all(value, axis, 0, 0, tiled=True)  50.4 us
    all_to_all x2, starting transfers between devices, swap(): return lax.all_to_all(value, axis, 0, 0, tiled=True)  19.2 us
    pallas_call x1, Pallas kernels, per_device(): call(sweep_kernel, [(16, 16, 8, 128)] * 2, 6, 2, [(16 * LAY * 8, 128)] *...  8.92 us
    ppermute x1, waiting for transfers between devices, per_device(): lo = lax.ppermute(up, 'tm', ring('tm', 1))  6.1 us
    ppermute x3, waiting for transfers between devices, per_device(): lax.ppermute(quarter[k], 'tm', [(4 * a, 4 * a + k) for a in range(4)])  4.32 us
    pallas_call x1, Pallas kernels, per_device(): pl.pallas_call(local_kernel, out_shape=[jax.ShapeDtypeStruct(shape, F32)...  3.41 us
    pallas_call x1, Pallas kernels, per_device(): call(known_kernel, [(16, 136, 128), (16, 128, 128), (16, 16, 128)], 5, 1)  2.97 us
    ppermute x1, waiting for transfers between devices, per_device(): hi = lax.ppermute(dn, 'tm', ring('tm', -1))  2.77 us
  transfers between devices with their start and end apart: 15, of which 6 were waited for; matrix products, arithmetic and copies ran while one was open for 3% of the time, Pallas kernels for 10%

profile of v2, /device:TPU:1, one launch (start us, length us, event | category | flops | bytes accessed | tf_op | source)
XLA Modules:
  0.0 128.7 jit_solution(10603502435354424208)
XLA Ops:
  1.3 3.4 %shard_map.94 = (f32[64,256]{1,0:T(8,128)}, f32[64,256]{1,0:T(8,128)}, f32[64,256]{1,0:T(8,128)}, f32[64,256]{1,0:T(8,128)}, f32[40,256]{1,0:T(8,128)}, /*index=...) custom-call(s32[3]{0:T(128)} %pad_add_fusion.at, f32[8]{0:T(128)} %rk_in.1, f32[16]{0:T(128)} %w_in.1, ...), custom_call_target="tpu_custom_call" | custom-call | tf_op jit(solution)/shard_map/pallas_call | solution.py:489
  4.8 2.2 %collective-permute-start = (f32[40,256]{1,0:T(8,128)}, f32[40,256]{1,0:T(8,128)S(1)}, u32[]{:S(2)}, u32[]{:S(2)}) collective-permute-start(f32[40,256]{1,0:T(8,128)} %get-tuple-element.31), channel_id=1, source_target_pairs={{0,4},{4,8},{8,12},{12,0},{1,5},{5,9},{9,13},{13,1},{2,6},{6,10},{... | collective-permute-start | bytes 122888 | tf_op jit(solution)/shard_map/ppermute | solution.py:499
  7.0 1.5 %collective-permute-start.1 = (f32[40,256]{1,0:T(8,128)}, f32[40,256]{1,0:T(8,128)S(1)}, u32[]{:S(2)}, u32[]{:S(2)}) collective-permute-start(f32[40,256]{1,0:T(8,128)} %get-tuple-element.32), channel_id=1, source_target_pairs={{0,12},{4,0},{8,4},{12,8},{1,13},{5,1},{9,5},{13,9},{2,14},{6,2},{... | collective-permute-start | bytes 122888 | tf_op jit(solution)/shard_map/ppermute | solution.py:500
  8.5 1.2 fusion.1
  12.4 1.3 %collective-permute-start.2 = (f32[80,256]{1,0:T(8,128)S(1)}, f32[80,256]{1,0:T(8,128)S(1)}, u32[]{:S(2)}, u32[]{:S(2)}) collective-permute-start(f32[80,256]{1,0:T(8,128)S(1)} %get-tuple-element.33), channel_id=1, source_target_pairs={{0,1},{1,2},{2,3},{3,0},{4,5},{5,6},{6,7},{7,4},{8,9},{9,10},{10,1... | collective-permute-start | bytes 245768 | tf_op jit(solution)/shard_map/ppermute | solution.py:504
  13.7 1.5 %collective-permute-start.3 = (f32[80,256]{1,0:T(8,128)S(1)}, f32[80,256]{1,0:T(8,128)S(1)}, u32[]{:S(2)}, u32[]{:S(2)}) collective-permute-start(f32[80,256]{1,0:T(8,128)S(1)} %get-tuple-element.34), channel_id=1, source_target_pairs={{0,3},{1,0},{2,1},{3,2},{4,7},{5,4},{6,5},{7,6},{8,11},{9,8},{10,9... | collective-permute-start | bytes 245768 | tf_op jit(solution)/shard_map/ppermute | solution.py:505
  16.1 0.9 collective-permute-done.2.ylo
  17.0 2.6 %shard_map.96 = f32[16,24,128]{2,1,0:T(8,128)} custom-call(s32[3]{0:T(128)S(1)} %copy-done.7, f32[1]{0:T(128)} %bitcast.3.omega, f32[64,256]{1,0:T(8,128)S(1)} %copy-done, f32[64,256]{1,0:T(8,128)S(1)} %copy-done.1, f32[64,256]{1,0:T(8,128)S(1)} %copy-done.2, f32[64,256]{1,0:T(8,128)S(1)} %copy-done.6, f32[40,256]{1,0:T(8,128)S(1)} %collective-permute-done.xlo, ...), custom_call_target="tpu_custom_call" | custom-call | tf_op jit(solution)/shard_map/pallas_call | solution.py:513
  19.6 15.5 %all-to-all-start = ((f32[16,24,128]{2,1,0:T(8,128)}), f32[16,24,128]{2,1,0:T(8,128)S(1)}, u32[]{:S(2)}, u32[]{:S(2)}) async-start(f32[16,24,128]{2,1,0:T(8,128)} %shard_map.96), calls=%async_computation | async-start | bytes 393216 | tf_op jit(solution)/shard_map/all_to_all | solution.py:467
  35.1 1.0 add_select_fusion
  37.5 1.3 %collective-permute-start.7 = (f32[128,128]{1,0:T(8,128)S(1)}, f32[128,128]{1,0:T(8,128)S(1)}, u32[]{:S(2)}, u32[]{:S(2)}) collective-permute-start(f32[128,128]{1,0:T(8,128)S(1)} %get-tuple-element.56), channel_id=1, source_target_pairs={{0,16},{64,80},{128,144},{192,208},{1,17},{65,81},{129,145},{193,2... | collective-permute-start | bytes 196616 | tf_op jit(solution)/shard_map/ppermute | solution.py:509
  39.1 4.3 %collective-permute-done.7 = f32[128,128]{1,0:T(8,128)S(1)} collective-permute-done((f32[128,128]{1,0:T(8,128)S(1)}, f32[128,128]{1,0:T(8,128)S(1)}, u32[]{:S(2)}, u32[]{:S(2)}) %collective-permute-start.7) | collective-permute-done | bytes 65568 | tf_op jit(solution)/shard_map/ppermute | solution.py:509
  43.5 2.0 %all-to-all-done.parts = f32[16,24,128]{2,1,0:T(8,128)S(1)} async-done(((f32[16,24,128]{2,1,0:T(8,128)}), f32[16,24,128]{2,1,0:T(8,128)S(1)}, u32[]{:S(2)}, u32[]{:S(2)}) %all-to-all-start) | async-done | bytes 196640 | tf_op jit(solution)/shard_map/all_to_all | solution.py:467
  45.5 3.0 %shard_map.97 = (f32[16,136,128]{2,1,0:T(8,128)S(1)}, f32[16,128,128]{2,1,0:T(8,128)}, f32[16,16,128]{2,1,0:T(8,128)S(1)}) custom-call(s32[3]{0:T(128)S(1)} %copy-done.7, f32[16,24,128]{2,1,0:T(8,128)S(1)} %all-to-all-done.parts, f32[256,128]{1,0:T(8,128)S(1)} %copy-done.5, f32[128,128]{1,0:T(8,128)S(1)} %fusion.start, f32[32,128]{1,0:T(8,128)S(1)} %reshape.56.coef), custom_call_target="tpu_custom_call" | custom-call | tf_op jit(solution)/shard_map/pallas_call | solution.py:518
  48.4 23.4 %all_to_all.20 = f32[16,136,128]{2,1,0:T(8,128)S(1)} all-to-all(f32[16,136,128]{2,1,0:T(8,128)S(1)} %get-tuple-element.37), channel_id=1, replica_groups=mesh['tm'=16,'gx'=4,'gy'=4] {'gx','gy'}, dimensions={0} | all-to-all | bytes 2228224 | tf_op jit(solution)/shard_map/all_to_all | solution.py:467
  71.8 3.7 %all-to-all-start.2 = ((f32[16,128,128]{2,1,0:T(8,128)}), f32[16,128,128]{2,1,0:T(8,128)S(1)}, u32[]{:S(2)}, u32[]{:S(2)}) async-start(f32[16,128,128]{2,1,0:T(8,128)} %get-tuple-element.39), calls=%async_computation.2 | async-start | bytes 2097152 | tf_op jit(solution)/shard_map/all_to_all | solution.py:467
  76.9 6.1 %collective-permute-done.10.lo = f32[135,8,128]{2,1,0:T(8,128)S(1)} collective-permute-done((f32[135,8,128]{2,1,0:T(8,128)S(1)}, f32[135,8,128]{2,1,0:T(8,128)S(1)}, u32[]{:S(2)}, u32[]{:S(2)}) %collective-permute-start.10) | collective-permute-done | bytes 552992 | tf_op jit(solution)/shard_map/ppermute | solution.py:526
  83.0 2.8 %collective-permute-done.11.hi = f32[135,8,128]{2,1,0:T(8,128)S(1)} collective-permute-done((f32[135,8,128]{2,1,0:T(8,128)S(1)}, f32[135,8,128]{2,1,0:T(8,128)S(1)}, u32[]{:S(2)}, u32[]{:S(2)}) %collective-permute-start.11) | collective-permute-done | bytes 552992 | tf_op jit(solution)/shard_map/ppermute | solution.py:527
  85.7 8.9 %shard_map.99 = (f32[16,16,8,128]{3,2,1,0:T(8,128)S(1)}, f32[16,16,8,128]{3,2,1,0:T(8,128)S(1)}) custom-call(s32[3]{0:T(128)S(1)} %copy-done.7, f32[16]{0:T(128)S(1)} %broadcast_multiply_fusion.beta, f32[16,16,8,128]{3,2,1,0:T(8,128)S(1)} %get-tuple-element.41.own, f32[16,8,128]{2,1,0:T(8,128)S(1)} %get-tuple-element.42.kown, ...), custom_call_target="tpu_custom_call" | custom-call | tf_op jit(solution)/shard_map/pallas_call | solution.py:529
  94.7 0.9 copy-done.4
  95.6 1.5 %shard_map.100 = f32[16,88,128]{2,1,0:T(8,128)S(1)} custom-call(s32[3]{0:T(128)S(1)} %copy-done.7, f32[2048,128]{1,0:T(8,128)S(1)} %bitcast.28, f32[2048,128]{1,0:T(8,128)S(1)} %bitcast.29, f32[2048,128]{1,0:T(8,128)S(1)} %bitcast.30, f32[16,24,128]{2,1,0:T(8,128)S(1)} %all-to-all-done.parts, f32[16,16,128]{2,1,0:T(8,128)S(1)} %copy-done.4, ...), custom_call_target="tpu_custom_call" | custom-call | tf_op jit(solution)/shard_map/pallas_call | solution.py:537
  97.1 27.0 %all_to_all.21.got = f32[16,88,128]{2,1,0:T(8,128)S(1)} all-to-all(f32[16,88,128]{2,1,0:T(8,128)S(1)} %shard_map.100), channel_id=1, replica_groups=mesh['tm'=16,'gx'=4,'gy'=4] {'tm'}, dimensions={0} | all-to-all | bytes 1441792 | tf_op jit(solution)/shard_map/all_to_all | solution.py:467
  124.0 2.2 %collective-permute-done.12.other = f32[16,88,128]{2,1,0:T(8,128)S(1)} collective-permute-done((f32[16,88,128]{2,1,0:T(8,128)S(1)}, f32[16,88,128]{2,1,0:T(8,128)S(1)}, u32[]{:S(2)}, u32[]{:S(2)}) %collective-permute-start.12) | collective-permute-done | bytes 720928 | tf_op jit(solution)/shard_map/ppermute | solution.py:541
  126.2 2.0 %shard_map.101 = (f32[16,64,256]{2,1,0:T(8,128)}, f32[64,256]{1,0:T(8,128)}, f32[8,128]{1,0:T(8,128)S(1)}) custom-call(s32[3]{0:T(128)S(1)} %copy-done.7, f32[16,88,128]{2,1,0:T(8,128)S(1)} %all_to_all.21.got, f32[16,88,128]{2,1,0:T(8,128)S(1)} %collective-permute-done.12.other, f32[32,128]{1,0:T(8,128)S(1)} %reshape.56.coef), custom_call_target="tpu_custom_call" | custom-call | tf_op jit(solution)/shard_map/pallas_call | solution.py:542
  (53 shorter events, 7.8 us)
Async XLA Ops:
  1.3 10.5 %copy-start.7 = (s32[3]{0:T(128)S(1)}, s32[3]{0:T(128)}, u32[]{:S(2)}) copy-start(s32[3]{0:T(128)} %pad_add_fusion.at) | copy-start | bytes 40
  4.7 7.0 %copy-start = (f32[64,256]{1,0:T(8,128)S(1)}, f32[64,256]{1,0:T(8,128)}, u32[]{:S(2)}) copy-start(f32[64,256]{1,0:T(8,128)} %get-tuple-element.27.u) | copy-start | bytes 196612
  4.7 7.0 %copy-start.1 = (f32[64,256]{1,0:T(8,128)S(1)}, f32[64,256]{1,0:T(8,128)}, u32[]{:S(2)}) copy-start(f32[64,256]{1,0:T(8,128)} %get-tuple-element.28.kap) | copy-start | bytes 196612
  4.7 7.0 %copy-start.2 = (f32[64,256]{1,0:T(8,128)S(1)}, f32[64,256]{1,0:T(8,128)}, u32[]{:S(2)}) copy-start(f32[64,256]{1,0:T(8,128)} %get-tuple-element.29.g0) | copy-start | bytes 196612
  4.7 10.4 %copy-start.8 = (f32[16]{0:T(128)S(1)}, f32[16]{0:T(128)}, u32[]{:S(2)}) copy-start(f32[16]{0:T(128)} %rate_in.1) | copy-start | bytes 196
  4.7 10.4 %copy-start.9 = (f32[16]{0:T(128)S(1)}, f32[16]{0:T(128)}, u32[]{:S(2)}) copy-start(f32[16]{0:T(128)} %w_in.1) | copy-start | bytes 196
  4.8 12.2 %copy-start.6 = (f32[64,256]{1,0:T(8,128)S(1)}, f32[64,256]{1,0:T(8,128)}, u32[]{:S(2)}) copy-start(f32[64,256]{1,0:T(8,128)} %get-tuple-element.30.q1s) | copy-start | bytes 196612
  4.8 7.0 %collective-permute-start = (f32[40,256]{1,0:T(8,128)}, f32[40,256]{1,0:T(8,128)S(1)}, u32[]{:S(2)}, u32[]{:S(2)}) collective-permute-start(f32[40,256]{1,0:T(8,128)} %get-tuple-element.31), channel_id=1, source_target_pairs={{0,4},{4,8},{8,12},{12,0},{1,5},{5,9},{9,13},{13,1},{2,6},{6,10},{... | collective-permute-start | bytes 122888 | tf_op jit(solution)/shard_map/ppermute | solution.py:499
  7.0 4.8 %collective-permute-start.1 = (f32[40,256]{1,0:T(8,128)}, f32[40,256]{1,0:T(8,128)S(1)}, u32[]{:S(2)}, u32[]{:S(2)}) collective-permute-start(f32[40,256]{1,0:T(8,128)} %get-tuple-element.32), channel_id=1, source_target_pairs={{0,12},{4,0},{8,4},{12,8},{1,13},{5,1},{9,5},{13,9},{2,14},{6,2},{... | collective-permute-start | bytes 122888 | tf_op jit(solution)/shard_map/ppermute | solution.py:500
  9.7 25.4 %collective-permute-start.5 = (f32[4,128,128]{2,1,0:T(8,128)S(1)}, f32[4,128,128]{2,1,0:T(8,128)S(1)}, u32[]{:S(2)}, u32[]{:S(2)}) collective-permute-start(f32[4,128,128]{2,1,0:T(8,128)S(1)} %get-tuple-element.51), channel_id=1, source_target_pairs={{0,128},{1,129},{2,130},{3,131},{4,132},{5,133},{6,134},{7,135},{8... | collective-permute-start | bytes 786440 | tf_op jit(solution)/shard_map/ppermute | solution.py:501
  10.3 24.7 %collective-permute-start.6 = (f32[4,128,128]{2,1,0:T(8,128)S(1)}, f32[4,128,128]{2,1,0:T(8,128)S(1)}, u32[]{:S(2)}, u32[]{:S(2)}) collective-permute-start(f32[4,128,128]{2,1,0:T(8,128)S(1)} %get-tuple-element.52), channel_id=1, source_target_pairs={{0,192},{1,193},{2,194},{3,195},{4,196},{5,197},{6,198},{7,199},{8... | collective-permute-start | bytes 786440 | tf_op jit(solution)/shard_map/ppermute | solution.py:501
  11.0 24.1 %collective-permute-start.4 = (f32[4,128,128]{2,1,0:T(8,128)S(1)}, f32[4,128,128]{2,1,0:T(8,128)S(1)}, u32[]{:S(2)}, u32[]{:S(2)}) collective-permute-start(f32[4,128,128]{2,1,0:T(8,128)S(1)} %get-tuple-element.53), channel_id=1, source_target_pairs={{0,64},{1,65},{2,66},{3,67},{4,68},{5,69},{6,70},{7,71},{8,72},{9,... | collective-permute-start | bytes 786440 | tf_op jit(solution)/shard_map/ppermute | solution.py:501
  12.4 4.6 %collective-permute-start.2 = (f32[80,256]{1,0:T(8,128)S(1)}, f32[80,256]{1,0:T(8,128)S(1)}, u32[]{:S(2)}, u32[]{:S(2)}) collective-permute-start(f32[80,256]{1,0:T(8,128)S(1)} %get-tuple-element.33), channel_id=1, source_target_pairs={{0,1},{1,2},{2,3},{3,0},{4,5},{5,6},{6,7},{7,4},{8,9},{9,10},{10,1... | collective-permute-start | bytes 245768 | tf_op jit(solution)/shard_map/ppermute | solution.py:504
  13.7 3.3 %collective-permute-start.3 = (f32[80,256]{1,0:T(8,128)S(1)}, f32[80,256]{1,0:T(8,128)S(1)}, u32[]{:S(2)}, u32[]{:S(2)}) collective-permute-start(f32[80,256]{1,0:T(8,128)S(1)} %get-tuple-element.34), channel_id=1, source_target_pairs={{0,3},{1,0},{2,1},{3,2},{4,7},{5,4},{6,5},{7,6},{8,11},{9,8},{10,9... | collective-permute-start | bytes 245768 | tf_op jit(solution)/shard_map/ppermute | solution.py:505
  19.6 25.9 %all-to-all-start = ((f32[16,24,128]{2,1,0:T(8,128)}), f32[16,24,128]{2,1,0:T(8,128)S(1)}, u32[]{:S(2)}, u32[]{:S(2)}) async-start(f32[16,24,128]{2,1,0:T(8,128)} %shard_map.96), calls=%async_computation | async-start | bytes 393216 | tf_op jit(solution)/shard_map/all_to_all | solution.py:467
  35.1 10.4 %copy-start.5 = (f32[256,128]{1,0:T(8,128)S(1)}, f32[256,128]{1,0:T(8,128)}, u32[]{:S(2)}) copy-start(f32[256,128]{1,0:T(8,128)} %get-tuple-element.35.sk) | copy-start | bytes 393220
  36.2 3.0 %collective-permute-start.8 = (f32[128,128]{1,0:T(8,128)S(1)}, f32[128,128]{1,0:T(8,128)S(1)}, u32[]{:S(2)}, u32[]{:S(2)}) collective-permute-start(f32[128,128]{1,0:T(8,128)S(1)} %get-tuple-element.54), channel_id=1, source_target_pairs={{0,32},{64,96},{128,160},{192,224},{1,33},{65,97},{129,161},{193,2... | collective-permute-start | bytes 196616 | tf_op jit(solution)/shard_map/ppermute | solution.py:509
  36.8 2.3 %collective-permute-start.9 = (f32[128,128]{1,0:T(8,128)S(1)}, f32[128,128]{1,0:T(8,128)S(1)}, u32[]{:S(2)}, u32[]{:S(2)}) collective-permute-start(f32[128,128]{1,0:T(8,128)S(1)} %get-tuple-element.55), channel_id=1, source_target_pairs={{0,48},{64,112},{128,176},{192,240},{1,49},{65,113},{129,177},{193... | collective-permute-start | bytes 196616 | tf_op jit(solution)/shard_map/ppermute | solution.py:509
  37.5 5.9 %collective-permute-start.7 = (f32[128,128]{1,0:T(8,128)S(1)}, f32[128,128]{1,0:T(8,128)S(1)}, u32[]{:S(2)}, u32[]{:S(2)}) collective-permute-start(f32[128,128]{1,0:T(8,128)S(1)} %get-tuple-element.56), channel_id=1, source_target_pairs={{0,16},{64,80},{128,144},{192,208},{1,17},{65,81},{129,145},{193,2... | collective-permute-start | bytes 196616 | tf_op jit(solution)/shard_map/ppermute | solution.py:509
  48.4 23.4 %copy-start.3 = (f32[16,16,128]{2,1,0:T(8,128)}, f32[16,16,128]{2,1,0:T(8,128)S(1)}, u32[]{:S(2)}) copy-start(f32[16,16,128]{2,1,0:T(8,128)S(1)} %get-tuple-element.47.known) | copy-start | bytes 393220
  71.8 22.8 %all-to-all-start.2 = ((f32[16,128,128]{2,1,0:T(8,128)}), f32[16,128,128]{2,1,0:T(8,128)S(1)}, u32[]{:S(2)}, u32[]{:S(2)}) async-start(f32[16,128,128]{2,1,0:T(8,128)} %get-tuple-element.39), calls=%async_computation.2 | async-start | bytes 2097152 | tf_op jit(solution)/shard_map/all_to_all | solution.py:467
  75.9 7.0 %collective-permute-start.10 = (f32[135,8,128]{2,1,0:T(8,128)S(1)}, f32[135,8,128]{2,1,0:T(8,128)S(1)}, u32[]{:S(2)}, u32[]{:S(2)}) collective-permute-start(f32[135,8,128]{2,1,0:T(8,128)S(1)} %get-tuple-element.43), channel_id=1, source_target_pairs={{0,16},{16,32},{32,48},{48,64},{64,80},{80,96},{96,112},{112,128},... | collective-permute-start | bytes 1658888 | tf_op jit(solution)/shard_map/ppermute | solution.py:526
  76.5 9.2 %collective-permute-start.11 = (f32[135,8,128]{2,1,0:T(8,128)S(1)}, f32[135,8,128]{2,1,0:T(8,128)S(1)}, u32[]{:S(2)}, u32[]{:S(2)}) collective-permute-start(f32[135,8,128]{2,1,0:T(8,128)S(1)} %get-tuple-element.44), channel_id=1, source_target_pairs={{0,240},{16,0},{32,16},{48,32},{64,48},{80,64},{96,80},{112,96},{1... | collective-permute-start | bytes 1658888 | tf_op jit(solution)/shard_map/ppermute | solution.py:527
  124.0 2.2 %collective-permute-start.12 = (f32[16,88,128]{2,1,0:T(8,128)S(1)}, f32[16,88,128]{2,1,0:T(8,128)S(1)}, u32[]{:S(2)}, u32[]{:S(2)}) collective-permute-start(f32[16,88,128]{2,1,0:T(8,128)S(1)} %all_to_all.21.got), channel_id=1, source_target_pairs={{0,16},{16,0},{32,48},{48,32},{64,80},{80,64},{96,112},{112,96},{1... | collective-permute-start | bytes 2162696 | tf_op jit(solution)/shard_map/ppermute | solution.py:541
  (1 other events, 0.9 us)

commit v3 on v2

v3 whole, which is shorter than its diff:
```python
import functools
import jax
import jax.numpy as jnp
from jax import lax
from jax.experimental import pallas as pl
from jax.experimental.pallas import tpu as pltpu
from jax.sharding import PartitionSpec as P

STEP = 0.12
F32 = jnp.float32
VM = pl.BlockSpec(memory_space=pltpu.VMEM)
SM = pl.BlockSpec(memory_space=pltpu.SMEM)
ANY = pl.BlockSpec(memory_space=pl.ANY)
MIB = 1024 * 1024
HALO = 15
TRI = [HALO] + [HALO - j for j in range(1, HALO)]
OFF = [sum(TRI[:j]) for j in range(HALO)]
KOFF = sum(TRI)
MSG = KOFF + HALO
LAY = 48
NEW = 46
GROUP = 16


def call(kernel, outs, ins, smem, scratch=(), limit=16):
    return pl.pallas_call(
        kernel,
        out_shape=[jax.ShapeDtypeStruct(shape, F32) for shape in outs],
        in_specs=[SM] * smem + [VM] * (ins - smem),
        out_specs=[VM] * len(outs),
        scratch_shapes=[pltpu.VMEM(shape, F32) for shape in scratch],
        compiler_params=pltpu.CompilerParams(vmem_limit_bytes=limit * MIB),
    )


def lane_low(shape):
    return lax.broadcasted_iota(jnp.int32, shape, len(shape) - 1) < 64


def local_kernel(rk_in, w_in, rate_in, u_in, reg_in, s_in, modes_in, u, kap, g0, q1s, up, dn, sk,
                 rk, w, rate, reg, s, modes, sems):
    pairs = [(u_in, u), (reg_in, reg), (s_in, s), (rk_in, rk), (w_in, w), (rate_in, rate)]
    pairs += [(modes_in.at[pl.ds(4 * i, 4)], modes.at[pl.ds(4 * i, 4)]) for i in range(4)]
    copies = [pltpu.make_async_copy(a, b, sems.at[i]) for i, (a, b) in enumerate(pairs)]
    for copy in copies:
        copy.start()
    for copy in copies[:6]:
        copy.wait()
    for x in range(8):
        rows = slice(8 * x, 8 * x + 8)
        region = reg[rows]
        k = jnp.zeros((8, 256), F32)
        for r in range(8):
            k = jnp.where(region == r, rk[r], k)
        kap[rows] = k
    half = [jnp.exp(jnp.full((8, 256), -0.5 * rate[m], F32)) for m in range(16)]
    a = [s[8 * x : 8 * x + 8] for x in range(8)]
    b = [s[8 * x : 8 * x + 8] for x in range(8)]
    for m in range(16):
        if m % 4 == 0:
            copies[6 + m // 4].wait()
        for x in range(8):
            h = w[m] * modes[m, 8 * x : 8 * x + 8]
            a[x] = a[x] - h
            b[x] = b[x] - half[m] * h
    for x in range(8):
        g0[8 * x : 8 * x + 8] = a[x]
        q1s[8 * x : 8 * x + 8] = b[x]
    up[0:16] = u[48:64]
    up[16:32] = kap[48:64]
    up[32:40] = g0[56:64]
    dn[0:16] = u[0:16]
    dn[16:32] = kap[0:16]
    dn[32:40] = g0[0:8]
    sk[...] = jnp.concatenate([s[...], kap[...]], axis=0).T


def scatter_kernel(after, modes_in, out0, out1, out2, out3, modes, packed, sems):
    @pl.when(lax.axis_index("tm") == 0)
    def _():
        copies = [
            pltpu.make_async_copy(modes_in.at[pl.ds(4 * i, 4)], modes.at[pl.ds(4 * i, 4)], sems.at[i])
            for i in range(4)
        ]
        for copy in copies:
            copy.start()
        for copy in copies:
            copy.wait()
        for m in range(8):
            both = jnp.concatenate([modes[m], modes[m + 8]], axis=0).T
            packed[:, 16 * m : 16 * m + 16] = both.reshape(16, 16, 128)
        copies = [
            pltpu.make_async_copy(packed.at[pl.ds(4 * i, 4)], out, sems.at[4 + i])
            for i, out in enumerate((out0, out1, out2, out3))
        ]
        for copy in copies:
            copy.start()
        for copy in copies:
            copy.wait()


def side_kernel(u, kap, g0, xlo, xhi, yup, ydn):
    has_lo = jnp.where(lax.axis_index("gx") > 0, 1.0, 0.0).astype(F32)
    has_hi = jnp.where(lax.axis_index("gx") < 3, 1.0, 0.0).astype(F32)
    for out, first in ((yup, 6), (ydn, 0)):
        for piece in range(5):
            if piece < 4:
                src, base = (u, 0) if piece < 2 else (kap, 16)
                y = first + piece % 2
                out[16 * piece : 16 * piece + 1] = has_lo * xlo[base + 8 + y : base + 9 + y]
                out[16 * piece + 9 : 16 * piece + 10] = has_hi * xhi[base + y : base + y + 1]
            else:
                src = g0
                y = 7 if first else 0
            for x in range(8):
                at_row = 16 * piece + 1 + x
                out[at_row : at_row + 1] = src[8 * x + y : 8 * x + y + 1]


def fine_kernel(omega, u, kap, g0, q1s, xlo, xhi, ylo, yhi, fine, both, up, kp, gp, u1):
    gx, gy = lax.axis_index("gx"), lax.axis_index("gy")
    zero = jnp.zeros((24, 256), F32)
    for ref in (up, kp, gp):
        for x in range(12):
            ref[x] = zero
    for x in range(8):
        rows = slice(8 * x, 8 * x + 8)
        up[2 + x, 8:16] = u[rows]
        kp[2 + x, 8:16] = kap[rows]
        gp[2 + x, 8:16] = g0[rows]

    @pl.when(gx > 0)
    def _():
        for i in range(2):
            up[i, 8:16] = xlo[8 * i : 8 * i + 8]
            kp[i, 8:16] = xlo[16 + 8 * i : 24 + 8 * i]
        gp[1, 8:16] = xlo[32:40]

    @pl.when(gx < 3)
    def _():
        for i in range(2):
            up[10 + i, 8:16] = xhi[8 * i : 8 * i + 8]
            kp[10 + i, 8:16] = xhi[16 + 8 * i : 24 + 8 * i]
        gp[10, 8:16] = xhi[32:40]

    for cond, ref, row in ((gy > 0, ylo, 6), (gy < 3, yhi, 16)):

        @pl.when(cond)
        def _(ref=ref, row=row):
            for x in range(10):
                for i in range(2):
                    up[1 + x, row + i : row + i + 1] = ref[16 * i + x : 16 * i + x + 1]
                    kp[1 + x, row + i : row + i + 1] = ref[32 + 16 * i + x : 33 + 16 * i + x]
                if 1 <= x <= 8:
                    near = 7 if row == 6 else 16
                    gp[1 + x, near : near + 1] = ref[64 + x : 65 + x]

    z = lax.broadcasted_iota(jnp.int32, (24, 256), 1)

    def above(v):
        return jnp.where(z == 255, 0.0, pltpu.roll(v, 255, 1))

    def below(v):
        return jnp.where(z == 0, 0.0, pltpu.roll(v, 1, 1))

    def laplace(ref, x):
        uc, kc = ref[x], kp[x]
        total = jnp.zeros((24, 256), F32)
        for near_u, near_k in (
            (ref[x + 1], kp[x + 1]),
            (ref[x - 1], kp[x - 1]),
            (pltpu.roll(uc, 23, 0), pltpu.roll(kc, 23, 0)),
            (pltpu.roll(uc, 1, 0), pltpu.roll(kc, 1, 0)),
            (above(uc), above(kc)),
            (below(uc), below(kc)),
        ):
            total += (kc + near_k) * (near_u - uc)
        return 0.5 * total

    for x in range(1, 11):
        change = (0.5 * STEP) * (laplace(up, x) + gp[x])
        u1[x] = up[x] + change
        gp[x] = change

    @pl.when(gx == 0)
    def _():
        u1[1] = zero

    @pl.when(gx == 3)
    def _():
        u1[10] = zero

    @pl.when(gy == 0)
    def _():
        for x in range(1, 11):
            u1[x, 0:8] = zero[0:8]

    @pl.when(gy == 3)
    def _():
        for x in range(1, 11):
            u1[x, 16:24] = zero[0:8]

    first, second = [], []
    for x in range(8):
        rows = slice(8 * x, 8 * x + 8)
        c1 = gp[2 + x, 8:16]
        lap = laplace(u1, 2 + x)[8:16]
        c2 = (0.5 * STEP) * (lap + q1s[rows] - omega[0] * c1)
        fine[rows] = u1[2 + x, 8:16] + c2
        first.append(c1)
        second.append(c2)
    both[:, 0:16] = jnp.concatenate(first + second, axis=0).T.reshape(16, 16, 128)
    now = jnp.concatenate([u[...], u[...]], axis=0).T.reshape(16, 16, 128)
    both[:, 16:24] = jnp.where(lane_low((16, 8, 128)), now[:, 0:8], now[:, 8:16])


def doubled(v, low):
    turned = pltpu.roll(v, 64, 1)
    return jnp.where(low, v, turned), jnp.where(low, turned, v)


def unpacked(v):
    low = lane_low((8, 128))
    first, second = doubled(v, low)
    return jnp.concatenate([first, second], axis=0)


def packed_rows(v):
    return jnp.where(lane_low((8, 128)), v[0:8], v[8:16])


def known_kernel(parts, sk, start, coef, msg, known):
    low = lane_low((16, 128))
    slab = sk[pl.ds(pl.multiple_of(lax.axis_index("tm") * 16, 16), 16), :]
    source, kap = doubled(slab, low)
    h = [start[16 * m : 16 * m + 16] for m in range(8)]
    seen = []
    for j in range(16):
        c1, c2 = doubled(parts[j, 0:16], low)
        if j == 0:
            n = 2.0 * c1
            seen.append(unpacked(parts[0, 16:24]) + c1 + c2)
        else:
            q = coef[24:25] * h[0]
            for m in range(1, 8):
                q += coef[24 + m : 25 + m] * h[m]
            n = STEP * (source - (q + pltpu.roll(q, 64, 1)))
            seen.append(n + c2 - c1)
        known[j] = n
        xn = c2 - 2.0 * c1 + n
        yn = n - c1
        for m in range(8):
            h[m] = coef[m : m + 1] * h[m] + coef[16 + m : 17 + m] * (xn + coef[8 + m : 9 + m] * yn)
    last = packed_rows(kap)
    for j in range(8):
        v = jnp.where(low, seen[j], seen[j + 8])
        for p in range(16):
            msg[p, 16 * j : 16 * j + 16] = v
    for p in range(16):
        msg[p, 128:136] = last


def gather_kernel(got, own, kap, up, dn):
    low = lane_low((8, 128))

    def pair(row):
        even = got[pl.ds(row, 8, stride=272), :]
        odd = got[pl.ds(row + 136, 8, stride=272), :]
        left = jnp.where(low, even, pltpu.roll(odd, 64, 1))
        right = jnp.where(low, pltpu.roll(even, 64, 1), odd)
        return left, right

    def place(j, z, v):
        own[j, z] = v
        if j < HALO:
            if z < TRI[j]:
                dn[OFF[j] + z] = v
            if z >= 16 - TRI[j]:
                up[OFF[j] + z - (16 - TRI[j])] = v

    for j in range(8):
        for z in range(16):
            left, right = pair(16 * j + z)
            place(j, z, left)
            place(j + 8, z, right)
    for z in range(8):
        left, right = pair(128 + z)
        for at, v in ((z, left), (z + 8, right)):
            kap[at] = v
            if at < HALO:
                dn[KOFF + at] = v
            if at >= 1:
                up[KOFF + at - 1] = v


def sweep_kernel(beta, own, kown, lo, hi, parts_in, known_in, start_in, coef_in, out,
                 e, g, c, kw, parts, known, start, coef, sems):
    pairs = ((parts_in, parts), (known_in, known), (start_in, start), (coef_in, coef))
    copies = [pltpu.make_async_copy(a, b, sems.at[i]) for i, (a, b) in enumerate(pairs)]
    for copy in copies:
        copy.start()
    t = lax.axis_index("tm")
    has_lo = jnp.where(t > 0, 1.0, 0.0).astype(F32)
    has_hi = jnp.where(t < 15, 1.0, 0.0).astype(F32)

    def pick(j, first, last):
        if last <= HALO:
            start = OFF[j] + first - HALO + TRI[j]
            return has_lo * lo[start : start + last - first]
        if first > 30:
            start = OFF[j] + first - 31
            return has_hi * hi[start : start + last - first]
        return own[j, first - HALO : last - HALO]

    def groups(first, last):
        ranges = []
        for a, b in ((first, HALO), (HALO, 31), (31, last)):
            pieces = -(-(b - a) // GROUP)
            edge = [a + (b - a) * k // pieces for k in range(pieces + 1)] if pieces else []
            ranges += list(zip(edge[:-1], edge[1:]))
        return ranges

    zero = jnp.zeros((8, 128), F32)
    kw[0] = zero
    kw[47] = zero
    kw[1:16] = has_lo * lo[KOFF:MSG]
    kw[16:32] = kown[...]
    kw[32:47] = has_hi * hi[KOFF:MSG]

    lane = lax.broadcasted_iota(jnp.int32, (8, 128), 1)
    sub = lax.broadcasted_iota(jnp.int32, (8, 128), 0)
    x_start, x_end = lane < 8, lane >= 120
    y_start, y_end = lane % 8 == 0, lane % 8 == 7
    inside = (
        jnp.logical_not(x_end & (sub % 2 == 1)),
        jnp.logical_not(x_start & (sub % 2 == 0)),
        jnp.logical_not(y_end & (sub // 2 == 3)),
        jnp.logical_not(y_start & (sub // 2 == 0)),
    )

    def near(a):
        down, up = pltpu.roll(a, 8, 2), pltpu.roll(a, 120, 2)
        xm = jnp.where(x_start, pltpu.roll(down, 1, 1), down)
        xp = jnp.where(x_end, pltpu.roll(up, 7, 1), up)
        yp = pltpu.roll(jnp.where(y_start, pltpu.roll(down, 6, 1), a), 127, 2)
        ym = pltpu.roll(jnp.where(y_end, pltpu.roll(up, 2, 1), a), 1, 2)
        return xp, xm, yp, ym

    for first, last in groups(1, NEW - 1):
        kc = kw[first + 1 : last + 1]
        layer = lax.broadcasted_iota(jnp.int32, kc.shape, 0) + first
        place = t * 16 - HALO + layer
        scale = jnp.where((place >= 0) & (place < 256), 0.5 * STEP, 0.0).astype(F32)
        total = jnp.zeros_like(kc)
        for i, kn in enumerate(near(kc)):
            face = scale * (kc + jnp.where(inside[i], kn, 0.0))
            total += face
            c[i, first:last] = jnp.where(inside[i], face, 0.0)
        for i, kn in ((4, kw[first + 2 : last + 2]), (5, kw[first:last])):
            face = scale * (kc + kn)
            total += face
            c[i, first:last] = face
        c[6, first:last] = -total

    for first, last in groups(0, NEW):
        e[0, first:last] = pick(0, first, last)
    for j in range(1, 16):
        for first, last in groups(j, NEW - j):
            mid = e[j - 1, first:last]
            acc = c[6, first:last] * mid
            acc += c[4, first:last] * e[j - 1, first + 1 : last + 1]
            acc += c[5, first:last] * e[j - 1, first - 1 : last - 1]
            for d, un in enumerate(near(mid)):
                acc += c[d, first:last] * un
            for i in range(1, j):
                acc -= beta[j - 1 - i] * g[i, first:last]
            now = mid + acc + pick(j, first, last)
            g[j, first:last] = acc
            e[j, first:last] = now
    for copy in copies:
        copy.wait()
    low = lane_low((16, 128))
    p = lax.axis_index("gy") * 4 + lax.axis_index("gx")
    sublane = p // 2
    mine = low == (p % 2 == 0)
    e_rows = e.reshape(16 * LAY * 8, 128)
    g_rows = g.reshape(16 * LAY * 8, 128)

    def block_of(ref, j):
        first = (j * LAY + HALO) * 8 + sublane
        a = ref[pl.ds(first, 8, stride=8), :]
        b = ref[pl.ds(first + 64, 8, stride=8), :]
        both = jnp.concatenate([a, b], axis=0)
        return jnp.where(mine, both, pltpu.roll(both, 64, 1))

    h = [start[16 * m : 16 * m + 16] for m in range(8)]
    for j in range(16):
        c1, c2 = doubled(parts[j, 0:16], low)
        n = known[j]
        if j > 0:
            n = n + block_of(g_rows, j)
        xn = c2 - 2.0 * c1 + n
        yn = n - c1
        for m in range(8):
            h[m] = coef[m : m + 1] * h[m] + coef[16 + m : 17 + m] * (xn + coef[8 + m : 9 + m] * yn)
            if j % 2 == 0:
                at_row = 16 * (m % 4)
                out[j + m // 4, at_row : at_row + 16] = h[m]
        out[j, 64:72] = packed_rows(block_of(e_rows, j))


def rows_of(ref):
    return jnp.concatenate([unpacked(ref[t, 64:72]) for t in range(16)], axis=0)


def field_kernel(got, fine, field, part):
    now = rows_of(got).T[0:64]
    field[...] = now
    diff = now - fine[...]
    diff = diff * diff
    total = jnp.zeros((8, 128), F32)
    for x in range(8):
        total += diff[8 * x : 8 * x + 8, 0:128] + diff[8 * x : 8 * x + 8, 128:256]
    for p in range(16):
        part[p] = total


def final_kernel(got, other, mine, coef, modes):
    def finish(low, high, odd):
        x = y = None
        if odd:
            c1, c2 = doubled(mine[:, 0:16].reshape(256, 128), lane_low((256, 128)))
            x = rows_of(high) - rows_of(low) - c1
            y = x - c2 + c1
        for m in range(8):
            src = low if m < 4 else high
            first = 16 * (m % 4)
            both = src[:, first : first + 16].reshape(256, 128)
            if odd:
                both = coef[m : m + 1] * both
                both += coef[16 + m : 17 + m] * (x + coef[8 + m : 9 + m] * y)
            both = both.T
            modes[m] = both[0:64]
            modes[m + 8] = both[64:128]

    t = lax.axis_index("tm")

    @pl.when(t % 2 == 0)
    def _():
        finish(got, other, False)

    @pl.when(t % 2 == 1)
    def _():
        finish(other, got, True)


def ring(axis, step):
    n = lax.axis_size(axis)
    return [(i, (i + step) % n) for i in range(n)]


def swap(value, axis):
    return lax.all_to_all(value, axis, 0, 0, tiled=True)


def per_device(field, modes, source, regions, region_kappa, mode_rate, mode_weight):
    u = field.reshape(64, 256)
    h = modes.reshape(16, 64, 256)
    s = source.reshape(64, 256)
    reg = regions.reshape(64, 256)
    t = lax.axis_index("tm")

    f = jnp.exp(-0.5 * mode_rate)
    e = jnp.exp(-mode_rate)
    w = mode_weight
    omega = jnp.sum(w * (1.0 - f)).reshape(1)
    powers = jnp.exp(-mode_rate[None, :] * jnp.arange(16, dtype=F32)[:, None])
    beta = STEP * jnp.sum((w * (1.0 - e))[None, :] * powers, axis=1)
    coef = jnp.concatenate([e, f, 1.0 - f, w]).reshape(4, 2, 8).transpose(0, 2, 1)
    coef = jnp.broadcast_to(coef[..., None], (4, 8, 2, 64)).reshape(32, 128)

    plane = (64, 256)
    outs = [plane] * 4 + [(40, 256)] * 2 + [(256, 128)]
    u, kap, g0, q1s, up, dn, sk = pl.pallas_call(
        local_kernel,
        out_shape=[jax.ShapeDtypeStruct(shape, F32) for shape in outs],
        in_specs=[ANY] * 7,
        out_specs=[VM] * 7,
        scratch_shapes=[pltpu.SMEM((8,), F32), pltpu.SMEM((16,), F32), pltpu.SMEM((16,), F32)]
        + [pltpu.VMEM(plane, jnp.int32), pltpu.VMEM(plane, F32), pltpu.VMEM((16, 64, 256), F32)]
        + [pltpu.SemaphoreType.DMA((10,))],
        compiler_params=pltpu.CompilerParams(vmem_limit_bytes=60 * MIB),
    )(region_kappa, w, mode_rate, u, reg, s, h)
    xlo = lax.ppermute(up, "gx", ring("gx", 1))
    xhi = lax.ppermute(dn, "gx", ring("gx", -1))
    chunks = pl.pallas_call(
        scatter_kernel,
        out_shape=[jax.ShapeDtypeStruct((4, 128, 128), F32)] * 4,
        in_specs=[ANY, ANY],
        out_specs=[ANY] * 4,
        scratch_shapes=[pltpu.VMEM((16, 64, 256), F32), pltpu.VMEM((16, 128, 128), F32)]
        + [pltpu.SemaphoreType.DMA((8,))],
        compiler_params=pltpu.CompilerParams(vmem_limit_bytes=60 * MIB),
    )(sk, h)

    yup, ydn = call(side_kernel, [(80, 256)] * 2, 5, 0)(u, kap, g0, xlo, xhi)
    ylo = lax.ppermute(yup, "gy", ring("gy", 1))
    yhi = lax.ppermute(ydn, "gy", ring("gy", -1))
    far = [lax.ppermute(chunks[k], "tm", [(0, 4 * k)]) for k in (1, 2, 3)]

    fine, both = call(
        fine_kernel, [plane, (16, 24, 128)], 9, 1, [(12, 24, 256)] * 4
    )(omega, u, kap, g0, q1s, xlo, xhi, ylo, yhi)
    parts = swap(both, "tm")

    quarter = jnp.where(t == 0, chunks[0], far[0] + far[1] + far[2])
    close = [
        lax.ppermute(quarter[k], "tm", [(4 * a, 4 * a + k) for a in range(4)]) for k in (1, 2, 3)
    ]
    start = jnp.where(t % 4 == 0, quarter[0], close[0] + close[1] + close[2])

    msg, known = call(known_kernel, [(16, 136, 128), (16, 16, 128)], 4, 0)(
        parts, sk, start, coef
    )
    got = swap(msg, ("gy", "gx"))
    own, kown, up, dn = call(
        gather_kernel, [(16, 16, 8, 128), (16, 8, 128), (MSG, 8, 128), (MSG, 8, 128)], 1, 0
    )(got.reshape(16 * 136, 128))
    lo = lax.ppermute(up, "tm", ring("tm", 1))
    hi = lax.ppermute(dn, "tm", ring("tm", -1))
    out = pl.pallas_call(
        sweep_kernel,
        out_shape=jax.ShapeDtypeStruct((16, 72, 128), F32),
        in_specs=[SM] + [VM] * 4 + [ANY] * 4,
        out_specs=VM,
        scratch_shapes=[
            pltpu.VMEM(shape, F32)
            for shape in (
                (16, LAY, 8, 128),
                (16, LAY, 8, 128),
                (7, LAY, 8, 128),
                (LAY, 8, 128),
                (16, 24, 128),
                (16, 16, 128),
                (128, 128),
                (32, 128),
            )
        ]
        + [pltpu.SemaphoreType.DMA((4,))],
        compiler_params=pltpu.CompilerParams(vmem_limit_bytes=24 * MIB),
    )(beta, own, kown, lo, hi, parts, known, start, coef)
    back = swap(out, "tm")
    other = lax.ppermute(back, "tm", [(i, i ^ 1) for i in range(16)])
    new_field, part = call(field_kernel, [plane, (16, 8, 128)], 2, 0)(back, fine)
    parted = swap(part, ("gy", "gx"))
    new_modes = call(final_kernel, [(16, 64, 256)], 4, 0)(back, other, both, coef)[0]
    parted, new_modes = lax.optimization_barrier((parted, new_modes))
    size = jnp.sqrt(jnp.sum(parted) / 262144.0).reshape(1)
    return (new_field.reshape(1, 8, 8, 256), new_modes.reshape(1, 16, 8, 8, 256), size)


def solution(mesh):
    return jax.shard_map(
        per_device,
        mesh=mesh,
        in_specs=(
            P("tm", "gx", "gy", None),
            P("tm", None, "gx", "gy", None),
            P("gx", "gy", None),
            P("gx", "gy", None),
            P(),
            P(),
            P(),
        ),
        out_specs=(P("tm", "gx", "gy", None), P("tm", None, "gx", "gy", None), P("tm")),
        check_vma=False,
    )
```

time: 129 us -> 120 us (0.930)
  Pallas kernels: 22.4 us -> 15.1 us
  blocking collectives: 50.4 us -> 47.2 us
  waiting for transfers between devices: 18.3 us -> 21.1 us
  local copies, waits for them, and re-layouts: 3.23 us -> 0.66 us
  between operations: 0.92 us -> 2.74 us
    pallas_call x6 -> x7, Pallas kernels: 18.6 us -> 12.5 us  [the longest x1 5.79 us: per_device(): pl.pallas_call(sweep_kernel, out_shape=jax.ShapeDtypeStruct((16, 72, 128)...]
    all_to_all x2, waiting for transfers between devices: 1.99 us -> 7.01 us  [swap(): return lax.all_to_all(value, axis, 0, 0, tiled=True)]
    all_to_all x2, blocking collectives: 50.4 us -> 47.2 us  [swap(): return lax.all_to_all(value, axis, 0, 0, tiled=True)]
    ppermute x1, waiting for transfers between devices: 2.19 us -> 0.01 us  [per_device(): other = lax.ppermute(back, 'tm', [(i, i ^ 1) for i in range(16)])]
    slice x2 -> x0, local copies, waits for them, and re-layouts: 1.67 us -> none  [the longest x1 1.16 us: per_device(): packed[4 * k:4 * k + 4]]
  transfers between devices with their start and end apart: 15 -> 15, of which waited for: 6 -> 6; matrix products, arithmetic and copies ran while one was open for 3% -> 1% of each run, Pallas kernels for 10% -> 4%
where the time goes in v3:
time: 120 us; the launch traced here: 119 us
  blocking collectives  47.2 us (39%)
  starting transfers between devices  30.8 us (26%)
  waiting for transfers between devices  21.1 us (18%)
  Pallas kernels  15.1 us (13%)
  between operations  2.74 us (2%)
  other arithmetic  1.43 us (1%)
    all_to_all x2, blocking collectives, swap(): return lax.all_to_all(value, axis, 0, 0, tiled=True)  47.2 us
    all_to_all x2, starting transfers between devices, swap(): return lax.all_to_all(value, axis, 0, 0, tiled=True)  18.4 us
    all_to_all x2, waiting for transfers between devices, swap(): return lax.all_to_all(value, axis, 0, 0, tiled=True)  7.01 us
    ppermute x1, waiting for transfers between devices, per_device(): lo = lax.ppermute(up, 'tm', ring('tm', 1))  6.1 us
    pallas_call x1, Pallas kernels, per_device(): pl.pallas_call(sweep_kernel, out_shape=jax.ShapeDtypeStruct((16, 72, 128)...  5.79 us
    ppermute x3, waiting for transfers between devices, per_device(): lax.ppermute(quarter[k], 'tm', [(4 * a, 4 * a + k) for a in range(4)])  4.32 us
    ppermute x1, waiting for transfers between devices, per_device(): hi = lax.ppermute(dn, 'tm', ring('tm', -1))  2.77 us
    ppermute x3, starting transfers between devices, per_device(): lax.ppermute(quarter[k], 'tm', [(4 * a, 4 * a + k) for a in range(4)])  2.62 us
  transfers between devices with their start and end apart: 15, of which 6 were waited for; matrix products, arithmetic and copies ran while one was open for 1% of the time, Pallas kernels for 4%

profile of v3, /device:TPU:1, one launch (start us, length us, event | category | flops | bytes accessed | tf_op | source)
XLA Modules:
  0.0 119.1 jit_solution(12377961100728911571)
XLA Ops:
  0.7 2.2 %shard_map.94 = (f32[64,256]{1,0:T(8,128)}, f32[64,256]{1,0:T(8,128)}, f32[64,256]{1,0:T(8,128)}, f32[64,256]{1,0:T(8,128)}, f32[40,256]{1,0:T(8,128)}, /*index=5*/f32[40,256]{1,0:T(8,128)}, f32[256,128]{1,0:T(8,128)}) custom-call(f32[8]{0:T(128)} %rk_in.1, f32[16]{0:T(128)} %w_in.1, f32[16]{0:T(128)} %rate_in.1, f32[64,256]{1,0:T(8,128)} %bitcast.25, ...), custom_call_target="tpu_custom_call" | custom-call | tf_op jit(solution)/shard_map/pallas_call | solution.py:484
  2.9 2.2 %collective-permute-start = (f32[40,256]{1,0:T(8,128)}, f32[40,256]{1,0:T(8,128)S(1)}, u32[]{:S(2)}, u32[]{:S(2)}) collective-permute-start(f32[40,256]{1,0:T(8,128)} %get-tuple-element.32), channel_id=1, source_target_pairs={{0,4},{4,8},{8,12},{12,0},{1,5},{5,9},{9,13},{13,1},{2,6},{6,10},{... | collective-permute-start | bytes 122888 | tf_op jit(solution)/shard_map/ppermute | solution.py:494
  5.1 1.5 %collective-permute-start.1 = (f32[40,256]{1,0:T(8,128)}, f32[40,256]{1,0:T(8,128)S(1)}, u32[]{:S(2)}, u32[]{:S(2)}) collective-permute-start(f32[40,256]{1,0:T(8,128)} %get-tuple-element.33), channel_id=1, source_target_pairs={{0,12},{4,0},{8,4},{12,8},{1,13},{5,1},{9,5},{13,9},{2,14},{6,2},{... | collective-permute-start | bytes 122888 | tf_op jit(solution)/shard_map/ppermute | solution.py:495
  6.7 0.8 collective-permute-start.4
  7.5 0.7 collective-permute-start.5
  9.0 1.3 %collective-permute-start.2 = (f32[80,256]{1,0:T(8,128)S(1)}, f32[80,256]{1,0:T(8,128)S(1)}, u32[]{:S(2)}, u32[]{:S(2)}) collective-permute-start(f32[80,256]{1,0:T(8,128)S(1)} %get-tuple-element.34), channel_id=1, source_target_pairs={{0,1},{1,2},{2,3},{3,0},{4,5},{5,6},{6,7},{7,4},{8,9},{9,10},{10,1... | collective-permute-start | bytes 245768 | tf_op jit(solution)/shard_map/ppermute | solution.py:507
  10.3 1.5 %collective-permute-start.3 = (f32[80,256]{1,0:T(8,128)S(1)}, f32[80,256]{1,0:T(8,128)S(1)}, u32[]{:S(2)}, u32[]{:S(2)}) collective-permute-start(f32[80,256]{1,0:T(8,128)S(1)} %get-tuple-element.35), channel_id=1, source_target_pairs={{0,3},{1,0},{2,1},{3,2},{4,7},{5,4},{6,5},{7,6},{8,11},{9,8},{10,9... | collective-permute-start | bytes 245768 | tf_op jit(solution)/shard_map/ppermute | solution.py:508
  12.7 0.9 collective-permute-done.2.ylo
  13.6 2.0 %shard_map.96 = (f32[64,256]{1,0:T(8,128)S(1)}, f32[16,24,128]{2,1,0:T(8,128)}) custom-call(f32[1]{0:T(128)} %bitcast.omega, f32[64,256]{1,0:T(8,128)S(1)} %copy-done.1, f32[64,256]{1,0:T(8,128)S(1)} %copy-done.2, f32[64,256]{1,0:T(8,128)S(1)} %copy-done.3, f32[64,256]{1,0:T(8,128)S(1)} %copy-done.4, f32[40,256]{1,0:T(8,128)S(1)} %collective-permute-done.xlo, ...), custom_call_target="tpu_custom_call" | custom-call | tf_op jit(solution)/shard_map/pallas_call | solution.py:511
  15.6 14.9 %all-to-all-start = ((f32[16,24,128]{2,1,0:T(8,128)}), f32[16,24,128]{2,1,0:T(8,128)S(1)}, u32[]{:S(2)}, u32[]{:S(2)}) async-start(f32[16,24,128]{2,1,0:T(8,128)} %get-tuple-element.36.mine), calls=%async_computation | async-start | bytes 393216 | tf_op jit(solution)/shard_map/all_to_all | solution.py:463
  32.0 1.3 %collective-permute-start.7 = (f32[128,128]{1,0:T(8,128)S(1)}, f32[128,128]{1,0:T(8,128)S(1)}, u32[]{:S(2)}, u32[]{:S(2)}) collective-permute-start(f32[128,128]{1,0:T(8,128)S(1)} %get-tuple-element.55), channel_id=1, source_target_pairs={{0,16},{64,80},{128,144},{192,208},{1,17},{65,81},{129,145},{193,2... | collective-permute-start | bytes 196616 | tf_op jit(solution)/shard_map/ppermute | solution.py:518
  33.6 4.3 %collective-permute-done.7 = f32[128,128]{1,0:T(8,128)S(1)} collective-permute-done((f32[128,128]{1,0:T(8,128)S(1)}, f32[128,128]{1,0:T(8,128)S(1)}, u32[]{:S(2)}, u32[]{:S(2)}) %collective-permute-start.7) | collective-permute-done | bytes 65568 | tf_op jit(solution)/shard_map/ppermute | solution.py:518
  37.9 2.9 %all-to-all-done.parts.parts_in = f32[16,24,128]{2,1,0:T(8,128)S(1)} async-done(((f32[16,24,128]{2,1,0:T(8,128)}), f32[16,24,128]{2,1,0:T(8,128)S(1)}, u32[]{:S(2)}, u32[]{:S(2)}) %all-to-all-start) | async-done | bytes 196640 | tf_op jit(solution)/shard_map/all_to_all | solution.py:463
  40.9 1.4 %shard_map.98 = (f32[16,136,128]{2,1,0:T(8,128)S(1)}, f32[16,16,128]{2,1,0:T(8,128)S(1)}) custom-call(f32[16,24,128]{2,1,0:T(8,128)S(1)} %all-to-all-done.parts.parts_in, f32[256,128]{1,0:T(8,128)S(1)} %copy-done, f32[128,128]{1,0:T(8,128)S(1)} %fusion.start.start_in, f32[32,128]{1,0:T(8,128)S(1)} %reshape.50.coef.coef_in), custom_call_target="tpu_custom_call" | custom-call | tf_op jit(solution)/shard_map/pallas_call | solution.py:522
  42.3 23.1 %all_to_all.20 = f32[16,136,128]{2,1,0:T(8,128)S(1)} all-to-all(f32[16,136,128]{2,1,0:T(8,128)S(1)} %get-tuple-element.42), channel_id=1, replica_groups=mesh['tm'=16,'gx'=4,'gy'=4] {'gy','gx'}, dimensions={0} | all-to-all | bytes 2228224 | tf_op jit(solution)/shard_map/all_to_all | solution.py:463
  65.9 0.8 collective-permute-start.10
  67.0 6.1 %collective-permute-done.10.lo = f32[135,8,128]{2,1,0:T(8,128)S(1)} collective-permute-done((f32[135,8,128]{2,1,0:T(8,128)S(1)}, f32[135,8,128]{2,1,0:T(8,128)S(1)}, u32[]{:S(2)}, u32[]{:S(2)}) %collective-permute-start.10) | collective-permute-done | bytes 552992 | tf_op jit(solution)/shard_map/ppermute | solution.py:529
  73.1 2.8 %collective-permute-done.11.hi = f32[135,8,128]{2,1,0:T(8,128)S(1)} collective-permute-done((f32[135,8,128]{2,1,0:T(8,128)S(1)}, f32[135,8,128]{2,1,0:T(8,128)S(1)}, u32[]{:S(2)}, u32[]{:S(2)}) %collective-permute-start.11) | collective-permute-done | bytes 552992 | tf_op jit(solution)/shard_map/ppermute | solution.py:530
  75.8 5.8 %shard_map.100 = f32[16,72,128]{2,1,0:T(8,128)S(1)} custom-call(f32[16]{0:T(128)S(1)} %broadcast_multiply_fusion.beta, f32[16,16,8,128]{3,2,1,0:T(8,128)S(1)} %get-tuple-element.43.own, f32[16,8,128]{2,1,0:T(8,128)S(1)} %get-tuple-element.44.kown, f32[135,8,128]{2,1,0:T(8,128)S(1)} %collective-permute-done.10.lo, ...), custom_call_target="tpu_custom_call" | custom-call | tf_op jit(solution)/shard_map/pallas_call | solution.py:531
  81.6 24.1 %all_to_all.21.got = f32[16,72,128]{2,1,0:T(8,128)S(1)} all-to-all(f32[16,72,128]{2,1,0:T(8,128)S(1)} %shard_map.100), channel_id=1, replica_groups=mesh['tm'=16,'gx'=4,'gy'=4] {'tm'}, dimensions={0} | all-to-all | bytes 1179648 | tf_op jit(solution)/shard_map/all_to_all | solution.py:463
  105.9 0.8 shard_map.101
  106.7 3.5 %all-to-all-start.3 = ((f32[16,8,128]{2,1,0:T(8,128)}), f32[16,8,128]{2,1,0:T(8,128)S(1)}, u32[]{:S(2)}, u32[]{:S(2)}) async-start(f32[16,8,128]{2,1,0:T(8,128)} %get-tuple-element.50), calls=%async_computation.3 | async-start | bytes 131072 | tf_op jit(solution)/shard_map/all_to_all | solution.py:463
  110.2 2.4 %shard_map.102 = f32[16,64,256]{2,1,0:T(8,128)} custom-call(f32[16,72,128]{2,1,0:T(8,128)S(1)} %all_to_all.21.got, f32[16,72,128]{2,1,0:T(8,128)S(1)} %collective-permute-done.12.other, f32[16,24,128]{2,1,0:T(8,128)} %get-tuple-element.36.mine, f32[32,128]{1,0:T(8,128)S(1)} %reshape.50.coef.coef_in), custom_call_target="tpu_custom_call" | custom-call | tf_op jit(solution)/shard_map/pallas_call | solution.py:556
  112.6 4.1 %all-to-all-done.3 = f32[16,8,128]{2,1,0:T(8,128)S(1)} async-done(((f32[16,8,128]{2,1,0:T(8,128)}), f32[16,8,128]{2,1,0:T(8,128)S(1)}, u32[]{:S(2)}, u32[]{:S(2)}) %all-to-all-start.3) | async-done | bytes 65568 | tf_op jit(solution)/shard_map/all_to_all | solution.py:463
  (48 shorter events, 5.1 us)
Async XLA Ops:
  0.6 11.1 %copy-start.6 = (f32[16]{0:T(128)S(1)}, f32[16]{0:T(128)}, u32[]{:S(2)}) copy-start(f32[16]{0:T(128)} %rate_in.1) | copy-start | bytes 196
  0.6 11.1 %copy-start.7 = (f32[16]{0:T(128)S(1)}, f32[16]{0:T(128)}, u32[]{:S(2)}) copy-start(f32[16]{0:T(128)} %w_in.1) | copy-start | bytes 196
  2.8 6.1 %copy-start.1 = (f32[64,256]{1,0:T(8,128)S(1)}, f32[64,256]{1,0:T(8,128)}, u32[]{:S(2)}) copy-start(f32[64,256]{1,0:T(8,128)} %get-tuple-element.28.u) | copy-start | bytes 196612
  2.9 6.1 %copy-start.2 = (f32[64,256]{1,0:T(8,128)S(1)}, f32[64,256]{1,0:T(8,128)}, u32[]{:S(2)}) copy-start(f32[64,256]{1,0:T(8,128)} %get-tuple-element.29.kap) | copy-start | bytes 196612
  2.9 6.1 %copy-start.3 = (f32[64,256]{1,0:T(8,128)S(1)}, f32[64,256]{1,0:T(8,128)}, u32[]{:S(2)}) copy-start(f32[64,256]{1,0:T(8,128)} %get-tuple-element.30.g0) | copy-start | bytes 196612
  2.9 10.7 %copy-start.4 = (f32[64,256]{1,0:T(8,128)S(1)}, f32[64,256]{1,0:T(8,128)}, u32[]{:S(2)}) copy-start(f32[64,256]{1,0:T(8,128)} %get-tuple-element.31.q1s) | copy-start | bytes 196612
  2.9 6.0 %collective-permute-start = (f32[40,256]{1,0:T(8,128)}, f32[40,256]{1,0:T(8,128)S(1)}, u32[]{:S(2)}, u32[]{:S(2)}) collective-permute-start(f32[40,256]{1,0:T(8,128)} %get-tuple-element.32), channel_id=1, source_target_pairs={{0,4},{4,8},{8,12},{12,0},{1,5},{5,9},{9,13},{13,1},{2,6},{6,10},{... | collective-permute-start | bytes 122888 | tf_op jit(solution)/shard_map/ppermute | solution.py:494
  5.1 3.8 %collective-permute-start.1 = (f32[40,256]{1,0:T(8,128)}, f32[40,256]{1,0:T(8,128)S(1)}, u32[]{:S(2)}, u32[]{:S(2)}) collective-permute-start(f32[40,256]{1,0:T(8,128)} %get-tuple-element.33), channel_id=1, source_target_pairs={{0,12},{4,0},{8,4},{12,8},{1,13},{5,1},{9,5},{13,9},{2,14},{6,2},{... | collective-permute-start | bytes 122888 | tf_op jit(solution)/shard_map/ppermute | solution.py:495
  6.7 23.9 %copy-start.5 = (f32[4,128,128]{2,1,0:T(8,128)S(1)}, f32[4,128,128]{2,1,0:T(8,128)}, u32[]{:S(2)}) copy-start(f32[4,128,128]{2,1,0:T(8,128)} %get-tuple-element.38) | copy-start | bytes 786436
  6.7 23.8 %collective-permute-start.4 = (f32[4,128,128]{2,1,0:T(8,128)}, f32[4,128,128]{2,1,0:T(8,128)S(1)}, u32[]{:S(2)}, u32[]{:S(2)}) collective-permute-start(f32[4,128,128]{2,1,0:T(8,128)} %get-tuple-element.39), channel_id=1, source_target_pairs={{0,64},{1,65},{2,66},{3,67},{4,68},{5,69},{6,70},{7,71},{8,72},{9,... | collective-permute-start | bytes 786440 | tf_op jit(solution)/shard_map/ppermute | solution.py:509
  7.5 23.0 %collective-permute-start.5 = (f32[4,128,128]{2,1,0:T(8,128)}, f32[4,128,128]{2,1,0:T(8,128)S(1)}, u32[]{:S(2)}, u32[]{:S(2)}) collective-permute-start(f32[4,128,128]{2,1,0:T(8,128)} %get-tuple-element.40), channel_id=1, source_target_pairs={{0,128},{1,129},{2,130},{3,131},{4,132},{5,133},{6,134},{7,135},{8... | collective-permute-start | bytes 786440 | tf_op jit(solution)/shard_map/ppermute | solution.py:509
  8.2 22.3 %collective-permute-start.6 = (f32[4,128,128]{2,1,0:T(8,128)}, f32[4,128,128]{2,1,0:T(8,128)S(1)}, u32[]{:S(2)}, u32[]{:S(2)}) collective-permute-start(f32[4,128,128]{2,1,0:T(8,128)} %get-tuple-element.41), channel_id=1, source_target_pairs={{0,192},{1,193},{2,194},{3,195},{4,196},{5,197},{6,198},{7,199},{8... | collective-permute-start | bytes 786440 | tf_op jit(solution)/shard_map/ppermute | solution.py:509
  9.0 4.6 %collective-permute-start.2 = (f32[80,256]{1,0:T(8,128)S(1)}, f32[80,256]{1,0:T(8,128)S(1)}, u32[]{:S(2)}, u32[]{:S(2)}) collective-permute-start(f32[80,256]{1,0:T(8,128)S(1)} %get-tuple-element.34), channel_id=1, source_target_pairs={{0,1},{1,2},{2,3},{3,0},{4,5},{5,6},{6,7},{7,4},{8,9},{9,10},{10,1... | collective-permute-start | bytes 245768 | tf_op jit(solution)/shard_map/ppermute | solution.py:507
  10.3 3.3 %collective-permute-start.3 = (f32[80,256]{1,0:T(8,128)S(1)}, f32[80,256]{1,0:T(8,128)S(1)}, u32[]{:S(2)}, u32[]{:S(2)}) collective-permute-start(f32[80,256]{1,0:T(8,128)S(1)} %get-tuple-element.35), channel_id=1, source_target_pairs={{0,3},{1,0},{2,1},{3,2},{4,7},{5,4},{6,5},{7,6},{8,11},{9,8},{10,9... | collective-permute-start | bytes 245768 | tf_op jit(solution)/shard_map/ppermute | solution.py:508
  15.6 25.3 %all-to-all-start = ((f32[16,24,128]{2,1,0:T(8,128)}), f32[16,24,128]{2,1,0:T(8,128)S(1)}, u32[]{:S(2)}, u32[]{:S(2)}) async-start(f32[16,24,128]{2,1,0:T(8,128)} %get-tuple-element.36.mine), calls=%async_computation | async-start | bytes 393216 | tf_op jit(solution)/shard_map/all_to_all | solution.py:463
  30.5 10.4 %copy-start = (f32[256,128]{1,0:T(8,128)S(1)}, f32[256,128]{1,0:T(8,128)}, u32[]{:S(2)}) copy-start(f32[256,128]{1,0:T(8,128)} %get-tuple-element.37.after.sk) | copy-start | bytes 393220
  30.7 3.0 %collective-permute-start.8 = (f32[128,128]{1,0:T(8,128)S(1)}, f32[128,128]{1,0:T(8,128)S(1)}, u32[]{:S(2)}, u32[]{:S(2)}) collective-permute-start(f32[128,128]{1,0:T(8,128)S(1)} %get-tuple-element.53), channel_id=1, source_target_pairs={{0,32},{64,96},{128,160},{192,224},{1,33},{65,97},{129,161},{193,2... | collective-permute-start | bytes 196616 | tf_op jit(solution)/shard_map/ppermute | solution.py:518
  31.3 2.3 %collective-permute-start.9 = (f32[128,128]{1,0:T(8,128)S(1)}, f32[128,128]{1,0:T(8,128)S(1)}, u32[]{:S(2)}, u32[]{:S(2)}) collective-permute-start(f32[128,128]{1,0:T(8,128)S(1)} %get-tuple-element.54), channel_id=1, source_target_pairs={{0,48},{64,112},{128,176},{192,240},{1,49},{65,113},{129,177},{193... | collective-permute-start | bytes 196616 | tf_op jit(solution)/shard_map/ppermute | solution.py:518
  32.0 5.9 %collective-permute-start.7 = (f32[128,128]{1,0:T(8,128)S(1)}, f32[128,128]{1,0:T(8,128)S(1)}, u32[]{:S(2)}, u32[]{:S(2)}) collective-permute-start(f32[128,128]{1,0:T(8,128)S(1)} %get-tuple-element.55), channel_id=1, source_target_pairs={{0,16},{64,80},{128,144},{192,208},{1,17},{65,81},{129,145},{193,2... | collective-permute-start | bytes 196616 | tf_op jit(solution)/shard_map/ppermute | solution.py:518
  65.9 7.2 %collective-permute-start.10 = (f32[135,8,128]{2,1,0:T(8,128)S(1)}, f32[135,8,128]{2,1,0:T(8,128)S(1)}, u32[]{:S(2)}, u32[]{:S(2)}) collective-permute-start(f32[135,8,128]{2,1,0:T(8,128)S(1)} %get-tuple-element.45), channel_id=1, source_target_pairs={{0,16},{16,32},{32,48},{48,64},{64,80},{80,96},{96,112},{112,128},... | collective-permute-start | bytes 1658888 | tf_op jit(solution)/shard_map/ppermute | solution.py:529
  66.6 9.2 %collective-permute-start.11 = (f32[135,8,128]{2,1,0:T(8,128)S(1)}, f32[135,8,128]{2,1,0:T(8,128)S(1)}, u32[]{:S(2)}, u32[]{:S(2)}) collective-permute-start(f32[135,8,128]{2,1,0:T(8,128)S(1)} %get-tuple-element.46), channel_id=1, source_target_pairs={{0,240},{16,0},{32,16},{48,32},{64,48},{80,64},{96,80},{112,96},{1... | collective-permute-start | bytes 1658888 | tf_op jit(solution)/shard_map/ppermute | solution.py:530
  105.7 4.5 %collective-permute-start.12 = (f32[16,72,128]{2,1,0:T(8,128)S(1)}, f32[16,72,128]{2,1,0:T(8,128)S(1)}, u32[]{:S(2)}, u32[]{:S(2)}) collective-permute-start(f32[16,72,128]{2,1,0:T(8,128)S(1)} %all_to_all.21.got), channel_id=1, source_target_pairs={{0,16},{16,0},{32,48},{48,32},{64,80},{80,64},{96,112},{112,96},{1... | collective-permute-start | bytes 1769480 | tf_op jit(solution)/shard_map/ppermute | solution.py:553
  106.7 10.0 %all-to-all-start.3 = ((f32[16,8,128]{2,1,0:T(8,128)}), f32[16,8,128]{2,1,0:T(8,128)S(1)}, u32[]{:S(2)}, u32[]{:S(2)}) async-start(f32[16,8,128]{2,1,0:T(8,128)} %get-tuple-element.50), calls=%async_computation.3 | async-start | bytes 131072 | tf_op jit(solution)/shard_map/all_to_all | solution.py:463

commit v4 on v3

--- a/solution.py
+++ b/solution.py
@@ -12,6 +12,8 @@
 SM = pl.BlockSpec(memory_space=pltpu.SMEM)
 ANY = pl.BlockSpec(memory_space=pl.ANY)
 MIB = 1024 * 1024
+LONG = pl.CostEstimate(flops=20_000_000_000, bytes_accessed=1_000_000, transcendentals=0)
+SLOTS = [0, 1, 2, 3, 0, 0, 4, 5, 6, 7, 8, 9, 12, 13, 14, 15, 11, 10]
 HALO = 15
 TRI = [HALO] + [HALO - j for j in range(1, HALO)]
 OFF = [sum(TRI[:j]) for j in range(HALO)]
@@ -22,7 +24,7 @@
 GROUP = 16
 
 
-def call(kernel, outs, ins, smem, scratch=(), limit=16):
+def call(kernel, outs, ins, smem, scratch=(), limit=16, cost=None):
     return pl.pallas_call(
         kernel,
         out_shape=[jax.ShapeDtypeStruct(shape, F32) for shape in outs],
@@ -30,6 +32,7 @@
         out_specs=[VM] * len(outs),
         scratch_shapes=[pltpu.VMEM(shape, F32) for shape in scratch],
         compiler_params=pltpu.CompilerParams(vmem_limit_bytes=limit * MIB),
+        cost_estimate=cost,
     )
 
 
@@ -75,7 +78,7 @@
     sk[...] = jnp.concatenate([s[...], kap[...]], axis=0).T
 
 
-def scatter_kernel(after, modes_in, out0, out1, out2, out3, modes, packed, sems):
+def scatter_kernel(after, modes_in, out0, out1, out2, modes, packed, sems):
     @pl.when(lax.axis_index("tm") == 0)
     def _():
         copies = [
@@ -88,10 +91,12 @@
             copy.wait()
         for m in range(8):
             both = jnp.concatenate([modes[m], modes[m + 8]], axis=0).T
-            packed[:, 16 * m : 16 * m + 16] = both.reshape(16, 16, 128)
+            pieces = both.reshape(16, 16, 128)
+            for place, slot in enumerate(SLOTS):
+                packed[place, 16 * m : 16 * m + 16] = pieces[slot]
         copies = [
-            pltpu.make_async_copy(packed.at[pl.ds(4 * i, 4)], out, sems.at[4 + i])
-            for i, out in enumerate((out0, out1, out2, out3))
+            pltpu.make_async_copy(packed.at[pl.ds(6 * i, 6)], out, sems.at[4 + i])
+            for i, out in enumerate((out0, out1, out2))
         ]
         for copy in copies:
             copy.start()
@@ -495,29 +500,30 @@
     xhi = lax.ppermute(dn, "gx", ring("gx", -1))
     chunks = pl.pallas_call(
         scatter_kernel,
-        out_shape=[jax.ShapeDtypeStruct((4, 128, 128), F32)] * 4,
+        out_shape=[jax.ShapeDtypeStruct((6, 128, 128), F32)] * 3,
         in_specs=[ANY, ANY],
-        out_specs=[ANY] * 4,
-        scratch_shapes=[pltpu.VMEM((16, 64, 256), F32), pltpu.VMEM((16, 128, 128), F32)]
-        + [pltpu.SemaphoreType.DMA((8,))],
+        out_specs=[ANY] * 3,
+        scratch_shapes=[pltpu.VMEM((16, 64, 256), F32), pltpu.VMEM((18, 128, 128), F32)]
+        + [pltpu.SemaphoreType.DMA((7,))],
         compiler_params=pltpu.CompilerParams(vmem_limit_bytes=60 * MIB),
     )(sk, h)
 
     yup, ydn = call(side_kernel, [(80, 256)] * 2, 5, 0)(u, kap, g0, xlo, xhi)
     ylo = lax.ppermute(yup, "gy", ring("gy", 1))
     yhi = lax.ppermute(ydn, "gy", ring("gy", -1))
-    far = [lax.ppermute(chunks[k], "tm", [(0, 4 * k)]) for k in (1, 2, 3)]
+    far = [lax.ppermute(chunks[k], "tm", [(0, hub)]) for k, hub in ((1, 4), (2, 12))]
 
     fine, both = call(
-        fine_kernel, [plane, (16, 24, 128)], 9, 1, [(12, 24, 256)] * 4
+        fine_kernel, [plane, (16, 24, 128)], 9, 1, [(12, 24, 256)] * 4, 16, LONG
     )(omega, u, kap, g0, q1s, xlo, xhi, ylo, yhi)
     parts = swap(both, "tm")
 
-    quarter = jnp.where(t == 0, chunks[0], far[0] + far[1] + far[2])
-    close = [
-        lax.ppermute(quarter[k], "tm", [(4 * a, 4 * a + k) for a in range(4)]) for k in (1, 2, 3)
-    ]
-    start = jnp.where(t % 4 == 0, quarter[0], close[0] + close[1] + close[2])
+    share = jnp.where(t == 0, chunks[0], far[0] + far[1])
+    pairs = [[(0, k), (4, 4 + k), (12, 12 + k)] for k in (1, 2, 3)]
+    pairs += [[(4, 8), (12, 11)], [(4, 9), (12, 10)]]
+    close = [lax.ppermute(share[k + 1], "tm", pair) for k, pair in enumerate(pairs)]
+    hub = (t == 0) | (t == 4) | (t == 12)
+    start = jnp.where(hub, share[0], sum(close))
 
     msg, known = call(known_kernel, [(16, 136, 128), (16, 16, 128)], 4, 0)(
         parts, sk, start, coef

time: 120 us -> 119 us (level)
  waiting for transfers between devices: 21.1 us -> 19.8 us
    all_to_all x2, starting transfers between devices: 18.4 us -> 16.8 us  [swap(): return lax.all_to_all(value, axis, 0, 0, tiled=True)]
    all_to_all x2, waiting for transfers between devices: 7.01 us -> 5.66 us  [swap(): return lax.all_to_all(value, axis, 0, 0, tiled=True)]
    ppermute x6 -> x7, starting transfers between devices: 4.79 us -> 5.32 us  [the longest x5 3.95 us: per_device(): lax.ppermute(share[k + 1], 'tm', pair)]
    ppermute x6 -> x7, waiting for transfers between devices: 4.33 us -> 4.31 us  [the longest x5 4.3 us: per_device(): lax.ppermute(share[k + 1], 'tm', pair)]
  transfers between devices with their start and end apart: 15 -> 16, of which waited for: 6 -> 7; matrix products, arithmetic and copies ran while one was open for 1% -> 1% of each run, Pallas kernels for 4% -> 5%
where the time goes in v4:
time: 119 us; the launch traced here: 118 us
  blocking collectives  48.4 us (41%)
  starting transfers between devices  29.8 us (25%)
  waiting for transfers between devices  19.8 us (17%)
  Pallas kernels  15.2 us (13%)
  between operations  2.72 us (2%)
  other arithmetic  1.44 us (1%)
    all_to_all x2, blocking collectives, swap(): return lax.all_to_all(value, axis, 0, 0, tiled=True)  48.4 us
    all_to_all x2, starting transfers between devices, swap(): return lax.all_to_all(value, axis, 0, 0, tiled=True)  16.8 us
    ppermute x1, waiting for transfers between devices, per_device(): lo = lax.ppermute(up, 'tm', ring('tm', 1))  6.1 us
    pallas_call x1, Pallas kernels, per_device(): pl.pallas_call(sweep_kernel, out_shape=jax.ShapeDtypeStruct((16, 72, 128)...  5.79 us
    all_to_all x2, waiting for transfers between devices, swap(): return lax.all_to_all(value, axis, 0, 0, tiled=True)  5.66 us
    ppermute x5, waiting for transfers between devices, per_device(): lax.ppermute(share[k + 1], 'tm', pair)  4.3 us
    ppermute x5, starting transfers between devices, per_device(): lax.ppermute(share[k + 1], 'tm', pair)  3.95 us
    ppermute x1, waiting for transfers between devices, per_device(): hi = lax.ppermute(dn, 'tm', ring('tm', -1))  2.77 us
  transfers between devices with their start and end apart: 16, of which 7 were waited for; matrix products, arithmetic and copies ran while one was open for 1% of the time, Pallas kernels for 5%

profile of v4, /device:TPU:1, one launch (start us, length us, event | category | flops | bytes accessed | tf_op | source)
XLA Modules:
  0.0 118.1 jit_solution(10948868961351127730)
XLA Ops:
  0.7 2.2 %shard_map.94 = (f32[64,256]{1,0:T(8,128)}, f32[64,256]{1,0:T(8,128)}, f32[64,256]{1,0:T(8,128)}, f32[64,256]{1,0:T(8,128)}, f32[40,256]{1,0:T(8,128)}, /*index=5*/f32[40,256]{1,0:T(8,128)}, f32[256,128]{1,0:T(8,128)}) custom-call(f32[8]{0:T(128)} %rk_in.1, f32[16]{0:T(128)} %w_in.1, f32[16]{0:T(128)} %rate_in.1, f32[64,256]{1,0:T(8,128)} %bitcast.29, ...), custom_call_target="tpu_custom_call" | custom-call | tf_op jit(solution)/shard_map/pallas_call | solution.py:489
  2.9 2.2 %collective-permute-start = (f32[40,256]{1,0:T(8,128)}, f32[40,256]{1,0:T(8,128)S(1)}, u32[]{:S(2)}, u32[]{:S(2)}) collective-permute-start(f32[40,256]{1,0:T(8,128)} %get-tuple-element.31), channel_id=1, source_target_pairs={{0,4},{4,8},{8,12},{12,0},{1,5},{5,9},{9,13},{13,1},{2,6},{6,10},{... | collective-permute-start | bytes 122888 | tf_op jit(solution)/shard_map/ppermute | solution.py:499
  5.1 1.5 %collective-permute-start.1 = (f32[40,256]{1,0:T(8,128)}, f32[40,256]{1,0:T(8,128)S(1)}, u32[]{:S(2)}, u32[]{:S(2)}) collective-permute-start(f32[40,256]{1,0:T(8,128)} %get-tuple-element.32), channel_id=1, source_target_pairs={{0,12},{4,0},{8,4},{12,8},{1,13},{5,1},{9,5},{13,9},{2,14},{6,2},{... | collective-permute-start | bytes 122888 | tf_op jit(solution)/shard_map/ppermute | solution.py:500
  6.7 0.7 collective-permute-start.4
  7.4 0.7 collective-permute-start.5
  8.2 1.3 %collective-permute-start.2 = (f32[80,256]{1,0:T(8,128)S(1)}, f32[80,256]{1,0:T(8,128)S(1)}, u32[]{:S(2)}, u32[]{:S(2)}) collective-permute-start(f32[80,256]{1,0:T(8,128)S(1)} %get-tuple-element.33), channel_id=1, source_target_pairs={{0,1},{1,2},{2,3},{3,0},{4,5},{5,6},{6,7},{7,4},{8,9},{9,10},{10,1... | collective-permute-start | bytes 245768 | tf_op jit(solution)/shard_map/ppermute | solution.py:512
  9.5 1.5 %collective-permute-start.3 = (f32[80,256]{1,0:T(8,128)S(1)}, f32[80,256]{1,0:T(8,128)S(1)}, u32[]{:S(2)}, u32[]{:S(2)}) collective-permute-start(f32[80,256]{1,0:T(8,128)S(1)} %get-tuple-element.34), channel_id=1, source_target_pairs={{0,3},{1,0},{2,1},{3,2},{4,7},{5,4},{6,5},{7,6},{8,11},{9,8},{10,9... | collective-permute-start | bytes 245768 | tf_op jit(solution)/shard_map/ppermute | solution.py:513
  11.9 0.9 collective-permute-done.2.ylo
  12.8 2.1 %shard_map.96 = (f32[64,256]{1,0:T(8,128)S(1)}, f32[16,24,128]{2,1,0:T(8,128)}) custom-call(f32[1]{0:T(128)} %bitcast.omega, f32[64,256]{1,0:T(8,128)S(1)} %copy-done.1, f32[64,256]{1,0:T(8,128)S(1)} %copy-done.2, f32[64,256]{1,0:T(8,128)S(1)} %copy-done.3, f32[64,256]{1,0:T(8,128)S(1)} %copy-done.4, f32[40,256]{1,0:T(8,128)S(1)} %collective-permute-done.xlo, ...), custom_call_target="tpu_custom_call" | custom-call | flops 20000000000 | bytes 1000000 | tf_op jit(solution)/shard_map/pallas_call | solution.py:516
  14.9 13.3 %all-to-all-start = ((f32[16,24,128]{2,1,0:T(8,128)}), f32[16,24,128]{2,1,0:T(8,128)S(1)}, u32[]{:S(2)}, u32[]{:S(2)}) async-start(f32[16,24,128]{2,1,0:T(8,128)} %get-tuple-element.35.mine), calls=%async_computation | async-start | bytes 393216 | tf_op jit(solution)/shard_map/all_to_all | solution.py:468
  31.1 1.3 %collective-permute-start.6 = (f32[128,128]{1,0:T(8,128)S(1)}, f32[128,128]{1,0:T(8,128)S(1)}, u32[]{:S(2)}, u32[]{:S(2)}) collective-permute-start(f32[128,128]{1,0:T(8,128)S(1)} %get-tuple-element.55), channel_id=1, source_target_pairs={{0,16},{64,80},{192,208},{1,17},{65,81},{193,209},{2,18},{66,82},{... | collective-permute-start | bytes 196616 | tf_op jit(solution)/shard_map/ppermute | solution.py:524
  32.7 4.3 %collective-permute-done.6 = f32[128,128]{1,0:T(8,128)S(1)} collective-permute-done((f32[128,128]{1,0:T(8,128)S(1)}, f32[128,128]{1,0:T(8,128)S(1)}, u32[]{:S(2)}, u32[]{:S(2)}) %collective-permute-start.6) | collective-permute-done | bytes 65568 | tf_op jit(solution)/shard_map/ppermute | solution.py:524
  37.0 1.6 %all-to-all-done.parts.parts_in = f32[16,24,128]{2,1,0:T(8,128)S(1)} async-done(((f32[16,24,128]{2,1,0:T(8,128)}), f32[16,24,128]{2,1,0:T(8,128)S(1)}, u32[]{:S(2)}, u32[]{:S(2)}) %all-to-all-start) | async-done | bytes 196640 | tf_op jit(solution)/shard_map/all_to_all | solution.py:468
  38.6 1.4 %shard_map.98 = (f32[16,136,128]{2,1,0:T(8,128)S(1)}, f32[16,16,128]{2,1,0:T(8,128)S(1)}) custom-call(f32[16,24,128]{2,1,0:T(8,128)S(1)} %all-to-all-done.parts.parts_in, f32[256,128]{1,0:T(8,128)S(1)} %copy-done, f32[128,128]{1,0:T(8,128)S(1)} %fusion.start.start_in, f32[32,128]{1,0:T(8,128)S(1)} %reshape.50.coef.coef_in), custom_call_target="tpu_custom_call" | custom-call | tf_op jit(solution)/shard_map/pallas_call | solution.py:528
  40.0 23.1 %all_to_all.20 = f32[16,136,128]{2,1,0:T(8,128)S(1)} all-to-all(f32[16,136,128]{2,1,0:T(8,128)S(1)} %get-tuple-element.40), channel_id=1, replica_groups=mesh['tm'=16,'gx'=4,'gy'=4] {'gy','gx'}, dimensions={0} | all-to-all | bytes 2228224 | tf_op jit(solution)/shard_map/all_to_all | solution.py:468
  63.6 0.8 collective-permute-start.11
  64.7 6.1 %collective-permute-done.11.lo = f32[135,8,128]{2,1,0:T(8,128)S(1)} collective-permute-done((f32[135,8,128]{2,1,0:T(8,128)S(1)}, f32[135,8,128]{2,1,0:T(8,128)S(1)}, u32[]{:S(2)}, u32[]{:S(2)}) %collective-permute-start.11) | collective-permute-done | bytes 552992 | tf_op jit(solution)/shard_map/ppermute | solution.py:535
  70.8 2.8 %collective-permute-done.12.hi = f32[135,8,128]{2,1,0:T(8,128)S(1)} collective-permute-done((f32[135,8,128]{2,1,0:T(8,128)S(1)}, f32[135,8,128]{2,1,0:T(8,128)S(1)}, u32[]{:S(2)}, u32[]{:S(2)}) %collective-permute-start.12) | collective-permute-done | bytes 552992 | tf_op jit(solution)/shard_map/ppermute | solution.py:536
  73.6 5.8 %shard_map.100 = f32[16,72,128]{2,1,0:T(8,128)S(1)} custom-call(f32[16]{0:T(128)S(1)} %broadcast_multiply_fusion.beta, f32[16,16,8,128]{3,2,1,0:T(8,128)S(1)} %get-tuple-element.41.own, f32[16,8,128]{2,1,0:T(8,128)S(1)} %get-tuple-element.42.kown, f32[135,8,128]{2,1,0:T(8,128)S(1)} %collective-permute-done.11.lo, ...), custom_call_target="tpu_custom_call" | custom-call | tf_op jit(solution)/shard_map/pallas_call | solution.py:537
  79.4 25.3 %all_to_all.21.got = f32[16,72,128]{2,1,0:T(8,128)S(1)} all-to-all(f32[16,72,128]{2,1,0:T(8,128)S(1)} %shard_map.100), channel_id=1, replica_groups=mesh['tm'=16,'gx'=4,'gy'=4] {'tm'}, dimensions={0} | all-to-all | bytes 1179648 | tf_op jit(solution)/shard_map/all_to_all | solution.py:468
  104.9 0.8 shard_map.101
  105.7 3.5 %all-to-all-start.3 = ((f32[16,8,128]{2,1,0:T(8,128)}), f32[16,8,128]{2,1,0:T(8,128)S(1)}, u32[]{:S(2)}, u32[]{:S(2)}) async-start(f32[16,8,128]{2,1,0:T(8,128)} %get-tuple-element.48), calls=%async_computation.3 | async-start | bytes 131072 | tf_op jit(solution)/shard_map/all_to_all | solution.py:468
  109.2 2.4 %shard_map.102 = f32[16,64,256]{2,1,0:T(8,128)} custom-call(f32[16,72,128]{2,1,0:T(8,128)S(1)} %all_to_all.21.got, f32[16,72,128]{2,1,0:T(8,128)S(1)} %collective-permute-done.13.other, f32[16,24,128]{2,1,0:T(8,128)} %get-tuple-element.35.mine, f32[32,128]{1,0:T(8,128)S(1)} %reshape.50.coef.coef_in), custom_call_target="tpu_custom_call" | custom-call | tf_op jit(solution)/shard_map/pallas_call | solution.py:562
  111.6 4.1 %all-to-all-done.3 = f32[16,8,128]{2,1,0:T(8,128)S(1)} async-done(((f32[16,8,128]{2,1,0:T(8,128)}), f32[16,8,128]{2,1,0:T(8,128)S(1)}, u32[]{:S(2)}, u32[]{:S(2)}) %all-to-all-start.3) | async-done | bytes 65568 | tf_op jit(solution)/shard_map/all_to_all | solution.py:468
  (50 shorter events, 5.8 us)
Async XLA Ops:
  0.6 10.4 %copy-start.6 = (f32[16]{0:T(128)S(1)}, f32[16]{0:T(128)}, u32[]{:S(2)}) copy-start(f32[16]{0:T(128)} %rate_in.1) | copy-start | bytes 196
  0.6 10.4 %copy-start.7 = (f32[16]{0:T(128)S(1)}, f32[16]{0:T(128)}, u32[]{:S(2)}) copy-start(f32[16]{0:T(128)} %w_in.1) | copy-start | bytes 196
  2.8 5.3 %copy-start.1 = (f32[64,256]{1,0:T(8,128)S(1)}, f32[64,256]{1,0:T(8,128)}, u32[]{:S(2)}) copy-start(f32[64,256]{1,0:T(8,128)} %get-tuple-element.27.u) | copy-start | bytes 196612
  2.9 5.3 %copy-start.2 = (f32[64,256]{1,0:T(8,128)S(1)}, f32[64,256]{1,0:T(8,128)}, u32[]{:S(2)}) copy-start(f32[64,256]{1,0:T(8,128)} %get-tuple-element.28.kap) | copy-start | bytes 196612
  2.9 5.3 %copy-start.3 = (f32[64,256]{1,0:T(8,128)S(1)}, f32[64,256]{1,0:T(8,128)}, u32[]{:S(2)}) copy-start(f32[64,256]{1,0:T(8,128)} %get-tuple-element.29.g0) | copy-start | bytes 196612
  2.9 9.9 %copy-start.4 = (f32[64,256]{1,0:T(8,128)S(1)}, f32[64,256]{1,0:T(8,128)}, u32[]{:S(2)}) copy-start(f32[64,256]{1,0:T(8,128)} %get-tuple-element.30.q1s) | copy-start | bytes 196612
  2.9 5.2 %collective-permute-start = (f32[40,256]{1,0:T(8,128)}, f32[40,256]{1,0:T(8,128)S(1)}, u32[]{:S(2)}, u32[]{:S(2)}) collective-permute-start(f32[40,256]{1,0:T(8,128)} %get-tuple-element.31), channel_id=1, source_target_pairs={{0,4},{4,8},{8,12},{12,0},{1,5},{5,9},{9,13},{13,1},{2,6},{6,10},{... | collective-permute-start | bytes 122888 | tf_op jit(solution)/shard_map/ppermute | solution.py:499
  5.1 3.1 %collective-permute-start.1 = (f32[40,256]{1,0:T(8,128)}, f32[40,256]{1,0:T(8,128)S(1)}, u32[]{:S(2)}, u32[]{:S(2)}) collective-permute-start(f32[40,256]{1,0:T(8,128)} %get-tuple-element.32), channel_id=1, source_target_pairs={{0,12},{4,0},{8,4},{12,8},{1,13},{5,1},{9,5},{13,9},{2,14},{6,2},{... | collective-permute-start | bytes 122888 | tf_op jit(solution)/shard_map/ppermute | solution.py:500
  6.7 21.6 %collective-permute-start.4 = (f32[6,128,128]{2,1,0:T(8,128)}, f32[6,128,128]{2,1,0:T(8,128)S(1)}, u32[]{:S(2)}, u32[]{:S(2)}) collective-permute-start(f32[6,128,128]{2,1,0:T(8,128)} %get-tuple-element.38), channel_id=1, source_target_pairs={{0,64},{1,65},{2,66},{3,67},{4,68},{5,69},{6,70},{7,71},{8,72},{9,... | collective-permute-start | bytes 1179656 | tf_op jit(solution)/shard_map/ppermute | solution.py:514
  7.4 20.9 %collective-permute-start.5 = (f32[6,128,128]{2,1,0:T(8,128)}, f32[6,128,128]{2,1,0:T(8,128)S(1)}, u32[]{:S(2)}, u32[]{:S(2)}) collective-permute-start(f32[6,128,128]{2,1,0:T(8,128)} %get-tuple-element.39), channel_id=1, source_target_pairs={{0,192},{1,193},{2,194},{3,195},{4,196},{5,197},{6,198},{7,199},{8... | collective-permute-start | bytes 1179656 | tf_op jit(solution)/shard_map/ppermute | solution.py:514
  8.2 4.6 %collective-permute-start.2 = (f32[80,256]{1,0:T(8,128)S(1)}, f32[80,256]{1,0:T(8,128)S(1)}, u32[]{:S(2)}, u32[]{:S(2)}) collective-permute-start(f32[80,256]{1,0:T(8,128)S(1)} %get-tuple-element.33), channel_id=1, source_target_pairs={{0,1},{1,2},{2,3},{3,0},{4,5},{5,6},{6,7},{7,4},{8,9},{9,10},{10,1... | collective-permute-start | bytes 245768 | tf_op jit(solution)/shard_map/ppermute | solution.py:512
  9.5 3.3 %collective-permute-start.3 = (f32[80,256]{1,0:T(8,128)S(1)}, f32[80,256]{1,0:T(8,128)S(1)}, u32[]{:S(2)}, u32[]{:S(2)}) collective-permute-start(f32[80,256]{1,0:T(8,128)S(1)} %get-tuple-element.34), channel_id=1, source_target_pairs={{0,3},{1,0},{2,1},{3,2},{4,7},{5,4},{6,5},{7,6},{8,11},{9,8},{10,9... | collective-permute-start | bytes 245768 | tf_op jit(solution)/shard_map/ppermute | solution.py:513
  12.8 15.5 %copy-start.5 = (f32[6,128,128]{2,1,0:T(8,128)S(1)}, f32[6,128,128]{2,1,0:T(8,128)}, u32[]{:S(2)}) copy-start(f32[6,128,128]{2,1,0:T(8,128)} %get-tuple-element.37) | copy-start | bytes 1179652
  14.9 23.7 %all-to-all-start = ((f32[16,24,128]{2,1,0:T(8,128)}), f32[16,24,128]{2,1,0:T(8,128)S(1)}, u32[]{:S(2)}, u32[]{:S(2)}) async-start(f32[16,24,128]{2,1,0:T(8,128)} %get-tuple-element.35.mine), calls=%async_computation | async-start | bytes 393216 | tf_op jit(solution)/shard_map/all_to_all | solution.py:468
  28.3 10.4 %copy-start = (f32[256,128]{1,0:T(8,128)S(1)}, f32[256,128]{1,0:T(8,128)}, u32[]{:S(2)}) copy-start(f32[256,128]{1,0:T(8,128)} %get-tuple-element.36.after.sk) | copy-start | bytes 393220
  28.4 4.3 %collective-permute-start.7 = (f32[128,128]{1,0:T(8,128)S(1)}, f32[128,128]{1,0:T(8,128)S(1)}, u32[]{:S(2)}, u32[]{:S(2)}) collective-permute-start(f32[128,128]{1,0:T(8,128)S(1)} %get-tuple-element.51), channel_id=1, source_target_pairs={{0,32},{64,96},{192,224},{1,33},{65,97},{193,225},{2,34},{66,98},{... | collective-permute-start | bytes 196616 | tf_op jit(solution)/shard_map/ppermute | solution.py:524
  29.1 3.6 %collective-permute-start.10 = (f32[128,128]{1,0:T(8,128)S(1)}, f32[128,128]{1,0:T(8,128)S(1)}, u32[]{:S(2)}, u32[]{:S(2)}) collective-permute-start(f32[128,128]{1,0:T(8,128)S(1)} %get-tuple-element.52), channel_id=1, source_target_pairs={{64,144},{192,160},{65,145},{193,161},{66,146},{194,162},{67,147},... | collective-permute-start | bytes 196616 | tf_op jit(solution)/shard_map/ppermute | solution.py:524
  29.7 3.0 %collective-permute-start.9 = (f32[128,128]{1,0:T(8,128)S(1)}, f32[128,128]{1,0:T(8,128)S(1)}, u32[]{:S(2)}, u32[]{:S(2)}) collective-permute-start(f32[128,128]{1,0:T(8,128)S(1)} %get-tuple-element.53), channel_id=1, source_target_pairs={{64,128},{192,176},{65,129},{193,177},{66,130},{194,178},{67,131},... | collective-permute-start | bytes 196616 | tf_op jit(solution)/shard_map/ppermute | solution.py:524
  30.4 2.3 %collective-permute-start.8 = (f32[128,128]{1,0:T(8,128)S(1)}, f32[128,128]{1,0:T(8,128)S(1)}, u32[]{:S(2)}, u32[]{:S(2)}) collective-permute-start(f32[128,128]{1,0:T(8,128)S(1)} %get-tuple-element.54), channel_id=1, source_target_pairs={{0,48},{64,112},{192,240},{1,49},{65,113},{193,241},{2,50},{66,114... | collective-permute-start | bytes 196616 | tf_op jit(solution)/shard_map/ppermute | solution.py:524
  31.1 5.9 %collective-permute-start.6 = (f32[128,128]{1,0:T(8,128)S(1)}, f32[128,128]{1,0:T(8,128)S(1)}, u32[]{:S(2)}, u32[]{:S(2)}) collective-permute-start(f32[128,128]{1,0:T(8,128)S(1)} %get-tuple-element.55), channel_id=1, source_target_pairs={{0,16},{64,80},{192,208},{1,17},{65,81},{193,209},{2,18},{66,82},{... | collective-permute-start | bytes 196616 | tf_op jit(solution)/shard_map/ppermute | solution.py:524
  63.6 7.2 %collective-permute-start.11 = (f32[135,8,128]{2,1,0:T(8,128)S(1)}, f32[135,8,128]{2,1,0:T(8,128)S(1)}, u32[]{:S(2)}, u32[]{:S(2)}) collective-permute-start(f32[135,8,128]{2,1,0:T(8,128)S(1)} %get-tuple-element.43), channel_id=1, source_target_pairs={{0,16},{16,32},{32,48},{48,64},{64,80},{80,96},{96,112},{112,128},... | collective-permute-start | bytes 1658888 | tf_op jit(solution)/shard_map/ppermute | solution.py:535
  64.4 9.2 %collective-permute-start.12 = (f32[135,8,128]{2,1,0:T(8,128)S(1)}, f32[135,8,128]{2,1,0:T(8,128)S(1)}, u32[]{:S(2)}, u32[]{:S(2)}) collective-permute-start(f32[135,8,128]{2,1,0:T(8,128)S(1)} %get-tuple-element.44), channel_id=1, source_target_pairs={{0,240},{16,0},{32,16},{48,32},{64,48},{80,64},{96,80},{112,96},{1... | collective-permute-start | bytes 1658888 | tf_op jit(solution)/shard_map/ppermute | solution.py:536
  104.7 4.5 %collective-permute-start.13 = (f32[16,72,128]{2,1,0:T(8,128)S(1)}, f32[16,72,128]{2,1,0:T(8,128)S(1)}, u32[]{:S(2)}, u32[]{:S(2)}) collective-permute-start(f32[16,72,128]{2,1,0:T(8,128)S(1)} %all_to_all.21.got), channel_id=1, source_target_pairs={{0,16},{16,0},{32,48},{48,32},{64,80},{80,64},{96,112},{112,96},{1... | collective-permute-start | bytes 1769480 | tf_op jit(solution)/shard_map/ppermute | solution.py:559
  105.7 10.0 %all-to-all-start.3 = ((f32[16,8,128]{2,1,0:T(8,128)}), f32[16,8,128]{2,1,0:T(8,128)S(1)}, u32[]{:S(2)}, u32[]{:S(2)}) async-start(f32[16,8,128]{2,1,0:T(8,128)} %get-tuple-element.48), calls=%async_computation.3 | async-start | bytes 131072 | tf_op jit(solution)/shard_map/all_to_all | solution.py:468

commit v5 on v4

--- a/solution.py
+++ b/solution.py
@@ -122,7 +122,7 @@
                 out[at_row : at_row + 1] = src[8 * x + y : 8 * x + y + 1]
 
 
-def fine_kernel(omega, u, kap, g0, q1s, xlo, xhi, ylo, yhi, fine, both, up, kp, gp, u1):
+def fine_kernel(omega, u, kap, g0, q1s, xlo, xhi, ylo, yhi, both, up, kp, gp, u1):
     gx, gy = lax.axis_index("gx"), lax.axis_index("gy")
     zero = jnp.zeros((24, 256), F32)
     for ref in (up, kp, gp):
@@ -211,7 +211,6 @@
         c1 = gp[2 + x, 8:16]
         lap = laplace(u1, 2 + x)[8:16]
         c2 = (0.5 * STEP) * (lap + q1s[rows] - omega[0] * c1)
-        fine[rows] = u1[2 + x, 8:16] + c2
         first.append(c1)
         second.append(c2)
     both[:, 0:16] = jnp.concatenate(first + second, axis=0).T.reshape(16, 16, 128)
@@ -242,6 +241,7 @@
     seen = []
     for j in range(16):
         c1, c2 = doubled(parts[j, 0:16], low)
+        msg[j, 136:144] = packed_rows(unpacked(parts[j, 16:24]) + c1 + c2)
         if j == 0:
             n = 2.0 * c1
             seen.append(unpacked(parts[0, 16:24]) + c1 + c2)
@@ -265,12 +265,12 @@
         msg[p, 128:136] = last
 
 
-def gather_kernel(got, own, kap, up, dn):
+def gather_kernel(got, own, kap, fine, up, dn):
     low = lane_low((8, 128))
 
     def pair(row):
-        even = got[pl.ds(row, 8, stride=272), :]
-        odd = got[pl.ds(row + 136, 8, stride=272), :]
+        even = got[pl.ds(row, 8, stride=288), :]
+        odd = got[pl.ds(row + 144, 8, stride=288), :]
         left = jnp.where(low, even, pltpu.roll(odd, 64, 1))
         right = jnp.where(low, pltpu.roll(even, 64, 1), odd)
         return left, right
@@ -289,6 +289,7 @@
             place(j, z, left)
             place(j + 8, z, right)
     for z in range(8):
+        fine[z], fine[z + 8] = pair(136 + z)
         left, right = pair(128 + z)
         for at, v in ((z, left), (z + 8, right)):
             kap[at] = v
@@ -298,7 +299,7 @@
                 up[KOFF + at - 1] = v
 
 
-def sweep_kernel(beta, own, kown, lo, hi, parts_in, known_in, start_in, coef_in, out,
+def sweep_kernel(beta, own, kown, fown, lo, hi, parts_in, known_in, start_in, coef_in, out,
                  e, g, c, kw, parts, known, start, coef, sems):
     pairs = ((parts_in, parts), (known_in, known), (start_in, start), (coef_in, coef))
     copies = [pltpu.make_async_copy(a, b, sems.at[i]) for i, (a, b) in enumerate(pairs)]
@@ -412,22 +413,23 @@
                 at_row = 16 * (m % 4)
                 out[j + m // 4, at_row : at_row + 16] = h[m]
         out[j, 64:72] = packed_rows(block_of(e_rows, j))
+    diff = e[p, HALO:31] - fown[...]
+    part = jnp.sum(diff * diff, axis=0)
+    for j in range(16):
+        out[j, 72:80] = part
 
 
 def rows_of(ref):
     return jnp.concatenate([unpacked(ref[t, 64:72]) for t in range(16)], axis=0)
 
 
-def field_kernel(got, fine, field, part):
-    now = rows_of(got).T[0:64]
-    field[...] = now
-    diff = now - fine[...]
-    diff = diff * diff
-    total = jnp.zeros((8, 128), F32)
-    for x in range(8):
-        total += diff[8 * x : 8 * x + 8, 0:128] + diff[8 * x : 8 * x + 8, 128:256]
-    for p in range(16):
-        part[p] = total
+def field_kernel(got, field, size):
+    field[...] = rows_of(got).T[0:64]
+    part = got[0, 72:80]
+    for t in range(1, 16):
+        part += got[t, 72:80]
+    whole = jnp.sum(jnp.sum(part, axis=1, keepdims=True), axis=0, keepdims=True)
+    size[0] = jnp.sqrt(whole / 262144.0)[0, 0]
 
 
 def final_kernel(got, other, mine, coef, modes):
@@ -462,6 +464,21 @@
 def ring(axis, step):
     n = lax.axis_size(axis)
     return [(i, (i + step) % n) for i in range(n)]
+
+
+def turned():
+    def apart(a, b, n):
+        return min((a - b) % n, (b - a) % n)
+
+    def device(t, p):
+        return 16 * t + p % 4 * 4 + p // 4
+
+    pairs = []
+    for j in range(16):
+        far = sorted(range(16), key=lambda p: -apart(p % 4, j % 4, 4) - apart(p // 4, j // 4, 4))
+        near = sorted(range(16), key=lambda t: apart(t // 2, j // 2, 8))
+        pairs += [(device(t, j), device(j, p)) for t, p in zip(near, far)]
+    return pairs
 
 
 def swap(value, axis):
@@ -513,8 +530,8 @@
     yhi = lax.ppermute(ydn, "gy", ring("gy", -1))
     far = [lax.ppermute(chunks[k], "tm", [(0, hub)]) for k, hub in ((1, 4), (2, 12))]
 
-    fine, both = call(
-        fine_kernel, [plane, (16, 24, 128)], 9, 1, [(12, 24, 256)] * 4, 16, LONG
+    (both,) = call(
+        fine_kernel, [(16, 24, 128)], 9, 1, [(12, 24, 256)] * 4, 16, LONG
     )(omega, u, kap, g0, q1s, xlo, xhi, ylo, yhi)
     parts = swap(both, "tm")
 
@@ -525,19 +542,22 @@
     hub = (t == 0) | (t == 4) | (t == 12)
     start = jnp.where(hub, share[0], sum(close))
 
-    msg, known = call(known_kernel, [(16, 136, 128), (16, 16, 128)], 4, 0)(
+    msg, known = call(known_kernel, [(16, 144, 128), (16, 16, 128)], 4, 0)(
         parts, sk, start, coef
     )
     got = swap(msg, ("gy", "gx"))
-    own, kown, up, dn = call(
-        gather_kernel, [(16, 16, 8, 128), (16, 8, 128), (MSG, 8, 128), (MSG, 8, 128)], 1, 0
-    )(got.reshape(16 * 136, 128))
+    own, kown, fown, up, dn = call(
+        gather_kernel,
+        [(16, 16, 8, 128), (16, 8, 128), (16, 8, 128), (MSG, 8, 128), (MSG, 8, 128)],
+        1,
+        0,
+    )(got.reshape(16 * 144, 128))
     lo = lax.ppermute(up, "tm", ring("tm", 1))
     hi = lax.ppermute(dn, "tm", ring("tm", -1))
     out = pl.pallas_call(
         sweep_kernel,
-        out_shape=jax.ShapeDtypeStruct((16, 72, 128), F32),
-        in_specs=[SM] + [VM] * 4 + [ANY] * 4,
+        out_shape=jax.ShapeDtypeStruct((16, 80, 128), F32),
+        in_specs=[SM] + [VM] * 5 + [ANY] * 4,
         out_specs=VM,
         scratch_shapes=[
             pltpu.VMEM(shape, F32)
@@ -554,14 +574,19 @@
         ]
         + [pltpu.SemaphoreType.DMA((4,))],
         compiler_params=pltpu.CompilerParams(vmem_limit_bytes=24 * MIB),
-    )(beta, own, kown, lo, hi, parts, known, start, coef)
+    )(beta, own, kown, fown, lo, hi, parts, known, start, coef)
     back = swap(out, "tm")
     other = lax.ppermute(back, "tm", [(i, i ^ 1) for i in range(16)])
-    new_field, part = call(field_kernel, [plane, (16, 8, 128)], 2, 0)(back, fine)
-    parted = swap(part, ("gy", "gx"))
+    new_field, size = pl.pallas_call(
+        field_kernel,
+        out_shape=[jax.ShapeDtypeStruct(shape, F32) for shape in (plane, (1,))],
+        in_specs=[VM],
+        out_specs=[VM, SM],
+        compiler_params=pltpu.CompilerParams(vmem_limit_bytes=16 * MIB),
+    )(back)
+    size = lax.ppermute(size, ("tm", "gx", "gy"), turned())
     new_modes = call(final_kernel, [(16, 64, 256)], 4, 0)(back, other, both, coef)[0]
-    parted, new_modes = lax.optimization_barrier((parted, new_modes))
-    size = jnp.sqrt(jnp.sum(parted) / 262144.0).reshape(1)
+    size, new_modes = lax.optimization_barrier((size, new_modes))
     return (new_field.reshape(1, 8, 8, 256), new_modes.reshape(1, 16, 8, 8, 256), size)
 
 

time: 119 us -> 117 us (0.983); the launches traced: 118 us -> 115 us
  waiting for transfers between devices: 19.8 us -> 17.1 us
  starting transfers between devices: 29.8 us -> 27.8 us
  blocking collectives: 48.4 us -> 50.2 us
    all_to_all x2 -> x1, waiting for transfers between devices: 5.66 us -> 1.6 us  [swap(): return lax.all_to_all(value, axis, 0, 0, tiled=True)]
    all_to_all x2 -> x1, starting transfers between devices: 16.8 us -> 13.3 us  [swap(): return lax.all_to_all(value, axis, 0, 0, tiled=True)]
    all_to_all x2, blocking collectives: 48.4 us -> 50.2 us  [swap(): return lax.all_to_all(value, axis, 0, 0, tiled=True)]
    ppermute x0 -> x1, starting transfers between devices: none -> 1.68 us  [per_device(): size = lax.ppermute(size, ('tm', 'gx', 'gy'), turned())]
    ppermute x0 -> x1, waiting for transfers between devices: none -> 1.35 us  [per_device(): size = lax.ppermute(size, ('tm', 'gx', 'gy'), turned())]
where the time goes in v5:
time: 117 us; the launch traced here: 115 us
  blocking collectives  50.2 us (43%)
  starting transfers between devices  27.8 us (24%)
  waiting for transfers between devices  17.1 us (15%)
  Pallas kernels  15.5 us (13%)
  between operations  2.69 us (2%)
    all_to_all x2, blocking collectives, swap(): return lax.all_to_all(value, axis, 0, 0, tiled=True)  50.2 us
    all_to_all x1, starting transfers between devices, swap(): return lax.all_to_all(value, axis, 0, 0, tiled=True)  13.3 us
    ppermute x1, waiting for transfers between devices, per_device(): lo = lax.ppermute(up, 'tm', ring('tm', 1))  6.07 us
    pallas_call x1, Pallas kernels, per_device(): pl.pallas_call(sweep_kernel, out_shape=jax.ShapeDtypeStruct((16, 80, 128)...  5.79 us
    ppermute x5, waiting for transfers between devices, per_device(): lax.ppermute(share[k + 1], 'tm', pair)  4.3 us
    ppermute x5, starting transfers between devices, per_device(): lax.ppermute(share[k + 1], 'tm', pair)  3.95 us
    ppermute x1, waiting for transfers between devices, per_device(): hi = lax.ppermute(dn, 'tm', ring('tm', -1))  2.77 us
    pallas_call x1, Pallas kernels, per_device(): call(final_kernel, [(16, 64, 256)], 4, 0)(back, other, both, coef)[0]  2.38 us
  transfers between devices with their start and end apart: 16, of which 7 were waited for; matrix products, arithmetic and copies ran while one was open for 1% of the time, Pallas kernels for 5%

profile of v5, /device:TPU:1, one launch (start us, length us, event | category | flops | bytes accessed | tf_op | source)
XLA Modules:
  0.0 114.8 jit_solution(2751050629011092149)
XLA Ops:
  0.7 2.2 %shard_map.94 = (f32[64,256]{1,0:T(8,128)}, f32[64,256]{1,0:T(8,128)}, f32[64,256]{1,0:T(8,128)}, f32[64,256]{1,0:T(8,128)}, f32[40,256]{1,0:T(8,128)}, /*index=5*/f32[40,256]{1,0:T(8,128)}, f32[256,128]{1,0:T(8,128)}) custom-call(f32[8]{0:T(128)} %rk_in.1, f32[16]{0:T(128)} %w_in.1, f32[16]{0:T(128)} %rate_in.1, f32[64,256]{1,0:T(8,128)} %bitcast.28, ...), custom_call_target="tpu_custom_call" | custom-call | tf_op jit(solution)/shard_map/pallas_call | solution.py:506
  2.9 2.2 %collective-permute-start = (f32[40,256]{1,0:T(8,128)}, f32[40,256]{1,0:T(8,128)S(1)}, u32[]{:S(2)}, u32[]{:S(2)}) collective-permute-start(f32[40,256]{1,0:T(8,128)} %get-tuple-element.30), channel_id=1, source_target_pairs={{0,4},{4,8},{8,12},{12,0},{1,5},{5,9},{9,13},{13,1},{2,6},{6,10},{... | collective-permute-start | bytes 122888 | tf_op jit(solution)/shard_map/ppermute | solution.py:516
  5.1 1.5 %collective-permute-start.1 = (f32[40,256]{1,0:T(8,128)}, f32[40,256]{1,0:T(8,128)S(1)}, u32[]{:S(2)}, u32[]{:S(2)}) collective-permute-start(f32[40,256]{1,0:T(8,128)} %get-tuple-element.31), channel_id=1, source_target_pairs={{0,12},{4,0},{8,4},{12,8},{1,13},{5,1},{9,5},{13,9},{2,14},{6,2},{... | collective-permute-start | bytes 122888 | tf_op jit(solution)/shard_map/ppermute | solution.py:517
  6.7 0.7 collective-permute-start.4
  8.2 1.3 %collective-permute-start.2 = (f32[80,256]{1,0:T(8,128)S(1)}, f32[80,256]{1,0:T(8,128)S(1)}, u32[]{:S(2)}, u32[]{:S(2)}) collective-permute-start(f32[80,256]{1,0:T(8,128)S(1)} %get-tuple-element.32), channel_id=1, source_target_pairs={{0,1},{1,2},{2,3},{3,0},{4,5},{5,6},{6,7},{7,4},{8,9},{9,10},{10,1... | collective-permute-start | bytes 245768 | tf_op jit(solution)/shard_map/ppermute | solution.py:529
  9.5 1.5 %collective-permute-start.3 = (f32[80,256]{1,0:T(8,128)S(1)}, f32[80,256]{1,0:T(8,128)S(1)}, u32[]{:S(2)}, u32[]{:S(2)}) collective-permute-start(f32[80,256]{1,0:T(8,128)S(1)} %get-tuple-element.33), channel_id=1, source_target_pairs={{0,3},{1,0},{2,1},{3,2},{4,7},{5,4},{6,5},{7,6},{8,11},{9,8},{10,9... | collective-permute-start | bytes 245768 | tf_op jit(solution)/shard_map/ppermute | solution.py:530
  11.9 0.9 collective-permute-done.2.ylo
  12.8 2.1 %shard_map.96.mine = f32[16,24,128]{2,1,0:T(8,128)} custom-call(f32[1]{0:T(128)} %bitcast.omega, f32[64,256]{1,0:T(8,128)S(1)} %copy-done.1, f32[64,256]{1,0:T(8,128)S(1)} %copy-done.2, f32[64,256]{1,0:T(8,128)S(1)} %copy-done.3, f32[64,256]{1,0:T(8,128)S(1)} %copy-done.4, f32[40,256]{1,0:T(8,128)S(1)} %collective-permute-done.xlo, ...), custom_call_target="tpu_custom_call" | custom-call | flops 20000000000 | bytes 1000000 | tf_op jit(solution)/shard_map/pallas_call | solution.py:533
  14.9 13.3 %all-to-all-start = ((f32[16,24,128]{2,1,0:T(8,128)}), f32[16,24,128]{2,1,0:T(8,128)S(1)}, u32[]{:S(2)}, u32[]{:S(2)}) async-start(f32[16,24,128]{2,1,0:T(8,128)} %shard_map.96.mine), calls=%async_computation | async-start | bytes 393216 | tf_op jit(solution)/shard_map/all_to_all | solution.py:485
  31.1 1.3 %collective-permute-start.6 = (f32[128,128]{1,0:T(8,128)S(1)}, f32[128,128]{1,0:T(8,128)S(1)}, u32[]{:S(2)}, u32[]{:S(2)}) collective-permute-start(f32[128,128]{1,0:T(8,128)S(1)} %get-tuple-element.53), channel_id=1, source_target_pairs={{0,16},{64,80},{192,208},{1,17},{65,81},{193,209},{2,18},{66,82},{... | collective-permute-start | bytes 196616 | tf_op jit(solution)/shard_map/ppermute | solution.py:541
  32.7 4.3 %collective-permute-done.6 = f32[128,128]{1,0:T(8,128)S(1)} collective-permute-done((f32[128,128]{1,0:T(8,128)S(1)}, f32[128,128]{1,0:T(8,128)S(1)}, u32[]{:S(2)}, u32[]{:S(2)}) %collective-permute-start.6) | collective-permute-done | bytes 65568 | tf_op jit(solution)/shard_map/ppermute | solution.py:541
  37.0 1.6 %all-to-all-done.parts.parts_in = f32[16,24,128]{2,1,0:T(8,128)S(1)} async-done(((f32[16,24,128]{2,1,0:T(8,128)}), f32[16,24,128]{2,1,0:T(8,128)S(1)}, u32[]{:S(2)}, u32[]{:S(2)}) %all-to-all-start) | async-done | bytes 196640 | tf_op jit(solution)/shard_map/all_to_all | solution.py:485
  38.6 1.4 %shard_map.98 = (f32[16,144,128]{2,1,0:T(8,128)S(1)}, f32[16,16,128]{2,1,0:T(8,128)S(1)}) custom-call(f32[16,24,128]{2,1,0:T(8,128)S(1)} %all-to-all-done.parts.parts_in, f32[256,128]{1,0:T(8,128)S(1)} %copy-done, f32[128,128]{1,0:T(8,128)S(1)} %fusion.start.start_in, f32[32,128]{1,0:T(8,128)S(1)} %reshape.47.coef.coef_in), custom_call_target="tpu_custom_call" | custom-call | tf_op jit(solution)/shard_map/pallas_call | solution.py:545
  40.0 23.7 %all_to_all.15 = f32[16,144,128]{2,1,0:T(8,128)S(1)} all-to-all(f32[16,144,128]{2,1,0:T(8,128)S(1)} %get-tuple-element.38), channel_id=1, replica_groups=mesh['tm'=16,'gx'=4,'gy'=4] {'gy','gx'}, dimensions={0} | all-to-all | bytes 2359296 | tf_op jit(solution)/shard_map/all_to_all | solution.py:485
  63.7 0.8 shard_map.99
  64.4 0.8 collective-permute-start.11
  65.6 6.1 %collective-permute-done.11.lo = f32[135,8,128]{2,1,0:T(8,128)S(1)} collective-permute-done((f32[135,8,128]{2,1,0:T(8,128)S(1)}, f32[135,8,128]{2,1,0:T(8,128)S(1)}, u32[]{:S(2)}, u32[]{:S(2)}) %collective-permute-start.11) | collective-permute-done | bytes 552992 | tf_op jit(solution)/shard_map/ppermute | solution.py:555
  71.6 2.8 %collective-permute-done.12.hi = f32[135,8,128]{2,1,0:T(8,128)S(1)} collective-permute-done((f32[135,8,128]{2,1,0:T(8,128)S(1)}, f32[135,8,128]{2,1,0:T(8,128)S(1)}, u32[]{:S(2)}, u32[]{:S(2)}) %collective-permute-start.12) | collective-permute-done | bytes 552992 | tf_op jit(solution)/shard_map/ppermute | solution.py:556
  74.4 5.8 %shard_map.100 = f32[16,80,128]{2,1,0:T(8,128)S(1)} custom-call(f32[16]{0:T(128)S(1)} %broadcast_multiply_fusion.beta, f32[16,16,8,128]{3,2,1,0:T(8,128)S(1)} %get-tuple-element.39.own, f32[16,8,128]{2,1,0:T(8,128)S(1)} %get-tuple-element.40.kown, f32[16,8,128]{2,1,0:T(8,128)S(1)} %get-tuple-element.41.fown, f32[135,8,128]{2,1,0:T(8,128)S(1)} %collective-permute-done.11.lo, ...), custom_call_target="tpu_custom_call" | custom-call | tf_op jit(solution)/shard_map/pallas_call | solution.py:557
  80.2 26.5 %all_to_all.16.got = f32[16,80,128]{2,1,0:T(8,128)S(1)} all-to-all(f32[16,80,128]{2,1,0:T(8,128)S(1)} %shard_map.100), channel_id=1, replica_groups=mesh['tm'=16,'gx'=4,'gy'=4] {'tm'}, dimensions={0} | all-to-all | bytes 1310720 | tf_op jit(solution)/shard_map/all_to_all | solution.py:485
  106.8 0.8 shard_map.101
  107.6 1.7 %collective-permute-start.13 = (f32[1]{0:T(128)}, f32[1]{0:T(128)}, u32[]{:S(2)}, u32[]{:S(2)}) collective-permute-start(f32[1]{0:T(128)} %get-tuple-element.46), channel_id=1, source_target_pairs={{0,10},{16,9},{32,6},{48,14},{224,11},{240,8},{64,5},{80,13},{192,... | collective-permute-start | bytes 20 | tf_op jit(solution)/shard_map/ppermute | solution.py:587
  109.3 2.4 %shard_map.102 = f32[16,64,256]{2,1,0:T(8,128)} custom-call(f32[16,80,128]{2,1,0:T(8,128)S(1)} %all_to_all.16.got, f32[16,80,128]{2,1,0:T(8,128)S(1)} %collective-permute-done.14.other, f32[16,24,128]{2,1,0:T(8,128)} %shard_map.96.mine, f32[32,128]{1,0:T(8,128)S(1)} %reshape.47.coef.coef_in), custom_call_target="tpu_custom_call" | custom-call | tf_op jit(solution)/shard_map/pallas_call | solution.py:588
  111.6 1.4 %collective-permute-done.13 = f32[1]{0:T(128)} collective-permute-done((f32[1]{0:T(128)}, f32[1]{0:T(128)}, u32[]{:S(2)}, u32[]{:S(2)}) %collective-permute-start.13) | collective-permute-done | bytes 36 | tf_op jit(solution)/shard_map/ppermute | solution.py:587
  (49 shorter events, 5.3 us)
Async XLA Ops:
  0.6 10.3 %copy-start.6 = (f32[16]{0:T(128)S(1)}, f32[16]{0:T(128)}, u32[]{:S(2)}) copy-start(f32[16]{0:T(128)} %rate_in.1) | copy-start | bytes 196
  0.6 10.3 %copy-start.7 = (f32[16]{0:T(128)S(1)}, f32[16]{0:T(128)}, u32[]{:S(2)}) copy-start(f32[16]{0:T(128)} %w_in.1) | copy-start | bytes 196
  2.8 5.3 %copy-start.1 = (f32[64,256]{1,0:T(8,128)S(1)}, f32[64,256]{1,0:T(8,128)}, u32[]{:S(2)}) copy-start(f32[64,256]{1,0:T(8,128)} %get-tuple-element.26.u) | copy-start | bytes 196612
  2.9 5.3 %copy-start.2 = (f32[64,256]{1,0:T(8,128)S(1)}, f32[64,256]{1,0:T(8,128)}, u32[]{:S(2)}) copy-start(f32[64,256]{1,0:T(8,128)} %get-tuple-element.27.kap) | copy-start | bytes 196612
  2.9 5.3 %copy-start.3 = (f32[64,256]{1,0:T(8,128)S(1)}, f32[64,256]{1,0:T(8,128)}, u32[]{:S(2)}) copy-start(f32[64,256]{1,0:T(8,128)} %get-tuple-element.28.g0) | copy-start | bytes 196612
  2.9 9.9 %copy-start.4 = (f32[64,256]{1,0:T(8,128)S(1)}, f32[64,256]{1,0:T(8,128)}, u32[]{:S(2)}) copy-start(f32[64,256]{1,0:T(8,128)} %get-tuple-element.29.q1s) | copy-start | bytes 196612
  2.9 5.2 %collective-permute-start = (f32[40,256]{1,0:T(8,128)}, f32[40,256]{1,0:T(8,128)S(1)}, u32[]{:S(2)}, u32[]{:S(2)}) collective-permute-start(f32[40,256]{1,0:T(8,128)} %get-tuple-element.30), channel_id=1, source_target_pairs={{0,4},{4,8},{8,12},{12,0},{1,5},{5,9},{9,13},{13,1},{2,6},{6,10},{... | collective-permute-start | bytes 122888 | tf_op jit(solution)/shard_map/ppermute | solution.py:516
  5.1 3.1 %collective-permute-start.1 = (f32[40,256]{1,0:T(8,128)}, f32[40,256]{1,0:T(8,128)S(1)}, u32[]{:S(2)}, u32[]{:S(2)}) collective-permute-start(f32[40,256]{1,0:T(8,128)} %get-tuple-element.31), channel_id=1, source_target_pairs={{0,12},{4,0},{8,4},{12,8},{1,13},{5,1},{9,5},{13,9},{2,14},{6,2},{... | collective-permute-start | bytes 122888 | tf_op jit(solution)/shard_map/ppermute | solution.py:517
  6.7 21.5 %collective-permute-start.4 = (f32[6,128,128]{2,1,0:T(8,128)}, f32[6,128,128]{2,1,0:T(8,128)S(1)}, u32[]{:S(2)}, u32[]{:S(2)}) collective-permute-start(f32[6,128,128]{2,1,0:T(8,128)} %get-tuple-element.36), channel_id=1, source_target_pairs={{0,64},{1,65},{2,66},{3,67},{4,68},{5,69},{6,70},{7,71},{8,72},{9,... | collective-permute-start | bytes 1179656 | tf_op jit(solution)/shard_map/ppermute | solution.py:531
  7.4 20.9 %collective-permute-start.5 = (f32[6,128,128]{2,1,0:T(8,128)}, f32[6,128,128]{2,1,0:T(8,128)S(1)}, u32[]{:S(2)}, u32[]{:S(2)}) collective-permute-start(f32[6,128,128]{2,1,0:T(8,128)} %get-tuple-element.37), channel_id=1, source_target_pairs={{0,192},{1,193},{2,194},{3,195},{4,196},{5,197},{6,198},{7,199},{8... | collective-permute-start | bytes 1179656 | tf_op jit(solution)/shard_map/ppermute | solution.py:531
  8.2 4.6 %collective-permute-start.2 = (f32[80,256]{1,0:T(8,128)S(1)}, f32[80,256]{1,0:T(8,128)S(1)}, u32[]{:S(2)}, u32[]{:S(2)}) collective-permute-start(f32[80,256]{1,0:T(8,128)S(1)} %get-tuple-element.32), channel_id=1, source_target_pairs={{0,1},{1,2},{2,3},{3,0},{4,5},{5,6},{6,7},{7,4},{8,9},{9,10},{10,1... | collective-permute-start | bytes 245768 | tf_op jit(solution)/shard_map/ppermute | solution.py:529
  9.5 3.3 %collective-permute-start.3 = (f32[80,256]{1,0:T(8,128)S(1)}, f32[80,256]{1,0:T(8,128)S(1)}, u32[]{:S(2)}, u32[]{:S(2)}) collective-permute-start(f32[80,256]{1,0:T(8,128)S(1)} %get-tuple-element.33), channel_id=1, source_target_pairs={{0,3},{1,0},{2,1},{3,2},{4,7},{5,4},{6,5},{7,6},{8,11},{9,8},{10,9... | collective-permute-start | bytes 245768 | tf_op jit(solution)/shard_map/ppermute | solution.py:530
  12.8 15.4 %copy-start.5 = (f32[6,128,128]{2,1,0:T(8,128)S(1)}, f32[6,128,128]{2,1,0:T(8,128)}, u32[]{:S(2)}) copy-start(f32[6,128,128]{2,1,0:T(8,128)} %get-tuple-element.35) | copy-start | bytes 1179652
  14.9 23.7 %all-to-all-start = ((f32[16,24,128]{2,1,0:T(8,128)}), f32[16,24,128]{2,1,0:T(8,128)S(1)}, u32[]{:S(2)}, u32[]{:S(2)}) async-start(f32[16,24,128]{2,1,0:T(8,128)} %shard_map.96.mine), calls=%async_computation | async-start | bytes 393216 | tf_op jit(solution)/shard_map/all_to_all | solution.py:485
  28.3 10.4 %copy-start = (f32[256,128]{1,0:T(8,128)S(1)}, f32[256,128]{1,0:T(8,128)}, u32[]{:S(2)}) copy-start(f32[256,128]{1,0:T(8,128)} %get-tuple-element.34.after.sk) | copy-start | bytes 393220
  28.4 4.3 %collective-permute-start.7 = (f32[128,128]{1,0:T(8,128)S(1)}, f32[128,128]{1,0:T(8,128)S(1)}, u32[]{:S(2)}, u32[]{:S(2)}) collective-permute-start(f32[128,128]{1,0:T(8,128)S(1)} %get-tuple-element.49), channel_id=1, source_target_pairs={{0,32},{64,96},{192,224},{1,33},{65,97},{193,225},{2,34},{66,98},{... | collective-permute-start | bytes 196616 | tf_op jit(solution)/shard_map/ppermute | solution.py:541
  29.0 3.6 %collective-permute-start.10 = (f32[128,128]{1,0:T(8,128)S(1)}, f32[128,128]{1,0:T(8,128)S(1)}, u32[]{:S(2)}, u32[]{:S(2)}) collective-permute-start(f32[128,128]{1,0:T(8,128)S(1)} %get-tuple-element.50), channel_id=1, source_target_pairs={{64,144},{192,160},{65,145},{193,161},{66,146},{194,162},{67,147},... | collective-permute-start | bytes 196616 | tf_op jit(solution)/shard_map/ppermute | solution.py:541
  29.7 3.0 %collective-permute-start.9 = (f32[128,128]{1,0:T(8,128)S(1)}, f32[128,128]{1,0:T(8,128)S(1)}, u32[]{:S(2)}, u32[]{:S(2)}) collective-permute-start(f32[128,128]{1,0:T(8,128)S(1)} %get-tuple-element.51), channel_id=1, source_target_pairs={{64,128},{192,176},{65,129},{193,177},{66,130},{194,178},{67,131},... | collective-permute-start | bytes 196616 | tf_op jit(solution)/shard_map/ppermute | solution.py:541
  30.4 2.3 %collective-permute-start.8 = (f32[128,128]{1,0:T(8,128)S(1)}, f32[128,128]{1,0:T(8,128)S(1)}, u32[]{:S(2)}, u32[]{:S(2)}) collective-permute-start(f32[128,128]{1,0:T(8,128)S(1)} %get-tuple-element.52), channel_id=1, source_target_pairs={{0,48},{64,112},{192,240},{1,49},{65,113},{193,241},{2,50},{66,114... | collective-permute-start | bytes 196616 | tf_op jit(solution)/shard_map/ppermute | solution.py:541
  31.1 5.9 %collective-permute-start.6 = (f32[128,128]{1,0:T(8,128)S(1)}, f32[128,128]{1,0:T(8,128)S(1)}, u32[]{:S(2)}, u32[]{:S(2)}) collective-permute-start(f32[128,128]{1,0:T(8,128)S(1)} %get-tuple-element.53), channel_id=1, source_target_pairs={{0,16},{64,80},{192,208},{1,17},{65,81},{193,209},{2,18},{66,82},{... | collective-permute-start | bytes 196616 | tf_op jit(solution)/shard_map/ppermute | solution.py:541
  64.4 7.2 %collective-permute-start.11 = (f32[135,8,128]{2,1,0:T(8,128)S(1)}, f32[135,8,128]{2,1,0:T(8,128)S(1)}, u32[]{:S(2)}, u32[]{:S(2)}) collective-permute-start(f32[135,8,128]{2,1,0:T(8,128)S(1)} %get-tuple-element.42), channel_id=1, source_target_pairs={{0,16},{16,32},{32,48},{48,64},{64,80},{80,96},{96,112},{112,128},... | collective-permute-start | bytes 1658888 | tf_op jit(solution)/shard_map/ppermute | solution.py:555
  65.2 9.2 %collective-permute-start.12 = (f32[135,8,128]{2,1,0:T(8,128)S(1)}, f32[135,8,128]{2,1,0:T(8,128)S(1)}, u32[]{:S(2)}, u32[]{:S(2)}) collective-permute-start(f32[135,8,128]{2,1,0:T(8,128)S(1)} %get-tuple-element.43), channel_id=1, source_target_pairs={{0,240},{16,0},{32,16},{48,32},{64,48},{80,64},{96,80},{112,96},{1... | collective-permute-start | bytes 1658888 | tf_op jit(solution)/shard_map/ppermute | solution.py:556
  106.8 2.5 %collective-permute-start.14 = (f32[16,80,128]{2,1,0:T(8,128)S(1)}, f32[16,80,128]{2,1,0:T(8,128)S(1)}, u32[]{:S(2)}, u32[]{:S(2)}) collective-permute-start(f32[16,80,128]{2,1,0:T(8,128)S(1)} %all_to_all.16.got), channel_id=1, source_target_pairs={{0,16},{16,0},{32,48},{48,32},{64,80},{80,64},{96,112},{112,96},{1... | collective-permute-start | bytes 1966088 | tf_op jit(solution)/shard_map/ppermute | solution.py:579
  107.6 5.4 %collective-permute-start.13 = (f32[1]{0:T(128)}, f32[1]{0:T(128)}, u32[]{:S(2)}, u32[]{:S(2)}) collective-permute-start(f32[1]{0:T(128)} %get-tuple-element.46), channel_id=1, source_target_pairs={{0,10},{16,9},{32,6},{48,14},{224,11},{240,8},{64,5},{80,13},{192,... | collective-permute-start | bytes 20 | tf_op jit(solution)/shard_map/ppermute | solution.py:587

commit v6 on v5

--- a/solution.py
+++ b/solution.py
@@ -13,7 +13,6 @@
 ANY = pl.BlockSpec(memory_space=pl.ANY)
 MIB = 1024 * 1024
 LONG = pl.CostEstimate(flops=20_000_000_000, bytes_accessed=1_000_000, transcendentals=0)
-SLOTS = [0, 1, 2, 3, 0, 0, 4, 5, 6, 7, 8, 9, 12, 13, 14, 15, 11, 10]
 HALO = 15
 TRI = [HALO] + [HALO - j for j in range(1, HALO)]
 OFF = [sum(TRI[:j]) for j in range(HALO)]
@@ -78,7 +77,7 @@
     sk[...] = jnp.concatenate([s[...], kap[...]], axis=0).T
 
 
-def scatter_kernel(after, modes_in, out0, out1, out2, modes, packed, sems):
+def scatter_kernel(after, modes_in, out0, out1, out2, out3, modes, packed, sems):
     @pl.when(lax.axis_index("tm") == 0)
     def _():
         copies = [
@@ -91,12 +90,10 @@
             copy.wait()
         for m in range(8):
             both = jnp.concatenate([modes[m], modes[m + 8]], axis=0).T
-            pieces = both.reshape(16, 16, 128)
-            for place, slot in enumerate(SLOTS):
-                packed[place, 16 * m : 16 * m + 16] = pieces[slot]
+            packed[:, 16 * m : 16 * m + 16] = both.reshape(16, 16, 128)
         copies = [
-            pltpu.make_async_copy(packed.at[pl.ds(6 * i, 6)], out, sems.at[4 + i])
-            for i, out in enumerate((out0, out1, out2))
+            pltpu.make_async_copy(packed.at[pl.ds(4 * i, 4)], out, sems.at[4 + i])
+            for i, out in enumerate((out0, out1, out2, out3))
         ]
         for copy in copies:
             copy.start()
@@ -423,13 +420,16 @@
     return jnp.concatenate([unpacked(ref[t, 64:72]) for t in range(16)], axis=0)
 
 
-def field_kernel(got, field, size):
-    field[...] = rows_of(got).T[0:64]
+def size_kernel(got, size):
     part = got[0, 72:80]
     for t in range(1, 16):
         part += got[t, 72:80]
     whole = jnp.sum(jnp.sum(part, axis=1, keepdims=True), axis=0, keepdims=True)
     size[0] = jnp.sqrt(whole / 262144.0)[0, 0]
+
+
+def field_kernel(got, field):
+    field[...] = rows_of(got).T[0:64]
 
 
 def final_kernel(got, other, mine, coef, modes):
@@ -517,30 +517,29 @@
     xhi = lax.ppermute(dn, "gx", ring("gx", -1))
     chunks = pl.pallas_call(
         scatter_kernel,
-        out_shape=[jax.ShapeDtypeStruct((6, 128, 128), F32)] * 3,
+        out_shape=[jax.ShapeDtypeStruct((4, 128, 128), F32)] * 4,
         in_specs=[ANY, ANY],
-        out_specs=[ANY] * 3,
-        scratch_shapes=[pltpu.VMEM((16, 64, 256), F32), pltpu.VMEM((18, 128, 128), F32)]
-        + [pltpu.SemaphoreType.DMA((7,))],
+        out_specs=[ANY] * 4,
+        scratch_shapes=[pltpu.VMEM((16, 64, 256), F32), pltpu.VMEM((16, 128, 128), F32)]
+        + [pltpu.SemaphoreType.DMA((8,))],
         compiler_params=pltpu.CompilerParams(vmem_limit_bytes=60 * MIB),
     )(sk, h)
 
     yup, ydn = call(side_kernel, [(80, 256)] * 2, 5, 0)(u, kap, g0, xlo, xhi)
     ylo = lax.ppermute(yup, "gy", ring("gy", 1))
     yhi = lax.ppermute(ydn, "gy", ring("gy", -1))
-    far = [lax.ppermute(chunks[k], "tm", [(0, hub)]) for k, hub in ((1, 4), (2, 12))]
+    far = [lax.ppermute(chunks[k], "tm", [(0, 4 * k)]) for k in (2, 3, 1)]
 
     (both,) = call(
         fine_kernel, [(16, 24, 128)], 9, 1, [(12, 24, 256)] * 4, 16, LONG
     )(omega, u, kap, g0, q1s, xlo, xhi, ylo, yhi)
     parts = swap(both, "tm")
 
-    share = jnp.where(t == 0, chunks[0], far[0] + far[1])
-    pairs = [[(0, k), (4, 4 + k), (12, 12 + k)] for k in (1, 2, 3)]
-    pairs += [[(4, 8), (12, 11)], [(4, 9), (12, 10)]]
-    close = [lax.ppermute(share[k + 1], "tm", pair) for k, pair in enumerate(pairs)]
-    hub = (t == 0) | (t == 4) | (t == 12)
-    start = jnp.where(hub, share[0], sum(close))
+    share = jnp.where(t == 0, chunks[0], far[0] + far[1] + far[2])
+    close = [
+        lax.ppermute(share[k], "tm", [(4 * a, 4 * a + k) for a in range(4)]) for k in (1, 2, 3)
+    ]
+    start = jnp.where(t % 4 == 0, share[0], close[0] + close[1] + close[2])
 
     msg, known = call(known_kernel, [(16, 144, 128), (16, 16, 128)], 4, 0)(
         parts, sk, start, coef
@@ -577,16 +576,17 @@
     )(beta, own, kown, fown, lo, hi, parts, known, start, coef)
     back = swap(out, "tm")
     other = lax.ppermute(back, "tm", [(i, i ^ 1) for i in range(16)])
-    new_field, size = pl.pallas_call(
-        field_kernel,
-        out_shape=[jax.ShapeDtypeStruct(shape, F32) for shape in (plane, (1,))],
+    size = pl.pallas_call(
+        size_kernel,
+        out_shape=jax.ShapeDtypeStruct((1,), F32),
         in_specs=[VM],
-        out_specs=[VM, SM],
+        out_specs=SM,
         compiler_params=pltpu.CompilerParams(vmem_limit_bytes=16 * MIB),
     )(back)
     size = lax.ppermute(size, ("tm", "gx", "gy"), turned())
+    new_field = call(field_kernel, [plane], 1, 0)(back)[0]
     new_modes = call(final_kernel, [(16, 64, 256)], 4, 0)(back, other, both, coef)[0]
-    size, new_modes = lax.optimization_barrier((size, new_modes))
+    size, new_modes, new_field = lax.optimization_barrier((size, new_modes, new_field))
     return (new_field.reshape(1, 8, 8, 256), new_modes.reshape(1, 16, 8, 8, 256), size)
 
 

time: 117 us -> 118 us (level)
  starting transfers between devices: 27.8 us -> 29.3 us
  blocking collectives: 50.2 us -> 49 us
    all_to_all x1, starting transfers between devices: 13.3 us -> 15.5 us  [swap(): return lax.all_to_all(value, axis, 0, 0, tiled=True)]
    all_to_all x1, waiting for transfers between devices: 1.6 us -> 2.95 us  [swap(): return lax.all_to_all(value, axis, 0, 0, tiled=True)]
    ppermute x7 -> x6, starting transfers between devices: 5.32 us -> 4.65 us  [the longest x3 2.62 us: per_device(): lax.ppermute(share[k], 'tm', [(4 * a, 4 * a + k) for a in range(4)])]
    ppermute x7 -> x6, waiting for transfers between devices: 4.31 us -> 4.33 us  [the longest x3 4.32 us: per_device(): lax.ppermute(share[k], 'tm', [(4 * a, 4 * a + k) for a in range(4)])]
  transfers between devices with their start and end apart: 16 -> 15, of which waited for: 7 -> 6; matrix products, arithmetic and copies ran while one was open for 1% -> 1% of each run, Pallas kernels for 5% -> 5%
where the time goes in v6:
time: 118 us; the launch traced here: 116 us
  blocking collectives  49 us (42%)
  starting transfers between devices  29.3 us (25%)
  waiting for transfers between devices  17.6 us (15%)
  Pallas kernels  16.2 us (14%)
  between operations  2.73 us (2%)
    all_to_all x2, blocking collectives, swap(): return lax.all_to_all(value, axis, 0, 0, tiled=True)  49 us
    all_to_all x1, starting transfers between devices, swap(): return lax.all_to_all(value, axis, 0, 0, tiled=True)  15.5 us
    ppermute x1, waiting for transfers between devices, per_device(): lo = lax.ppermute(up, 'tm', ring('tm', 1))  6.07 us
    pallas_call x1, Pallas kernels, per_device(): pl.pallas_call(sweep_kernel, out_shape=jax.ShapeDtypeStruct((16, 80, 128)...  5.79 us
    ppermute x3, waiting for transfers between devices, per_device(): lax.ppermute(share[k], 'tm', [(4 * a, 4 * a + k) for a in range(4)])  4.32 us
    all_to_all x1, waiting for transfers between devices, swap(): return lax.all_to_all(value, axis, 0, 0, tiled=True)  2.95 us
    ppermute x1, waiting for transfers between devices, per_device(): hi = lax.ppermute(dn, 'tm', ring('tm', -1))  2.77 us
    ppermute x3, starting transfers between devices, per_device(): lax.ppermute(share[k], 'tm', [(4 * a, 4 * a + k) for a in range(4)])  2.62 us
  transfers between devices with their start and end apart: 15, of which 6 were waited for; matrix products, arithmetic and copies ran while one was open for 1% of the time, Pallas kernels for 5%

profile of v6, /device:TPU:1, one launch (start us, length us, event | category | flops | bytes accessed | tf_op | source)
XLA Modules:
  0.0 116.3 jit_solution(18221817412883468594)
XLA Ops:
  0.7 2.2 %shard_map.94 = (f32[64,256]{1,0:T(8,128)}, f32[64,256]{1,0:T(8,128)}, f32[64,256]{1,0:T(8,128)}, f32[64,256]{1,0:T(8,128)}, f32[40,256]{1,0:T(8,128)}, /*index=5*/f32[40,256]{1,0:T(8,128)}, f32[256,128]{1,0:T(8,128)}) custom-call(f32[8]{0:T(128)} %rk_in.1, f32[16]{0:T(128)} %w_in.1, f32[16]{0:T(128)} %rate_in.1, f32[64,256]{1,0:T(8,128)} %bitcast.25, ...), custom_call_target="tpu_custom_call" | custom-call | tf_op jit(solution)/shard_map/pallas_call | solution.py:506
  2.9 2.2 %collective-permute-start = (f32[40,256]{1,0:T(8,128)}, f32[40,256]{1,0:T(8,128)S(1)}, u32[]{:S(2)}, u32[]{:S(2)}) collective-permute-start(f32[40,256]{1,0:T(8,128)} %get-tuple-element.30), channel_id=1, source_target_pairs={{0,4},{4,8},{8,12},{12,0},{1,5},{5,9},{9,13},{13,1},{2,6},{6,10},{... | collective-permute-start | bytes 122888 | tf_op jit(solution)/shard_map/ppermute | solution.py:516
  5.1 1.5 %collective-permute-start.1 = (f32[40,256]{1,0:T(8,128)}, f32[40,256]{1,0:T(8,128)S(1)}, u32[]{:S(2)}, u32[]{:S(2)}) collective-permute-start(f32[40,256]{1,0:T(8,128)} %get-tuple-element.31), channel_id=1, source_target_pairs={{0,12},{4,0},{8,4},{12,8},{1,13},{5,1},{9,5},{13,9},{2,14},{6,2},{... | collective-permute-start | bytes 122888 | tf_op jit(solution)/shard_map/ppermute | solution.py:517
  7.4 0.7 collective-permute-start.5
  8.1 0.7 collective-permute-start.6
  8.9 1.3 %collective-permute-start.2 = (f32[80,256]{1,0:T(8,128)S(1)}, f32[80,256]{1,0:T(8,128)S(1)}, u32[]{:S(2)}, u32[]{:S(2)}) collective-permute-start(f32[80,256]{1,0:T(8,128)S(1)} %get-tuple-element.32), channel_id=1, source_target_pairs={{0,1},{1,2},{2,3},{3,0},{4,5},{5,6},{6,7},{7,4},{8,9},{9,10},{10,1... | collective-permute-start | bytes 245768 | tf_op jit(solution)/shard_map/ppermute | solution.py:529
  10.2 1.5 %collective-permute-start.3 = (f32[80,256]{1,0:T(8,128)S(1)}, f32[80,256]{1,0:T(8,128)S(1)}, u32[]{:S(2)}, u32[]{:S(2)}) collective-permute-start(f32[80,256]{1,0:T(8,128)S(1)} %get-tuple-element.33), channel_id=1, source_target_pairs={{0,3},{1,0},{2,1},{3,2},{4,7},{5,4},{6,5},{7,6},{8,11},{9,8},{10,9... | collective-permute-start | bytes 245768 | tf_op jit(solution)/shard_map/ppermute | solution.py:530
  12.6 0.9 collective-permute-done.2.ylo
  13.5 2.1 %shard_map.96.mine = f32[16,24,128]{2,1,0:T(8,128)} custom-call(f32[1]{0:T(128)} %bitcast.omega, f32[64,256]{1,0:T(8,128)S(1)} %copy-done.1, f32[64,256]{1,0:T(8,128)S(1)} %copy-done.2, f32[64,256]{1,0:T(8,128)S(1)} %copy-done.3, f32[64,256]{1,0:T(8,128)S(1)} %copy-done.4, f32[40,256]{1,0:T(8,128)S(1)} %collective-permute-done.xlo, ...), custom_call_target="tpu_custom_call" | custom-call | flops 20000000000 | bytes 1000000 | tf_op jit(solution)/shard_map/pallas_call | solution.py:533
  15.5 15.5 %all-to-all-start = ((f32[16,24,128]{2,1,0:T(8,128)}), f32[16,24,128]{2,1,0:T(8,128)S(1)}, u32[]{:S(2)}, u32[]{:S(2)}) async-start(f32[16,24,128]{2,1,0:T(8,128)} %shard_map.96.mine), calls=%async_computation | async-start | bytes 393216 | tf_op jit(solution)/shard_map/all_to_all | solution.py:485
  32.5 1.3 %collective-permute-start.7 = (f32[128,128]{1,0:T(8,128)S(1)}, f32[128,128]{1,0:T(8,128)S(1)}, u32[]{:S(2)}, u32[]{:S(2)}) collective-permute-start(f32[128,128]{1,0:T(8,128)S(1)} %get-tuple-element.51), channel_id=1, source_target_pairs={{0,16},{64,80},{128,144},{192,208},{1,17},{65,81},{129,145},{193,2... | collective-permute-start | bytes 196616 | tf_op jit(solution)/shard_map/ppermute | solution.py:540
  34.1 4.3 %collective-permute-done.7 = f32[128,128]{1,0:T(8,128)S(1)} collective-permute-done((f32[128,128]{1,0:T(8,128)S(1)}, f32[128,128]{1,0:T(8,128)S(1)}, u32[]{:S(2)}, u32[]{:S(2)}) %collective-permute-start.7) | collective-permute-done | bytes 65568 | tf_op jit(solution)/shard_map/ppermute | solution.py:540
  38.5 2.9 %all-to-all-done.parts.parts_in = f32[16,24,128]{2,1,0:T(8,128)S(1)} async-done(((f32[16,24,128]{2,1,0:T(8,128)}), f32[16,24,128]{2,1,0:T(8,128)S(1)}, u32[]{:S(2)}, u32[]{:S(2)}) %all-to-all-start) | async-done | bytes 196640 | tf_op jit(solution)/shard_map/all_to_all | solution.py:485
  41.4 1.4 %shard_map.98 = (f32[16,144,128]{2,1,0:T(8,128)S(1)}, f32[16,16,128]{2,1,0:T(8,128)S(1)}) custom-call(f32[16,24,128]{2,1,0:T(8,128)S(1)} %all-to-all-done.parts.parts_in, f32[256,128]{1,0:T(8,128)S(1)} %copy-done, f32[128,128]{1,0:T(8,128)S(1)} %fusion.start.start_in, f32[32,128]{1,0:T(8,128)S(1)} %reshape.47.coef.coef_in), custom_call_target="tpu_custom_call" | custom-call | tf_op jit(solution)/shard_map/pallas_call | solution.py:544
  42.8 23.7 %all_to_all.15 = f32[16,144,128]{2,1,0:T(8,128)S(1)} all-to-all(f32[16,144,128]{2,1,0:T(8,128)S(1)} %get-tuple-element.39), channel_id=1, replica_groups=mesh['tm'=16,'gx'=4,'gy'=4] {'gy','gx'}, dimensions={0} | all-to-all | bytes 2359296 | tf_op jit(solution)/shard_map/all_to_all | solution.py:485
  66.5 0.8 shard_map.99
  67.3 0.8 collective-permute-start.10
  68.4 6.1 %collective-permute-done.10.lo = f32[135,8,128]{2,1,0:T(8,128)S(1)} collective-permute-done((f32[135,8,128]{2,1,0:T(8,128)S(1)}, f32[135,8,128]{2,1,0:T(8,128)S(1)}, u32[]{:S(2)}, u32[]{:S(2)}) %collective-permute-start.10) | collective-permute-done | bytes 552992 | tf_op jit(solution)/shard_map/ppermute | solution.py:554
  74.5 2.8 %collective-permute-done.11.hi = f32[135,8,128]{2,1,0:T(8,128)S(1)} collective-permute-done((f32[135,8,128]{2,1,0:T(8,128)S(1)}, f32[135,8,128]{2,1,0:T(8,128)S(1)}, u32[]{:S(2)}, u32[]{:S(2)}) %collective-permute-start.11) | collective-permute-done | bytes 552992 | tf_op jit(solution)/shard_map/ppermute | solution.py:555
  77.2 5.8 %shard_map.100 = f32[16,80,128]{2,1,0:T(8,128)S(1)} custom-call(f32[16]{0:T(128)S(1)} %broadcast_multiply_fusion.beta, f32[16,16,8,128]{3,2,1,0:T(8,128)S(1)} %get-tuple-element.40.own, f32[16,8,128]{2,1,0:T(8,128)S(1)} %get-tuple-element.41.kown, f32[16,8,128]{2,1,0:T(8,128)S(1)} %get-tuple-element.42.fown, f32[135,8,128]{2,1,0:T(8,128)S(1)} %collective-permute-done.10.lo, ...), custom_call_target="tpu_custom_call" | custom-call | tf_op jit(solution)/shard_map/pallas_call | solution.py:556
  83.0 25.4 %all_to_all.16.got = f32[16,80,128]{2,1,0:T(8,128)S(1)} all-to-all(f32[16,80,128]{2,1,0:T(8,128)S(1)} %shard_map.100), channel_id=1, replica_groups=mesh['tm'=16,'gx'=4,'gy'=4] {'tm'}, dimensions={0} | all-to-all | bytes 1310720 | tf_op jit(solution)/shard_map/all_to_all | solution.py:485
  109.1 1.7 %collective-permute-start.12 = (f32[1]{0:T(128)}, f32[1]{0:T(128)}, u32[]{:S(2)}, u32[]{:S(2)}) collective-permute-start(f32[1]{0:T(128)} %shard_map.101), channel_id=1, source_target_pairs={{0,10},{16,9},{32,6},{48,14},{224,11},{240,8},{64,5},{80,13},{192,... | collective-permute-start | bytes 20 | tf_op jit(solution)/shard_map/ppermute | solution.py:586
  110.7 0.8 shard_map.103
  111.5 2.4 %shard_map.102 = f32[16,64,256]{2,1,0:T(8,128)} custom-call(f32[16,80,128]{2,1,0:T(8,128)S(1)} %all_to_all.16.got, f32[16,80,128]{2,1,0:T(8,128)S(1)} %collective-permute-done.13.other, f32[16,24,128]{2,1,0:T(8,128)} %shard_map.96.mine, f32[32,128]{1,0:T(8,128)S(1)} %reshape.47.coef.coef_in), custom_call_target="tpu_custom_call" | custom-call | tf_op jit(solution)/shard_map/pallas_call | solution.py:588
  (48 shorter events, 5.1 us)
Async XLA Ops:
  0.6 11.0 %copy-start.6 = (f32[16]{0:T(128)S(1)}, f32[16]{0:T(128)}, u32[]{:S(2)}) copy-start(f32[16]{0:T(128)} %rate_in.1) | copy-start | bytes 196
  0.6 11.0 %copy-start.7 = (f32[16]{0:T(128)S(1)}, f32[16]{0:T(128)}, u32[]{:S(2)}) copy-start(f32[16]{0:T(128)} %w_in.1) | copy-start | bytes 196
  2.8 5.9 %copy-start.1 = (f32[64,256]{1,0:T(8,128)S(1)}, f32[64,256]{1,0:T(8,128)}, u32[]{:S(2)}) copy-start(f32[64,256]{1,0:T(8,128)} %get-tuple-element.26.u) | copy-start | bytes 196612
  2.9 5.9 %copy-start.2 = (f32[64,256]{1,0:T(8,128)S(1)}, f32[64,256]{1,0:T(8,128)}, u32[]{:S(2)}) copy-start(f32[64,256]{1,0:T(8,128)} %get-tuple-element.27.kap) | copy-start | bytes 196612
  2.9 5.9 %copy-start.3 = (f32[64,256]{1,0:T(8,128)S(1)}, f32[64,256]{1,0:T(8,128)}, u32[]{:S(2)}) copy-start(f32[64,256]{1,0:T(8,128)} %get-tuple-element.28.g0) | copy-start | bytes 196612
  2.9 10.6 %copy-start.4 = (f32[64,256]{1,0:T(8,128)S(1)}, f32[64,256]{1,0:T(8,128)}, u32[]{:S(2)}) copy-start(f32[64,256]{1,0:T(8,128)} %get-tuple-element.29.q1s) | copy-start | bytes 196612
  2.9 5.9 %collective-permute-start = (f32[40,256]{1,0:T(8,128)}, f32[40,256]{1,0:T(8,128)S(1)}, u32[]{:S(2)}, u32[]{:S(2)}) collective-permute-start(f32[40,256]{1,0:T(8,128)} %get-tuple-element.30), channel_id=1, source_target_pairs={{0,4},{4,8},{8,12},{12,0},{1,5},{5,9},{9,13},{13,1},{2,6},{6,10},{... | collective-permute-start | bytes 122888 | tf_op jit(solution)/shard_map/ppermute | solution.py:516
  5.1 3.7 %collective-permute-start.1 = (f32[40,256]{1,0:T(8,128)}, f32[40,256]{1,0:T(8,128)S(1)}, u32[]{:S(2)}, u32[]{:S(2)}) collective-permute-start(f32[40,256]{1,0:T(8,128)} %get-tuple-element.31), channel_id=1, source_target_pairs={{0,12},{4,0},{8,4},{12,8},{1,13},{5,1},{9,5},{13,9},{2,14},{6,2},{... | collective-permute-start | bytes 122888 | tf_op jit(solution)/shard_map/ppermute | solution.py:517
  6.7 24.4 %collective-permute-start.4 = (f32[4,128,128]{2,1,0:T(8,128)}, f32[4,128,128]{2,1,0:T(8,128)S(1)}, u32[]{:S(2)}, u32[]{:S(2)}) collective-permute-start(f32[4,128,128]{2,1,0:T(8,128)} %get-tuple-element.36), channel_id=1, source_target_pairs={{0,128},{1,129},{2,130},{3,131},{4,132},{5,133},{6,134},{7,135},{8... | collective-permute-start | bytes 786440 | tf_op jit(solution)/shard_map/ppermute | solution.py:531
  7.4 23.7 %collective-permute-start.5 = (f32[4,128,128]{2,1,0:T(8,128)}, f32[4,128,128]{2,1,0:T(8,128)S(1)}, u32[]{:S(2)}, u32[]{:S(2)}) collective-permute-start(f32[4,128,128]{2,1,0:T(8,128)} %get-tuple-element.37), channel_id=1, source_target_pairs={{0,192},{1,193},{2,194},{3,195},{4,196},{5,197},{6,198},{7,199},{8... | collective-permute-start | bytes 786440 | tf_op jit(solution)/shard_map/ppermute | solution.py:531
  8.1 23.0 %collective-permute-start.6 = (f32[4,128,128]{2,1,0:T(8,128)}, f32[4,128,128]{2,1,0:T(8,128)S(1)}, u32[]{:S(2)}, u32[]{:S(2)}) collective-permute-start(f32[4,128,128]{2,1,0:T(8,128)} %get-tuple-element.38), channel_id=1, source_target_pairs={{0,64},{1,65},{2,66},{3,67},{4,68},{5,69},{6,70},{7,71},{8,72},{9,... | collective-permute-start | bytes 786440 | tf_op jit(solution)/shard_map/ppermute | solution.py:531
  8.9 4.6 %collective-permute-start.2 = (f32[80,256]{1,0:T(8,128)S(1)}, f32[80,256]{1,0:T(8,128)S(1)}, u32[]{:S(2)}, u32[]{:S(2)}) collective-permute-start(f32[80,256]{1,0:T(8,128)S(1)} %get-tuple-element.32), channel_id=1, source_target_pairs={{0,1},{1,2},{2,3},{3,0},{4,5},{5,6},{6,7},{7,4},{8,9},{9,10},{10,1... | collective-permute-start | bytes 245768 | tf_op jit(solution)/shard_map/ppermute | solution.py:529
  10.2 3.3 %collective-permute-start.3 = (f32[80,256]{1,0:T(8,128)S(1)}, f32[80,256]{1,0:T(8,128)S(1)}, u32[]{:S(2)}, u32[]{:S(2)}) collective-permute-start(f32[80,256]{1,0:T(8,128)S(1)} %get-tuple-element.33), channel_id=1, source_target_pairs={{0,3},{1,0},{2,1},{3,2},{4,7},{5,4},{6,5},{7,6},{8,11},{9,8},{10,9... | collective-permute-start | bytes 245768 | tf_op jit(solution)/shard_map/ppermute | solution.py:530
  13.4 17.6 %copy-start.5 = (f32[4,128,128]{2,1,0:T(8,128)S(1)}, f32[4,128,128]{2,1,0:T(8,128)}, u32[]{:S(2)}) copy-start(f32[4,128,128]{2,1,0:T(8,128)} %get-tuple-element.35) | copy-start | bytes 786436
  15.5 25.9 %all-to-all-start = ((f32[16,24,128]{2,1,0:T(8,128)}), f32[16,24,128]{2,1,0:T(8,128)S(1)}, u32[]{:S(2)}, u32[]{:S(2)}) async-start(f32[16,24,128]{2,1,0:T(8,128)} %shard_map.96.mine), calls=%async_computation | async-start | bytes 393216 | tf_op jit(solution)/shard_map/all_to_all | solution.py:485
  31.0 10.4 %copy-start = (f32[256,128]{1,0:T(8,128)S(1)}, f32[256,128]{1,0:T(8,128)}, u32[]{:S(2)}) copy-start(f32[256,128]{1,0:T(8,128)} %get-tuple-element.34.after.sk) | copy-start | bytes 393220
  31.2 3.0 %collective-permute-start.8 = (f32[128,128]{1,0:T(8,128)S(1)}, f32[128,128]{1,0:T(8,128)S(1)}, u32[]{:S(2)}, u32[]{:S(2)}) collective-permute-start(f32[128,128]{1,0:T(8,128)S(1)} %get-tuple-element.49), channel_id=1, source_target_pairs={{0,32},{64,96},{128,160},{192,224},{1,33},{65,97},{129,161},{193,2... | collective-permute-start | bytes 196616 | tf_op jit(solution)/shard_map/ppermute | solution.py:540
  31.9 2.3 %collective-permute-start.9 = (f32[128,128]{1,0:T(8,128)S(1)}, f32[128,128]{1,0:T(8,128)S(1)}, u32[]{:S(2)}, u32[]{:S(2)}) collective-permute-start(f32[128,128]{1,0:T(8,128)S(1)} %get-tuple-element.50), channel_id=1, source_target_pairs={{0,48},{64,112},{128,176},{192,240},{1,49},{65,113},{129,177},{193... | collective-permute-start | bytes 196616 | tf_op jit(solution)/shard_map/ppermute | solution.py:540
  32.5 5.9 %collective-permute-start.7 = (f32[128,128]{1,0:T(8,128)S(1)}, f32[128,128]{1,0:T(8,128)S(1)}, u32[]{:S(2)}, u32[]{:S(2)}) collective-permute-start(f32[128,128]{1,0:T(8,128)S(1)} %get-tuple-element.51), channel_id=1, source_target_pairs={{0,16},{64,80},{128,144},{192,208},{1,17},{65,81},{129,145},{193,2... | collective-permute-start | bytes 196616 | tf_op jit(solution)/shard_map/ppermute | solution.py:540
  67.3 7.2 %collective-permute-start.10 = (f32[135,8,128]{2,1,0:T(8,128)S(1)}, f32[135,8,128]{2,1,0:T(8,128)S(1)}, u32[]{:S(2)}, u32[]{:S(2)}) collective-permute-start(f32[135,8,128]{2,1,0:T(8,128)S(1)} %get-tuple-element.43), channel_id=1, source_target_pairs={{0,16},{16,32},{32,48},{48,64},{64,80},{80,96},{96,112},{112,128},... | collective-permute-start | bytes 1658888 | tf_op jit(solution)/shard_map/ppermute | solution.py:554
  68.0 9.2 %collective-permute-start.11 = (f32[135,8,128]{2,1,0:T(8,128)S(1)}, f32[135,8,128]{2,1,0:T(8,128)S(1)}, u32[]{:S(2)}, u32[]{:S(2)}) collective-permute-start(f32[135,8,128]{2,1,0:T(8,128)S(1)} %get-tuple-element.44), channel_id=1, source_target_pairs={{0,240},{16,0},{32,16},{48,32},{64,48},{80,64},{96,80},{112,96},{1... | collective-permute-start | bytes 1658888 | tf_op jit(solution)/shard_map/ppermute | solution.py:555
  108.4 3.1 %collective-permute-start.13 = (f32[16,80,128]{2,1,0:T(8,128)S(1)}, f32[16,80,128]{2,1,0:T(8,128)S(1)}, u32[]{:S(2)}, u32[]{:S(2)}) collective-permute-start(f32[16,80,128]{2,1,0:T(8,128)S(1)} %all_to_all.16.got), channel_id=1, source_target_pairs={{0,16},{16,0},{32,48},{48,32},{64,80},{80,64},{96,112},{112,96},{1... | collective-permute-start | bytes 1966088 | tf_op jit(solution)/shard_map/ppermute | solution.py:578
  109.1 5.4 %collective-permute-start.12 = (f32[1]{0:T(128)}, f32[1]{0:T(128)}, u32[]{:S(2)}, u32[]{:S(2)}) collective-permute-start(f32[1]{0:T(128)} %shard_map.101), channel_id=1, source_target_pairs={{0,10},{16,9},{32,6},{48,14},{224,11},{240,8},{64,5},{80,13},{192,... | collective-permute-start | bytes 20 | tf_op jit(solution)/shard_map/ppermute | solution.py:586

commit v7 on v5

--- a/solution.py
+++ b/solution.py
@@ -13,7 +13,7 @@
 ANY = pl.BlockSpec(memory_space=pl.ANY)
 MIB = 1024 * 1024
 LONG = pl.CostEstimate(flops=20_000_000_000, bytes_accessed=1_000_000, transcendentals=0)
-SLOTS = [0, 1, 2, 3, 0, 0, 4, 5, 6, 7, 8, 9, 12, 13, 14, 15, 11, 10]
+SLOTS = [0, 2, 3, 10, 9, 1, 4, 5, 6, 7, 8, 0, 12, 13, 14, 15, 11, 0]
 HALO = 15
 TRI = [HALO] + [HALO - j for j in range(1, HALO)]
 OFF = [sum(TRI[:j]) for j in range(HALO)]
@@ -536,8 +536,13 @@
     parts = swap(both, "tm")
 
     share = jnp.where(t == 0, chunks[0], far[0] + far[1])
-    pairs = [[(0, k), (4, 4 + k), (12, 12 + k)] for k in (1, 2, 3)]
-    pairs += [[(4, 8), (12, 11)], [(4, 9), (12, 10)]]
+    pairs = [
+        [(0, 2), (4, 5), (12, 13)],
+        [(0, 3), (4, 6), (12, 14)],
+        [(0, 10), (4, 7), (12, 15)],
+        [(0, 9), (4, 8), (12, 11)],
+        [(0, 1)],
+    ]
     close = [lax.ppermute(share[k + 1], "tm", pair) for k, pair in enumerate(pairs)]
     hub = (t == 0) | (t == 4) | (t == 12)
     start = jnp.where(hub, share[0], sum(close))

time: 117 us -> 119 us (1.017)
  starting transfers between devices: 27.8 us -> 31.6 us
  blocking collectives: 50.2 us -> 48.3 us
    ppermute x1, starting transfers between devices: 0.77 us -> 4.53 us  [per_device(): lo = lax.ppermute(up, 'tm', ring('tm', 1))]
    all_to_all x1, waiting for transfers between devices: 1.6 us -> 4.47 us  [swap(): return lax.all_to_all(value, axis, 0, 0, tiled=True)]
    ppermute x5, waiting for transfers between devices: 4.3 us -> 1.44 us  [per_device(): lax.ppermute(share[k + 1], 'tm', pair)]
    all_to_all x2, blocking collectives: 50.2 us -> 48.3 us  [swap(): return lax.all_to_all(value, axis, 0, 0, tiled=True)]
where the time goes in v7:
time: 119 us; the launch traced here: 117 us
  blocking collectives  48.3 us (41%)
  starting transfers between devices  31.6 us (27%)
  waiting for transfers between devices  17 us (14%)
  Pallas kernels  15.5 us (13%)
  between operations  2.68 us (2%)
    all_to_all x2, blocking collectives, swap(): return lax.all_to_all(value, axis, 0, 0, tiled=True)  48.3 us
    all_to_all x1, starting transfers between devices, swap(): return lax.all_to_all(value, axis, 0, 0, tiled=True)  13.3 us
    ppermute x1, waiting for transfers between devices, per_device(): lo = lax.ppermute(up, 'tm', ring('tm', 1))  6.1 us
    pallas_call x1, Pallas kernels, per_device(): pl.pallas_call(sweep_kernel, out_shape=jax.ShapeDtypeStruct((16, 80, 128)...  5.79 us
    ppermute x1, starting transfers between devices, per_device(): lo = lax.ppermute(up, 'tm', ring('tm', 1))  4.53 us
    all_to_all x1, waiting for transfers between devices, swap(): return lax.all_to_all(value, axis, 0, 0, tiled=True)  4.47 us
    ppermute x5, starting transfers between devices, per_device(): lax.ppermute(share[k + 1], 'tm', pair)  3.95 us
    ppermute x1, waiting for transfers between devices, per_device(): hi = lax.ppermute(dn, 'tm', ring('tm', -1))  2.77 us
  transfers between devices with their start and end apart: 16, of which 7 were waited for; matrix products, arithmetic and copies ran while one was open for 1% of the time, Pallas kernels for 5%

profile of v7, /device:TPU:1, one launch (start us, length us, event | category | flops | bytes accessed | tf_op | source)
XLA Modules:
  0.0 116.7 jit_solution(11066979724262152643)
XLA Ops:
  0.7 2.2 %shard_map.94 = (f32[64,256]{1,0:T(8,128)}, f32[64,256]{1,0:T(8,128)}, f32[64,256]{1,0:T(8,128)}, f32[64,256]{1,0:T(8,128)}, f32[40,256]{1,0:T(8,128)}, /*index=5*/f32[40,256]{1,0:T(8,128)}, f32[256,128]{1,0:T(8,128)}) custom-call(f32[8]{0:T(128)} %rk_in.1, f32[16]{0:T(128)} %w_in.1, f32[16]{0:T(128)} %rate_in.1, f32[64,256]{1,0:T(8,128)} %bitcast.28, ...), custom_call_target="tpu_custom_call" | custom-call | tf_op jit(solution)/shard_map/pallas_call | solution.py:506
  2.9 2.2 %collective-permute-start = (f32[40,256]{1,0:T(8,128)}, f32[40,256]{1,0:T(8,128)S(1)}, u32[]{:S(2)}, u32[]{:S(2)}) collective-permute-start(f32[40,256]{1,0:T(8,128)} %get-tuple-element.30), channel_id=1, source_target_pairs={{0,4},{4,8},{8,12},{12,0},{1,5},{5,9},{9,13},{13,1},{2,6},{6,10},{... | collective-permute-start | bytes 122888 | tf_op jit(solution)/shard_map/ppermute | solution.py:516
  5.1 1.5 %collective-permute-start.1 = (f32[40,256]{1,0:T(8,128)}, f32[40,256]{1,0:T(8,128)S(1)}, u32[]{:S(2)}, u32[]{:S(2)}) collective-permute-start(f32[40,256]{1,0:T(8,128)} %get-tuple-element.31), channel_id=1, source_target_pairs={{0,12},{4,0},{8,4},{12,8},{1,13},{5,1},{9,5},{13,9},{2,14},{6,2},{... | collective-permute-start | bytes 122888 | tf_op jit(solution)/shard_map/ppermute | solution.py:517
  6.7 0.7 collective-permute-start.4
  8.2 1.3 %collective-permute-start.2 = (f32[80,256]{1,0:T(8,128)S(1)}, f32[80,256]{1,0:T(8,128)S(1)}, u32[]{:S(2)}, u32[]{:S(2)}) collective-permute-start(f32[80,256]{1,0:T(8,128)S(1)} %get-tuple-element.32), channel_id=1, source_target_pairs={{0,1},{1,2},{2,3},{3,0},{4,5},{5,6},{6,7},{7,4},{8,9},{9,10},{10,1... | collective-permute-start | bytes 245768 | tf_op jit(solution)/shard_map/ppermute | solution.py:529
  9.5 1.5 %collective-permute-start.3 = (f32[80,256]{1,0:T(8,128)S(1)}, f32[80,256]{1,0:T(8,128)S(1)}, u32[]{:S(2)}, u32[]{:S(2)}) collective-permute-start(f32[80,256]{1,0:T(8,128)S(1)} %get-tuple-element.33), channel_id=1, source_target_pairs={{0,3},{1,0},{2,1},{3,2},{4,7},{5,4},{6,5},{7,6},{8,11},{9,8},{10,9... | collective-permute-start | bytes 245768 | tf_op jit(solution)/shard_map/ppermute | solution.py:530
  11.9 0.9 collective-permute-done.2.ylo
  12.8 2.1 %shard_map.96.mine = f32[16,24,128]{2,1,0:T(8,128)} custom-call(f32[1]{0:T(128)} %bitcast.omega, f32[64,256]{1,0:T(8,128)S(1)} %copy-done.1, f32[64,256]{1,0:T(8,128)S(1)} %copy-done.2, f32[64,256]{1,0:T(8,128)S(1)} %copy-done.3, f32[64,256]{1,0:T(8,128)S(1)} %copy-done.4, f32[40,256]{1,0:T(8,128)S(1)} %collective-permute-done.xlo, ...), custom_call_target="tpu_custom_call" | custom-call | flops 20000000000 | bytes 1000000 | tf_op jit(solution)/shard_map/pallas_call | solution.py:533
  14.9 13.3 %all-to-all-start = ((f32[16,24,128]{2,1,0:T(8,128)}), f32[16,24,128]{2,1,0:T(8,128)S(1)}, u32[]{:S(2)}, u32[]{:S(2)}) async-start(f32[16,24,128]{2,1,0:T(8,128)} %shard_map.96.mine), calls=%async_computation | async-start | bytes 393216 | tf_op jit(solution)/shard_map/all_to_all | solution.py:485
  29.0 1.3 %collective-permute-start.10 = (f32[128,128]{1,0:T(8,128)S(1)}, f32[128,128]{1,0:T(8,128)S(1)}, u32[]{:S(2)}, u32[]{:S(2)}) collective-permute-start(f32[128,128]{1,0:T(8,128)S(1)} %get-tuple-element.50), channel_id=1, source_target_pairs={{0,16},{1,17},{2,18},{3,19},{4,20},{5,21},{6,22},{7,23},{8,24},{9,... | collective-permute-start | bytes 196616 | tf_op jit(solution)/shard_map/ppermute | solution.py:546
  32.7 1.4 %collective-permute-done.10 = f32[128,128]{1,0:T(8,128)S(1)} collective-permute-done((f32[128,128]{1,0:T(8,128)S(1)}, f32[128,128]{1,0:T(8,128)S(1)}, u32[]{:S(2)}, u32[]{:S(2)}) %collective-permute-start.10) | collective-permute-done | bytes 65568 | tf_op jit(solution)/shard_map/ppermute | solution.py:546
  34.1 4.5 %all-to-all-done.parts.parts_in = f32[16,24,128]{2,1,0:T(8,128)S(1)} async-done(((f32[16,24,128]{2,1,0:T(8,128)}), f32[16,24,128]{2,1,0:T(8,128)S(1)}, u32[]{:S(2)}, u32[]{:S(2)}) %all-to-all-start) | async-done | bytes 196640 | tf_op jit(solution)/shard_map/all_to_all | solution.py:485
  38.6 1.4 %shard_map.98 = (f32[16,144,128]{2,1,0:T(8,128)S(1)}, f32[16,16,128]{2,1,0:T(8,128)S(1)}) custom-call(f32[16,24,128]{2,1,0:T(8,128)S(1)} %all-to-all-done.parts.parts_in, f32[256,128]{1,0:T(8,128)S(1)} %copy-done, f32[128,128]{1,0:T(8,128)S(1)} %fusion.start.start_in, f32[32,128]{1,0:T(8,128)S(1)} %reshape.47.coef.coef_in), custom_call_target="tpu_custom_call" | custom-call | tf_op jit(solution)/shard_map/pallas_call | solution.py:550
  40.0 19.9 %all_to_all.15 = f32[16,144,128]{2,1,0:T(8,128)S(1)} all-to-all(f32[16,144,128]{2,1,0:T(8,128)S(1)} %get-tuple-element.38), channel_id=1, replica_groups=mesh['tm'=16,'gx'=4,'gy'=4] {'gy','gx'}, dimensions={0} | all-to-all | bytes 2359296 | tf_op jit(solution)/shard_map/all_to_all | solution.py:485
  59.9 0.8 shard_map.99
  60.7 4.5 %collective-permute-start.11 = (f32[135,8,128]{2,1,0:T(8,128)S(1)}, f32[135,8,128]{2,1,0:T(8,128)S(1)}, u32[]{:S(2)}, u32[]{:S(2)}) collective-permute-start(f32[135,8,128]{2,1,0:T(8,128)S(1)} %get-tuple-element.42), channel_id=1, source_target_pairs={{0,16},{16,32},{32,48},{48,64},{64,80},{80,96},{96,112},{112,128},... | collective-permute-start | bytes 1658888 | tf_op jit(solution)/shard_map/ppermute | solution.py:560
  65.5 6.1 %collective-permute-done.11.lo = f32[135,8,128]{2,1,0:T(8,128)S(1)} collective-permute-done((f32[135,8,128]{2,1,0:T(8,128)S(1)}, f32[135,8,128]{2,1,0:T(8,128)S(1)}, u32[]{:S(2)}, u32[]{:S(2)}) %collective-permute-start.11) | collective-permute-done | bytes 552992 | tf_op jit(solution)/shard_map/ppermute | solution.py:560
  71.6 2.8 %collective-permute-done.12.hi = f32[135,8,128]{2,1,0:T(8,128)S(1)} collective-permute-done((f32[135,8,128]{2,1,0:T(8,128)S(1)}, f32[135,8,128]{2,1,0:T(8,128)S(1)}, u32[]{:S(2)}, u32[]{:S(2)}) %collective-permute-start.12) | collective-permute-done | bytes 552992 | tf_op jit(solution)/shard_map/ppermute | solution.py:561
  74.4 5.8 %shard_map.100 = f32[16,80,128]{2,1,0:T(8,128)S(1)} custom-call(f32[16]{0:T(128)S(1)} %broadcast_multiply_fusion.beta, f32[16,16,8,128]{3,2,1,0:T(8,128)S(1)} %get-tuple-element.39.own, f32[16,8,128]{2,1,0:T(8,128)S(1)} %get-tuple-element.40.kown, f32[16,8,128]{2,1,0:T(8,128)S(1)} %get-tuple-element.41.fown, f32[135,8,128]{2,1,0:T(8,128)S(1)} %collective-permute-done.11.lo, ...), custom_call_target="tpu_custom_call" | custom-call | tf_op jit(solution)/shard_map/pallas_call | solution.py:562
  80.2 28.4 %all_to_all.16.got = f32[16,80,128]{2,1,0:T(8,128)S(1)} all-to-all(f32[16,80,128]{2,1,0:T(8,128)S(1)} %shard_map.100), channel_id=1, replica_groups=mesh['tm'=16,'gx'=4,'gy'=4] {'tm'}, dimensions={0} | all-to-all | bytes 1310720 | tf_op jit(solution)/shard_map/all_to_all | solution.py:485
  108.7 0.8 shard_map.101
  109.5 1.7 %collective-permute-start.13 = (f32[1]{0:T(128)}, f32[1]{0:T(128)}, u32[]{:S(2)}, u32[]{:S(2)}) collective-permute-start(f32[1]{0:T(128)} %get-tuple-element.46), channel_id=1, source_target_pairs={{0,10},{16,9},{32,6},{48,14},{224,11},{240,8},{64,5},{80,13},{192,... | collective-permute-start | bytes 20 | tf_op jit(solution)/shard_map/ppermute | solution.py:592
  111.2 2.4 %shard_map.102 = f32[16,64,256]{2,1,0:T(8,128)} custom-call(f32[16,80,128]{2,1,0:T(8,128)S(1)} %all_to_all.16.got, f32[16,80,128]{2,1,0:T(8,128)S(1)} %collective-permute-done.14.other, f32[16,24,128]{2,1,0:T(8,128)} %shard_map.96.mine, f32[32,128]{1,0:T(8,128)S(1)} %reshape.47.coef.coef_in), custom_call_target="tpu_custom_call" | custom-call | tf_op jit(solution)/shard_map/pallas_call | solution.py:593
  113.6 1.3 %collective-permute-done.13 = f32[1]{0:T(128)} collective-permute-done((f32[1]{0:T(128)}, f32[1]{0:T(128)}, u32[]{:S(2)}, u32[]{:S(2)}) %collective-permute-start.13) | collective-permute-done | bytes 36 | tf_op jit(solution)/shard_map/ppermute | solution.py:592
  (49 shorter events, 5.3 us)
Async XLA Ops:
  0.6 10.3 %copy-start.6 = (f32[16]{0:T(128)S(1)}, f32[16]{0:T(128)}, u32[]{:S(2)}) copy-start(f32[16]{0:T(128)} %rate_in.1) | copy-start | bytes 196
  0.6 10.3 %copy-start.7 = (f32[16]{0:T(128)S(1)}, f32[16]{0:T(128)}, u32[]{:S(2)}) copy-start(f32[16]{0:T(128)} %w_in.1) | copy-start | bytes 196
  2.8 5.3 %copy-start.1 = (f32[64,256]{1,0:T(8,128)S(1)}, f32[64,256]{1,0:T(8,128)}, u32[]{:S(2)}) copy-start(f32[64,256]{1,0:T(8,128)} %get-tuple-element.26.u) | copy-start | bytes 196612
  2.9 5.3 %copy-start.2 = (f32[64,256]{1,0:T(8,128)S(1)}, f32[64,256]{1,0:T(8,128)}, u32[]{:S(2)}) copy-start(f32[64,256]{1,0:T(8,128)} %get-tuple-element.27.kap) | copy-start | bytes 196612
  2.9 5.3 %copy-start.3 = (f32[64,256]{1,0:T(8,128)S(1)}, f32[64,256]{1,0:T(8,128)}, u32[]{:S(2)}) copy-start(f32[64,256]{1,0:T(8,128)} %get-tuple-element.28.g0) | copy-start | bytes 196612
  2.9 9.9 %copy-start.4 = (f32[64,256]{1,0:T(8,128)S(1)}, f32[64,256]{1,0:T(8,128)}, u32[]{:S(2)}) copy-start(f32[64,256]{1,0:T(8,128)} %get-tuple-element.29.q1s) | copy-start | bytes 196612
  2.9 5.2 %collective-permute-start = (f32[40,256]{1,0:T(8,128)}, f32[40,256]{1,0:T(8,128)S(1)}, u32[]{:S(2)}, u32[]{:S(2)}) collective-permute-start(f32[40,256]{1,0:T(8,128)} %get-tuple-element.30), channel_id=1, source_target_pairs={{0,4},{4,8},{8,12},{12,0},{1,5},{5,9},{9,13},{13,1},{2,6},{6,10},{... | collective-permute-start | bytes 122888 | tf_op jit(solution)/shard_map/ppermute | solution.py:516
  5.1 3.1 %collective-permute-start.1 = (f32[40,256]{1,0:T(8,128)}, f32[40,256]{1,0:T(8,128)S(1)}, u32[]{:S(2)}, u32[]{:S(2)}) collective-permute-start(f32[40,256]{1,0:T(8,128)} %get-tuple-element.31), channel_id=1, source_target_pairs={{0,12},{4,0},{8,4},{12,8},{1,13},{5,1},{9,5},{13,9},{2,14},{6,2},{... | collective-permute-start | bytes 122888 | tf_op jit(solution)/shard_map/ppermute | solution.py:517
  6.7 21.5 %collective-permute-start.4 = (f32[6,128,128]{2,1,0:T(8,128)}, f32[6,128,128]{2,1,0:T(8,128)S(1)}, u32[]{:S(2)}, u32[]{:S(2)}) collective-permute-start(f32[6,128,128]{2,1,0:T(8,128)} %get-tuple-element.36), channel_id=1, source_target_pairs={{0,64},{1,65},{2,66},{3,67},{4,68},{5,69},{6,70},{7,71},{8,72},{9,... | collective-permute-start | bytes 1179656 | tf_op jit(solution)/shard_map/ppermute | solution.py:531
  7.4 20.9 %collective-permute-start.5 = (f32[6,128,128]{2,1,0:T(8,128)}, f32[6,128,128]{2,1,0:T(8,128)S(1)}, u32[]{:S(2)}, u32[]{:S(2)}) collective-permute-start(f32[6,128,128]{2,1,0:T(8,128)} %get-tuple-element.37), channel_id=1, source_target_pairs={{0,192},{1,193},{2,194},{3,195},{4,196},{5,197},{6,198},{7,199},{8... | collective-permute-start | bytes 1179656 | tf_op jit(solution)/shard_map/ppermute | solution.py:531
  8.2 4.6 %collective-permute-start.2 = (f32[80,256]{1,0:T(8,128)S(1)}, f32[80,256]{1,0:T(8,128)S(1)}, u32[]{:S(2)}, u32[]{:S(2)}) collective-permute-start(f32[80,256]{1,0:T(8,128)S(1)} %get-tuple-element.32), channel_id=1, source_target_pairs={{0,1},{1,2},{2,3},{3,0},{4,5},{5,6},{6,7},{7,4},{8,9},{9,10},{10,1... | collective-permute-start | bytes 245768 | tf_op jit(solution)/shard_map/ppermute | solution.py:529
  9.5 3.3 %collective-permute-start.3 = (f32[80,256]{1,0:T(8,128)S(1)}, f32[80,256]{1,0:T(8,128)S(1)}, u32[]{:S(2)}, u32[]{:S(2)}) collective-permute-start(f32[80,256]{1,0:T(8,128)S(1)} %get-tuple-element.33), channel_id=1, source_target_pairs={{0,3},{1,0},{2,1},{3,2},{4,7},{5,4},{6,5},{7,6},{8,11},{9,8},{10,9... | collective-permute-start | bytes 245768 | tf_op jit(solution)/shard_map/ppermute | solution.py:530
  12.8 15.4 %copy-start.5 = (f32[6,128,128]{2,1,0:T(8,128)S(1)}, f32[6,128,128]{2,1,0:T(8,128)}, u32[]{:S(2)}) copy-start(f32[6,128,128]{2,1,0:T(8,128)} %get-tuple-element.35) | copy-start | bytes 1179652
  14.9 23.7 %all-to-all-start = ((f32[16,24,128]{2,1,0:T(8,128)}), f32[16,24,128]{2,1,0:T(8,128)S(1)}, u32[]{:S(2)}, u32[]{:S(2)}) async-start(f32[16,24,128]{2,1,0:T(8,128)} %shard_map.96.mine), calls=%async_computation | async-start | bytes 393216 | tf_op jit(solution)/shard_map/all_to_all | solution.py:485
  28.3 10.4 %copy-start = (f32[256,128]{1,0:T(8,128)S(1)}, f32[256,128]{1,0:T(8,128)}, u32[]{:S(2)}) copy-start(f32[256,128]{1,0:T(8,128)} %get-tuple-element.34.after.sk) | copy-start | bytes 393220
  28.4 4.3 %collective-permute-start.7 = (f32[128,128]{1,0:T(8,128)S(1)}, f32[128,128]{1,0:T(8,128)S(1)}, u32[]{:S(2)}, u32[]{:S(2)}) collective-permute-start(f32[128,128]{1,0:T(8,128)S(1)} %get-tuple-element.49), channel_id=1, source_target_pairs={{0,48},{64,96},{192,224},{1,49},{65,97},{193,225},{2,50},{66,98},{... | collective-permute-start | bytes 196616 | tf_op jit(solution)/shard_map/ppermute | solution.py:546
  29.0 5.1 %collective-permute-start.10 = (f32[128,128]{1,0:T(8,128)S(1)}, f32[128,128]{1,0:T(8,128)S(1)}, u32[]{:S(2)}, u32[]{:S(2)}) collective-permute-start(f32[128,128]{1,0:T(8,128)S(1)} %get-tuple-element.50), channel_id=1, source_target_pairs={{0,16},{1,17},{2,18},{3,19},{4,20},{5,21},{6,22},{7,23},{8,24},{9,... | collective-permute-start | bytes 196616 | tf_op jit(solution)/shard_map/ppermute | solution.py:546
  30.3 3.8 %collective-permute-start.9 = (f32[128,128]{1,0:T(8,128)S(1)}, f32[128,128]{1,0:T(8,128)S(1)}, u32[]{:S(2)}, u32[]{:S(2)}) collective-permute-start(f32[128,128]{1,0:T(8,128)S(1)} %get-tuple-element.51), channel_id=1, source_target_pairs={{0,144},{64,128},{192,176},{1,145},{65,129},{193,177},{2,146},{66,... | collective-permute-start | bytes 196616 | tf_op jit(solution)/shard_map/ppermute | solution.py:546
  31.0 3.1 %collective-permute-start.8 = (f32[128,128]{1,0:T(8,128)S(1)}, f32[128,128]{1,0:T(8,128)S(1)}, u32[]{:S(2)}, u32[]{:S(2)}) collective-permute-start(f32[128,128]{1,0:T(8,128)S(1)} %get-tuple-element.52), channel_id=1, source_target_pairs={{0,160},{64,112},{192,240},{1,161},{65,113},{193,241},{2,162},{66,... | collective-permute-start | bytes 196616 | tf_op jit(solution)/shard_map/ppermute | solution.py:546
  31.7 2.4 %collective-permute-start.6 = (f32[128,128]{1,0:T(8,128)S(1)}, f32[128,128]{1,0:T(8,128)S(1)}, u32[]{:S(2)}, u32[]{:S(2)}) collective-permute-start(f32[128,128]{1,0:T(8,128)S(1)} %get-tuple-element.53), channel_id=1, source_target_pairs={{0,32},{64,80},{192,208},{1,33},{65,81},{193,209},{2,34},{66,82},{... | collective-permute-start | bytes 196616 | tf_op jit(solution)/shard_map/ppermute | solution.py:546
  60.7 11.0 %collective-permute-start.11 = (f32[135,8,128]{2,1,0:T(8,128)S(1)}, f32[135,8,128]{2,1,0:T(8,128)S(1)}, u32[]{:S(2)}, u32[]{:S(2)}) collective-permute-start(f32[135,8,128]{2,1,0:T(8,128)S(1)} %get-tuple-element.42), channel_id=1, source_target_pairs={{0,16},{16,32},{32,48},{48,64},{64,80},{80,96},{96,112},{112,128},... | collective-permute-start | bytes 1658888 | tf_op jit(solution)/shard_map/ppermute | solution.py:560
  65.2 9.2 %collective-permute-start.12 = (f32[135,8,128]{2,1,0:T(8,128)S(1)}, f32[135,8,128]{2,1,0:T(8,128)S(1)}, u32[]{:S(2)}, u32[]{:S(2)}) collective-permute-start(f32[135,8,128]{2,1,0:T(8,128)S(1)} %get-tuple-element.43), channel_id=1, source_target_pairs={{0,240},{16,0},{32,16},{48,32},{64,48},{80,64},{96,80},{112,96},{1... | collective-permute-start | bytes 1658888 | tf_op jit(solution)/shard_map/ppermute | solution.py:561
  108.6 2.6 %collective-permute-start.14 = (f32[16,80,128]{2,1,0:T(8,128)S(1)}, f32[16,80,128]{2,1,0:T(8,128)S(1)}, u32[]{:S(2)}, u32[]{:S(2)}) collective-permute-start(f32[16,80,128]{2,1,0:T(8,128)S(1)} %all_to_all.16.got), channel_id=1, source_target_pairs={{0,16},{16,0},{32,48},{48,32},{64,80},{80,64},{96,112},{112,96},{1... | collective-permute-start | bytes 1966088 | tf_op jit(solution)/shard_map/ppermute | solution.py:584
  109.5 5.4 %collective-permute-start.13 = (f32[1]{0:T(128)}, f32[1]{0:T(128)}, u32[]{:S(2)}, u32[]{:S(2)}) collective-permute-start(f32[1]{0:T(128)} %get-tuple-element.46), channel_id=1, source_target_pairs={{0,10},{16,9},{32,6},{48,14},{224,11},{240,8},{64,5},{80,13},{192,... | collective-permute-start | bytes 20 | tf_op jit(solution)/shard_map/ppermute | solution.py:592
